TPU v7x, 512 devices: a whole 4x8x8 slice. The times are simulated.
512 devices in a mesh: dp: 64 (over x, y, core), tensor: 8 (over z).
Axes of the slice: x: 4, y: 8, z: 8, core: 2. Of those that a mesh axis runs over, the one named last changes fastest.
Arguments:
- features: bfloat16 [8192, 4096], P('dp', 'tensor'), may hold values from -6 to 6
- out_grad: bfloat16 [8192, 14336], P('dp', 'tensor'), may hold values from -0.0625 to 0.0625
- weight: bfloat16 [4096, 14336], P('dp', 'tensor'), may hold values from -4 to 4
- basis: bfloat16 [4096, 128], replicated, may hold values from -0.09375 to 0.09375
- moment_one: float32 [8, 1792, 128], P('tensor', 'dp'), may hold values from -3 to 3
- moment_two: float32 [8, 1792, 128], P('tensor', 'dp'), may hold values from 0.05 to 1
Outputs:
- feature_grad: bfloat16 [8192, 4096], P('dp', 'tensor')
- new_moment_one: float32 [8, 1792, 128], P('tensor', 'dp')
- new_moment_two: float32 [8, 1792, 128], P('tensor', 'dp')
- direction: float32 [8, 1792, 4096], P('tensor', 'dp')
All inputs are finite; a program needn't handle non-finite values.
Results may differ from a plain program's by a relative error of at most 0.017.
Values may be sent and summed in bfloat16 or wider, within the bound.
No kernel may reach another device: no remote copies, remote signals or barrier semaphores. Data moves between devices by JAX's collectives and lax.ppermute only.
A program may use at most 128 MiB of HBM per device.

v0:
```python
import jax
import jax.numpy as jnp
from jax import lax
from jax.sharding import PartitionSpec as P

beta_one = 0.9
beta_two = 0.95
bias_one = 1.0 - 0.9**20
bias_two = 1.0 - 0.95**20
adam_epsilon = 1e-08


def body(features, out_grad, weight, basis, moment_one, moment_two):
    partial_value = jnp.einsum(
        "tf,df->td",
        out_grad,
        lax.all_gather(weight, "dp", axis=0, tiled=True),
        preferred_element_type=jnp.float32,
    )
    feature_grad = lax.psum_scatter(
        partial_value.astype(jnp.bfloat16), "tensor", scatter_dimension=1, tiled=True
    )
    part_width = features.shape[1]
    basis_part = lax.dynamic_slice_in_dim(
        basis, lax.axis_index("tensor") * part_width, part_width, 0
    )
    local_coords = jnp.dot(features, basis_part, preferred_element_type=jnp.float32)
    coords = lax.psum(local_coords, "tensor")
    coords = coords.astype(jnp.bfloat16)
    projected = lax.psum_scatter(
        jnp.einsum("tf,tr->fr", out_grad, coords, preferred_element_type=jnp.float32),
        "dp",
        scatter_dimension=0,
        tiled=True,
    )
    first = moment_one[0]
    second = moment_two[0]
    new_one = beta_one * first + (1.0 - beta_one) * projected
    new_two = beta_two * second + (1.0 - beta_two) * projected * projected
    step_dir = (new_one / bias_one / (jnp.sqrt(new_two / bias_two) + adam_epsilon)).astype(
        jnp.bfloat16
    )
    direction = jnp.einsum("cr,dr->cd", step_dir, basis, preferred_element_type=jnp.float32)
    return (feature_grad, new_one[None], new_two[None], direction[None])


def solution(mesh):
    in_specs = (
        P("dp", "tensor"),
        P("dp", "tensor"),
        P("dp", "tensor"),
        P(),
        P("tensor", "dp", None),
        P("tensor", "dp", None),
    )
    out_specs = (
        P("dp", "tensor"),
        P("tensor", "dp", None),
        P("tensor", "dp", None),
        P("tensor", "dp", None),
    )
    return jax.shard_map(body, mesh=mesh, in_specs=in_specs, out_specs=out_specs, check_vma=False)
```

profile of v0, /device:TPU:6, one launch (start us, length us, event | category | flops | bytes accessed | tf_op | source)
XLA Modules:
  0.0 363.4 jit_solution(8995397619001780233)
XLA Ops:
  7.2 0.0 copy-start
  7.2 0.0 copy-start.1
  7.2 0.0 copy-start.2
  7.2 0.0 all-gather.2.cloned.1.call-start
  7.2 0.7 all-gather.2.cloned.1.call-update
  7.9 0.0 all-reduce.3.cloned.1.call-start
  8.0 0.4 copy-done
  8.4 1.1 convolution_bitcast_fusion.2
  9.5 36.4 %psum.7 = bf16[128,128]{0,1:T(8,128)(2,1)S(1)} all-reduce(f32[128,128]{0,1:T(8,128)S(1)} %convolution_bitcast_fusion.2), channel_id=1, replica_groups=mesh['dp'=64,'tensor'=8] {'tensor'}, use_global_device_ids=true, to_apply=%region_1.0 | all-reduce | flops 16384 | bytes 98304 | tf_op jit(solution)/shard_map/psum | solution.py:28
  45.9 2.2 convolution_bitcast_fusion.1
  48.1 0.0 all-reduce.3.cloned.1.call-update
  48.2 0.0 reduce-scatter.3.cloned.1.call-start
  48.2 65.7 %all-gather.2.cloned.1.call-done = bf16[4096,1792]{1,0:T(8,128)(2,1)} async-done(((bf16[64,1792]{1,0:T(8,128)(2,1)}), bf16[4096,1792]{1,0:T(8,128)(2,1)}) %all-gather.2.cloned.1.call-update) | async-done | bytes 14680080 | tf_op jit(solution)/shard_map/all_gather | solution.py:17
  113.9 11.2 %convolution_convert_fusion = bf16[128,4096]{1,0:T(8,128)(2,1)} fusion(bf16[128,1792]{1,0:T(8,128)(2,1)} %param.7, bf16[4096,1792]{1,0:T(8,128)(2,1)} %all-gather.2.cloned.1.call-done), kind=kOutput, calls=%fused_computation | convolution fusion | flops 1879572480 | bytes 16187392 | tf_op jit(solution)/shard_map/tf,df->td/dot_general | solution.py:14
  125.1 0.0 reduce-scatter.3.cloned.1.call-update
  125.1 0.0 copy-done.1
  125.1 0.1 copy.16
  125.2 0.0 copy-done.2
  125.3 0.1 copy.15
  125.4 1.3 dynamic-slice
  127.3 184.8 %all-reduce.3.cloned.1.call-done = f32[1792,128]{0,1:T(8,128)} async-done(((f32[1792,128]{0,1:T(8,128)}), f32[1792,128]{0,1:T(8,128)}) %all-reduce.3.cloned.1.call-update) | async-done | bytes 917520
  312.1 1.0 fusion.8
  313.1 0.7 copy.17
  313.7 0.7 copy.18
  314.4 1.5 convolution_bitcast_fusion
  315.9 1.3 copy.19
  317.2 39.7 %reduce-scatter.3.cloned.1.call-done = bf16[128,512]{1,0:T(8,128)(2,1)} async-done(((bf16[128,4096]{1,0:T(8,128)(2,1)}), bf16[128,512]{1,0:T(8,128)(2,1)}) %reduce-scatter.3.cloned.1.call-update) | async-done | bytes 131088 | tf_op jit(solution)/shard_map/reduce_scatter | solution.py:20
Async XLA Ops:
  7.2 1.2 copy-start
  7.2 118.0 %copy-start.1 = (f32[1,28,128]{2,0,1:T(1,128)S(1)}, f32[1,28,128]{2,0,1:T(1,128)}, u32[]{:S(2)}) copy-start(f32[1,28,128]{2,0,1:T(1,128)} %param.11) | copy-start | bytes 43012
  7.2 118.1 %copy-start.2 = (f32[1,28,128]{2,0,1:T(1,128)S(1)}, f32[1,28,128]{2,0,1:T(1,128)}, u32[]{:S(2)}) copy-start(f32[1,28,128]{2,0,1:T(1,128)} %param.10) | copy-start | bytes 43012
  7.2 106.7 %all-gather.2.cloned.1.call-start = ((), (), s32[]{:S(2)}) async-start(), calls=%async_computation.1 | async-start | bytes 14909440 | tf_op jit(solution)/shard_map/all_gather | solution.py:17
  7.9 304.1 %all-reduce.3.cloned.1.call-start = ((), (), s32[]{:S(2)}) async-start(), calls=%async_computation.3 | async-start | bytes 1835008
  48.2 308.7 %reduce-scatter.3.cloned.1.call-start = ((), (), s32[]{:S(2)}) async-start(), calls=%async_computation.2 | async-start | bytes 1179648 | tf_op jit(solution)/shard_map/reduce_scatter | solution.py:20
Sparse Core Ops, SparseCore 0:
  11.4 102.5 all-gather.1
  117.4 194.6 all-reduce.2
  315.7 41.1 reduce-scatter.2
where the time goes:
time: 364 us; the launch traced here: 363 us
  waiting for transfers between devices  291 us (80%)
  blocking collectives  36.4 us (10%)
  matrix products  16 us (4%)
  between operations  14.5 us (4%)
  local copies, waits for them, and re-layouts  4.53 us (1%)
    unnamed x4, waiting for transfers between devices  185 us
    all_gather x1, waiting for transfers between devices, body(): lax.all_gather(weight, 'dp', axis=0, tiled=True)  65.7 us
    reduce_scatter x1, waiting for transfers between devices, body(): lax.psum_scatter(partial_value.astype(jnp.bfloat16), 'tensor', scatter_di...  39.7 us
    psum x1, blocking collectives, body(): coords = lax.psum(local_coords, 'tensor')  36.4 us
    dot_general x1, matrix products, body(): jnp.einsum('tf,df->td', out_grad, lax.all_gather(weight, 'dp', axis=0, ti...  11.2 us
  transfers between devices with their start and end apart: 3, of which 3 were waited for; matrix products, arithmetic and copies ran while one was open for 6% of the time, Pallas kernels for 0%

commit v1 on v0

--- a/solution.py
+++ b/solution.py
@@ -9,30 +9,61 @@
 bias_two = 1.0 - 0.95**20
 adam_epsilon = 1e-08
 
+NX, NY, NC, NZ = 4, 8, 2, 8
+
+
+def dp_of(x, y, c):
+    return (x * NY + y) * NC + c
+
+
+ALONG_X = [[dp_of(x, y, c) for x in range(NX)] for y in range(NY) for c in range(NC)]
+ALONG_YC = [[dp_of(x, y, c) for y in range(NY) for c in range(NC)] for x in range(NX)]
+
+HOME = [
+    (dp_of(x, y, c) * NZ + z, dp_of(z // 2, y, c) * NZ + 2 * x + z % 2)
+    for x in range(NX)
+    for y in range(NY)
+    for c in range(NC)
+    for z in range(NZ)
+]
+
 
 def body(features, out_grad, weight, basis, moment_one, moment_two):
-    partial_value = jnp.einsum(
-        "tf,df->td",
-        out_grad,
-        lax.all_gather(weight, "dp", axis=0, tiled=True),
-        preferred_element_type=jnp.float32,
-    )
-    feature_grad = lax.psum_scatter(
-        partial_value.astype(jnp.bfloat16), "tensor", scatter_dimension=1, tiled=True
-    )
+    tokens, hidden = out_grad.shape
     part_width = features.shape[1]
+    rank = basis.shape[1]
+
+    rows = lax.all_gather(weight, "dp", axis=0, tiled=True, axis_index_groups=ALONG_YC)
+
     basis_part = lax.dynamic_slice_in_dim(
         basis, lax.axis_index("tensor") * part_width, part_width, 0
     )
     local_coords = jnp.dot(features, basis_part, preferred_element_type=jnp.float32)
-    coords = lax.psum(local_coords, "tensor")
-    coords = coords.astype(jnp.bfloat16)
-    projected = lax.psum_scatter(
-        jnp.einsum("tf,tr->fr", out_grad, coords, preferred_element_type=jnp.float32),
+    all_coords = lax.all_to_all(
+        jnp.broadcast_to(local_coords.astype(jnp.bfloat16), (NZ, tokens, rank)), "tensor", 0, 0
+    )
+    coords = jnp.sum(all_coords.astype(jnp.float32), axis=0).astype(jnp.bfloat16)
+
+    joined = jnp.concatenate([out_grad, coords], axis=1)
+    joined = lax.all_to_all(
+        jnp.broadcast_to(joined, (NX,) + joined.shape), "dp", 0, 0, axis_index_groups=ALONG_X
+    ).reshape(NX * tokens, hidden + rank)
+    grads = joined[:, :hidden]
+    coords = joined[:, hidden:]
+
+    partial_proj = jnp.einsum("tf,tr->fr", grads, coords, preferred_element_type=jnp.float32)
+    own = hidden // NX
+    x = lax.axis_index("dp") // (NY * NC)
+    partial_proj = lax.dynamic_slice_in_dim(partial_proj, x * own, own, 0)
+    partial_proj = lax.all_to_all(
+        partial_proj.reshape(NY * NC, own // (NY * NC), rank),
         "dp",
-        scatter_dimension=0,
-        tiled=True,
+        0,
+        0,
+        axis_index_groups=ALONG_YC,
     )
+    projected = jnp.sum(partial_proj, axis=0)
+
     first = moment_one[0]
     second = moment_two[0]
     new_one = beta_one * first + (1.0 - beta_one) * projected
@@ -41,6 +72,18 @@
         jnp.bfloat16
     )
     direction = jnp.einsum("cr,dr->cd", step_dir, basis, preferred_element_type=jnp.float32)
+
+    partial_value = jnp.einsum(
+        "xtf,hdf->xhtd",
+        grads.reshape(NX, tokens, hidden),
+        rows.reshape(2, part_width, hidden),
+        preferred_element_type=jnp.float32,
+    ).astype(jnp.bfloat16)
+    pieces = lax.all_to_all(
+        partial_value.reshape(NZ, tokens, part_width), "tensor", 0, 0
+    )
+    summed = jnp.sum(pieces.astype(jnp.float32), axis=0).astype(jnp.bfloat16)
+    feature_grad = lax.ppermute(summed, ("dp", "tensor"), HOME)
     return (feature_grad, new_one[None], new_two[None], direction[None])
 
 

time: 364 us -> 138 us (0.38)
  waiting for transfers between devices: 291 us -> 65.9 us
  starting transfers between devices: 0.12 us -> 19.2 us
  blocking collectives: 36.4 us -> 22 us
  matrix products: 16 us -> 7.94 us
    unnamed x4 -> x1, waiting for transfers between devices: 185 us -> 0.68 us
    all_gather x1, waiting for transfers between devices: 65.7 us -> 0.02 us  [body(): lax.all_gather(weight, 'dp', axis=0, tiled=True, axis_index_groups=ALONG_YC)]
    all_to_all x0 -> x3, waiting for transfers between devices: none -> 56 us  [the longest x1 29.5 us: body(): lax.all_to_all(partial_value.reshape(NZ, tokens, part_width), 'tensor', 0...]
    reduce_scatter x1 -> x0, waiting for transfers between devices: 39.7 us -> none  [body(): lax.psum_scatter(partial_value.astype(jnp.bfloat16), 'tensor', scatter_di...]
    psum x1 -> x0, blocking collectives: 36.4 us -> none  [body(): coords = lax.psum(local_coords, 'tensor')]
    all_to_all x0 -> x1, blocking collectives: none -> 22 us  [body(): lax.all_to_all(jnp.broadcast_to(local_coords.astype(jnp.bfloat16), (NZ, t...]
    all_to_all x0 -> x3, starting transfers between devices: none -> 15.5 us  [the longest x1 7.22 us: body(): lax.all_to_all(partial_proj.reshape(NY * NC, own // (NY * NC), rank), 'dp...]
    ppermute x0 -> x1, waiting for transfers between devices: none -> 9.18 us  [body(): feature_grad = lax.ppermute(summed, ('dp', 'tensor'), HOME)]
  transfers between devices with their start and end apart: 3 -> 5, of which waited for: 3 -> 4; matrix products, arithmetic and copies ran while one was open for 6% -> 10% of each run, Pallas kernels for 0% -> 0%
where the time goes in v1:
time: 138 us; the launch traced here: 136 us
  waiting for transfers between devices  65.9 us (48%)
  blocking collectives  22 us (16%)
  starting transfers between devices  19.2 us (14%)
  between operations  14.2 us (10%)
  matrix products  7.94 us (6%)
  local copies, waits for them, and re-layouts  6.11 us (4%)
    all_to_all x1, waiting for transfers between devices, body(): lax.all_to_all(partial_value.reshape(NZ, tokens, part_width), 'tensor', 0...  29.5 us
    all_to_all x1, blocking collectives, body(): lax.all_to_all(jnp.broadcast_to(local_coords.astype(jnp.bfloat16), (NZ, t...  22 us
    all_to_all x1, waiting for transfers between devices, body(): lax.all_to_all(jnp.broadcast_to(joined, (NX,) + joined.shape), 'dp', 0, 0...  21.1 us
    ppermute x1, waiting for transfers between devices, body(): feature_grad = lax.ppermute(summed, ('dp', 'tensor'), HOME)  9.18 us
    all_to_all x1, starting transfers between devices, body(): lax.all_to_all(partial_proj.reshape(NY * NC, own // (NY * NC), rank), 'dp...  7.22 us
    dot_general x1, matrix products, body(): jnp.einsum('xtf,hdf->xhtd', grads.reshape(NX, tokens, hidden), rows.resha...  5.68 us
    all_to_all x1, waiting for transfers between devices, body(): lax.all_to_all(partial_proj.reshape(NY * NC, own // (NY * NC), rank), 'dp...  5.46 us
    all_to_all x1, starting transfers between devices, body(): lax.all_to_all(jnp.broadcast_to(joined, (NX,) + joined.shape), 'dp', 0, 0...  4.77 us
  transfers between devices with their start and end apart: 5, of which 4 were waited for; matrix products, arithmetic and copies ran while one was open for 10% of the time, Pallas kernels for 0%

profile of v1, /device:TPU:6, one launch (start us, length us, event | category | flops | bytes accessed | tf_op | source)
XLA Modules:
  0.0 136.2 jit_solution(16038663816497399602)
XLA Ops:
  7.2 0.0 copy-start
  7.2 0.0 copy-start.1
  7.2 0.0 all-gather.2.cloned.1.call-start
  7.2 0.7 all-gather.2.cloned.1.call-update
  7.9 0.5 copy-done
  8.4 1.1 fusion
  9.5 0.1 copy.18
  9.7 22.0 %all_to_all.20 = bf16[8,128,128]{2,1,0:T(8,128)(2,1)S(1)} all-to-all(bf16[8,128,128]{2,1,0:T(8,128)(2,1)S(1)} %broadcast_in_dim.11), channel_id=1, replica_groups=mesh['dp'=64,'tensor'=8] {'tensor'}, dimensions={0} | all-to-all | bytes 524288 | tf_op jit(solution)/shard_map/all_to_all | solution.py:42
  31.7 0.0 copy-done.1
  31.8 1.5 %broadcast_in_dim.12 = bf16[4,128,1920]{2,1,0:T(8,128)(2,1)} broadcast(bf16[128,1920]{1,0:T(8,128)(2,1)S(1)} %pad_maximum_fusion), dimensions={1,2} | broadcast | bytes 2457600 | tf_op jit(solution)/shard_map/broadcast_in_dim | solution.py:49
  33.2 4.8 %all-to-all-start.1 = ((bf16[4,128,1920]{2,1,0:T(8,128)(2,1)}), bf16[4,128,1920]{2,1,0:T(8,128)(2,1)S(1)}, u32[]{:S(2)}, u32[]{:S(2)}) async-start(bf16[4,128,1920]{2,1,0:T(8,128)(2,1)} %broadcast_in_dim.12), calls=%async_computation.1 | async-start | bytes 3932160 | tf_op jit(solution)/shard_map/all_to_all | solution.py:48
  38.0 21.1 %all-to-all-done.1 = bf16[4,128,1920]{2,1,0:T(8,128)(2,1)S(1)} async-done(((bf16[4,128,1920]{2,1,0:T(8,128)(2,1)}), bf16[4,128,1920]{2,1,0:T(8,128)(2,1)S(1)}, u32[]{:S(2)}, u32[]{:S(2)}) %all-to-all-start.1) | async-done | bytes 1966112 | tf_op jit(solution)/shard_map/all_to_all | solution.py:48
  59.1 1.4 %slice.8 = bf16[512,1792]{1,0:T(8,128)(2,1)} slice(bf16[512,1920]{1,0:T(8,128)(2,1)S(1)} %bitcast.34), slice={[0:512], [0:1792]} | slice | bytes 3670016 | tf_op jit(solution)/shard_map/slice | solution.py:51
  60.4 0.7 fusion.1
  61.1 0.7 reshape.48
  61.9 7.2 %all-to-all-start.3 = ((f32[16,28,128]{2,1,0:T(8,128)}), f32[16,28,128]{2,1,0:T(8,128)S(1)}, u32[]{:S(2)}, u32[]{:S(2)}) async-start(f32[16,28,128]{2,1,0:T(8,128)} %reshape.48), calls=%async_computation.3 | async-start | bytes 524288 | tf_op jit(solution)/shard_map/all_to_all | solution.py:58
  69.1 0.0 all-gather.2.cloned.1.call-done
  69.1 5.7 %convolution_convert_fusion = bf16[4,128,2,512]{3,1,2,0:T(8,128)(2,1)} fusion(bf16[4,128,1792,1]{2,1,3,0:T(8,128)(2,1)} %bitcast.36, bf16[2,512,1792,1]{2,1,0,3:T(8,128)(2,1)} %bitcast.37), kind=kOutput, calls=%fused_computation.1 | convolution fusion | flops 1879572480 | bytes 6553600 | tf_op jit(solution)/shard_map/xtf,hdf->xhtd/dot_general | solution.py:76
  74.8 0.0 copy-start.2
  74.8 0.0 copy-start.3
  74.8 5.5 %all-to-all-done.3 = f32[16,28,128]{2,1,0:T(8,128)S(1)} async-done(((f32[16,28,128]{2,1,0:T(8,128)}), f32[16,28,128]{2,1,0:T(8,128)S(1)}, u32[]{:S(2)}, u32[]{:S(2)}) %all-to-all-start.3) | async-done | bytes 229408 | tf_op jit(solution)/shard_map/all_to_all | solution.py:58
  80.3 3.6 %all-to-all-start.2 = ((bf16[8,128,512]{2,1,0:T(8,128)(2,1)}), bf16[8,128,512]{2,1,0:T(8,128)(2,1)S(1)}, u32[]{:S(2)}, u32[]{:S(2)}) async-start(bf16[8,128,512]{2,1,0:T(8,128)(2,1)} %bitcast.8), calls=%async_computation.2 | async-start | bytes 2097152 | tf_op jit(solution)/shard_map/all_to_all | solution.py:82
  83.8 0.0 copy-done.2
  83.9 0.0 copy-done.3
  83.9 0.7 fusion.11
  84.6 29.5 %all-to-all-done.2 = bf16[8,128,512]{2,1,0:T(8,128)(2,1)S(1)} async-done(((bf16[8,128,512]{2,1,0:T(8,128)(2,1)}), bf16[8,128,512]{2,1,0:T(8,128)(2,1)S(1)}, u32[]{:S(2)}, u32[]{:S(2)}) %all-to-all-start.2) | async-done | bytes 1048608 | tf_op jit(solution)/shard_map/all_to_all | solution.py:82
  114.0 0.1 reduce_sum.36
  114.2 3.6 %collective-permute-start = (bf16[128,512]{1,0:T(8,128)(2,1)S(1)}, bf16[128,512]{1,0:T(8,128)(2,1)S(1)}, u32[]{:S(2)}, u32[]{:S(2)}) collective-permute-start(bf16[128,512]{1,0:T(8,128)(2,1)S(1)} %reduce_sum.36), channel_id=1, source_target_pairs={{0,0},{1,1},{2,128},{3,129},{4,256},{5,257},{6,384},{7,385},{8,8},... | collective-permute-start | bytes 393224 | tf_op jit(solution)/shard_map/ppermute | solution.py:86
  117.8 0.5 convolution_bitcast_fusion
  118.3 1.3 copy.21
  119.5 9.2 %collective-permute-done = bf16[128,512]{1,0:T(8,128)(2,1)S(1)} collective-permute-done((bf16[128,512]{1,0:T(8,128)(2,1)S(1)}, bf16[128,512]{1,0:T(8,128)(2,1)S(1)}, u32[]{:S(2)}, u32[]{:S(2)}) %collective-permute-start) | collective-permute-done | bytes 131104 | tf_op jit(solution)/shard_map/ppermute | solution.py:86
  128.7 0.7 copy.34
  (6 shorter events, 0.2 us)
Async XLA Ops:
  7.2 1.2 copy-start
  7.2 24.6 %copy-start.1 = (bf16[128,1792]{1,0:T(8,128)(2,1)S(1)}, bf16[128,1792]{1,0:T(8,128)(2,1)}, u32[]{:S(2)}) copy-start(bf16[128,1792]{1,0:T(8,128)(2,1)} %param.7) | copy-start | bytes 1376260
  7.2 61.9 %all-gather.2.cloned.1.call-start = ((), (), s32[]{:S(2)}) async-start(), calls=%async_computation.4 | async-start | bytes 3899392 | tf_op jit(solution)/shard_map/all_gather | solution.py:36
  33.2 25.8 %all-to-all-start.1 = ((bf16[4,128,1920]{2,1,0:T(8,128)(2,1)}), bf16[4,128,1920]{2,1,0:T(8,128)(2,1)S(1)}, u32[]{:S(2)}, u32[]{:S(2)}) async-start(bf16[4,128,1920]{2,1,0:T(8,128)(2,1)} %broadcast_in_dim.12), calls=%async_computation.1 | async-start | bytes 3932160 | tf_op jit(solution)/shard_map/all_to_all | solution.py:48
  61.9 18.4 %all-to-all-start.3 = ((f32[16,28,128]{2,1,0:T(8,128)}), f32[16,28,128]{2,1,0:T(8,128)S(1)}, u32[]{:S(2)}, u32[]{:S(2)}) async-start(f32[16,28,128]{2,1,0:T(8,128)} %reshape.48), calls=%async_computation.3 | async-start | bytes 524288 | tf_op jit(solution)/shard_map/all_to_all | solution.py:58
  74.8 9.0 %copy-start.2 = (f32[1,28,128]{2,0,1:T(1,128)S(1)}, f32[1,28,128]{2,0,1:T(1,128)}, u32[]{:S(2)}) copy-start(f32[1,28,128]{2,0,1:T(1,128)} %param.11) | copy-start | bytes 43012
  74.8 9.1 %copy-start.3 = (f32[1,28,128]{2,0,1:T(1,128)S(1)}, f32[1,28,128]{2,0,1:T(1,128)}, u32[]{:S(2)}) copy-start(f32[1,28,128]{2,0,1:T(1,128)} %param.10) | copy-start | bytes 43012
  80.3 33.8 %all-to-all-start.2 = ((bf16[8,128,512]{2,1,0:T(8,128)(2,1)}), bf16[8,128,512]{2,1,0:T(8,128)(2,1)S(1)}, u32[]{:S(2)}, u32[]{:S(2)}) async-start(bf16[8,128,512]{2,1,0:T(8,128)(2,1)} %bitcast.8), calls=%async_computation.2 | async-start | bytes 2097152 | tf_op jit(solution)/shard_map/all_to_all | solution.py:82
  114.2 14.5 %collective-permute-start = (bf16[128,512]{1,0:T(8,128)(2,1)S(1)}, bf16[128,512]{1,0:T(8,128)(2,1)S(1)}, u32[]{:S(2)}, u32[]{:S(2)}) collective-permute-start(bf16[128,512]{1,0:T(8,128)(2,1)S(1)} %reduce_sum.36), channel_id=1, source_target_pairs={{0,0},{1,1},{2,128},{3,129},{4,256},{5,257},{6,384},{7,385},{8,8},... | collective-permute-start | bytes 393224 | tf_op jit(solution)/shard_map/ppermute | solution.py:86
Sparse Core Ops, SparseCore 0:
  10.1 48.6 all-gather.1

commit v2 on v0

v2 whole, which is shorter than its diff:
```python
import jax
import jax.numpy as jnp
from jax import lax
from jax.experimental import pallas as pl
from jax.experimental.pallas import tpu as pltpu
from jax.sharding import PartitionSpec as P

beta_one = 0.9
beta_two = 0.95
bias_one = 1.0 - 0.9**20
bias_two = 1.0 - 0.95**20
adam_epsilon = 1e-08

NX, NY, NC, NZ = 4, 8, 2, 8


def dp_of(x, y, c):
    return (x * NY + y) * NC + c


CHIPS = [(x, y, c) for x in range(NX) for y in range(NY) for c in range(NC)]
ALONG_X = [[dp_of(x, y, c) for x in range(NX)] for y in range(NY) for c in range(NC)]
ALONG_YC = [[dp_of(x, y, c) for y in range(NY) for c in range(NC)] for x in range(NX)]
SAME_PARITY = [
    [dp_of(x, p + 2 * j, c) for j in range(NY // 2)]
    for x in range(NX)
    for p in range(2)
    for c in range(NC)
]
TO_NEIGHBOUR = [(dp_of(x, y, c), dp_of(x, (y + 1 - 2 * c) % NY, c)) for x, y, c in CHIPS]
OTHER_CORE = [(dp_of(x, y, c), dp_of(x, y, 1 - c)) for x, y, c in CHIPS]

HOME = [
    (dp_of(x, y, c) * NZ + 2 * q + h, dp_of((x + q) % NX, y, c) * NZ + 2 * x + h)
    for x, y, c in CHIPS
    for q in range(NX)
    for h in range(2)
]

FINISH_FLOPS = int(4e9)
VMEM_BYTES = 24 * 1024 * 1024
TILE_VMEM_BYTES = 62 * 1024 * 1024


def whole(count):
    return [pl.BlockSpec(memory_space=pltpu.VMEM)] * count


def in_hbm(count):
    return [pl.BlockSpec(memory_space=pltpu.HBM)] * count


def spread_kernel(grads, out_ref, sems):
    copies = [pltpu.make_async_copy(grads, out_ref.at[x], sems.at[x]) for x in range(NX)]
    for copy in copies:
        copy.start()
    for copy in copies:
        copy.wait()


def spread(grads):
    return pl.pallas_call(
        spread_kernel,
        out_shape=jax.ShapeDtypeStruct((NX,) + grads.shape, grads.dtype),
        in_specs=whole(1),
        out_specs=in_hbm(1)[0],
        scratch_shapes=[pltpu.SemaphoreType.DMA((NX,))],
    )(grads)


def products(left, right, x, out_ref, buffer, sems):
    tokens = out_ref.shape[1]
    half = right.shape[0] // 2
    copies = []
    for h in range(2):
        product = lax.dot_general(
            left[...],
            right[h * half : (h + 1) * half, :],
            (((1,), (1,)), ((), ())),
            preferred_element_type=jnp.float32,
        ).astype(jnp.bfloat16)
        for block in range(NX):
            k = 2 * block + h
            buffer[k, :, :half] = product[block * tokens : (block + 1) * tokens]
            piece = 2 * lax.rem(block - x + NX, NX) + h
            copies.append(
                pltpu.make_async_copy(buffer.at[k], out_ref.at[piece], sems.at[k])
            )
            copies[-1].start()
    return copies


def place(right, height, j, core, mine, other):
    right[pl.ds(pl.multiple_of((NC * j + core) * height, height), height), :] = mine
    right[pl.ds(pl.multiple_of((NC * j + 1 - core) * height, height), height), :] = other


def first_kernel(
    where_ref, left, same, same_other, features, basis, out_ref, near_ref, right, part, buffer,
    sems, near_sems, sem
):
    x, core, z = where_ref[0], where_ref[1], where_ref[2]
    height, width = same.shape[1], features.shape[1]
    start = pl.multiple_of(z * width, width)
    copy = pltpu.make_async_copy(basis.at[pl.ds(start, width), :], part, sem)
    copy.start()
    copies = [
        pltpu.make_async_copy(
            rows.at[pl.ds(NY // 4 * core, NY // 4)], near_ref.at[k], near_sems.at[k]
        )
        for k, rows in enumerate((same, same_other))
    ]
    for near in copies:
        near.start()
    for j in range(NY // 2):
        place(right, height, j, core, same[j], same_other[j])
    copy.wait()
    coords = jnp.dot(features[...], part[...], preferred_element_type=jnp.float32).astype(
        jnp.bfloat16
    )
    for k in range(NZ):
        buffer[k, :, right.shape[0] // 2 :] = coords
    copies += products(left, right, x, out_ref, buffer, sems)
    for piece in copies:
        piece.wait()


def second_kernel(where_ref, left, near, far, out_ref, right, buffer, sems):
    x, core = where_ref[0], where_ref[1]
    height = near.shape[2]
    for j in range(NY // 4):
        place(right, height, NY // 4 * core + j, core, near[0, j], near[1, j])
        place(right, height, NY // 4 * (1 - core) + j, 1 - core, far[0, j], far[1, j])
    for piece in products(left, right, x, out_ref, buffer, sems):
        piece.wait()


def tile_cost(tokens, hidden, rows):
    return pl.CostEstimate(
        flops=2 * tokens * hidden * rows,
        bytes_accessed=2 * (tokens * hidden + rows * hidden + tokens * rows),
        transcendentals=0,
    )


def first_tiles(where, grads, same, same_other, features, basis):
    tokens, hidden = grads.shape[1:]
    count, height = same.shape[:2]
    width, rank = features.shape[1], basis.shape[1]
    rows = 2 * count * height
    return pl.pallas_call(
        first_kernel,
        out_shape=(
            jax.ShapeDtypeStruct((NZ, tokens, rows // 2 + rank), jnp.bfloat16),
            jax.ShapeDtypeStruct((2, count // 2, height, hidden), jnp.bfloat16),
        ),
        in_specs=[pl.BlockSpec(memory_space=pltpu.SMEM)] + whole(4) + in_hbm(1),
        out_specs=tuple(in_hbm(2)),
        scratch_shapes=[
            pltpu.VMEM((rows, hidden), jnp.bfloat16),
            pltpu.VMEM((width, rank), jnp.bfloat16),
            pltpu.VMEM((NZ, tokens, rows // 2 + rank), jnp.bfloat16),
            pltpu.SemaphoreType.DMA((NZ,)),
            pltpu.SemaphoreType.DMA((2,)),
            pltpu.SemaphoreType.DMA,
        ],
        compiler_params=pltpu.CompilerParams(vmem_limit_bytes=TILE_VMEM_BYTES),
        cost_estimate=tile_cost(NX * tokens, hidden, rows),
    )(where, grads.reshape(NX * tokens, hidden), same, same_other, features, basis)


def second_tiles(where, grads, near, far):
    tokens, hidden = grads.shape[1:]
    rows = (near.size + far.size) // hidden
    return pl.pallas_call(
        second_kernel,
        out_shape=jax.ShapeDtypeStruct((NZ, tokens, rows // 2), jnp.bfloat16),
        in_specs=[pl.BlockSpec(memory_space=pltpu.SMEM)] + whole(3),
        out_specs=in_hbm(1)[0],
        scratch_shapes=[
            pltpu.VMEM((rows, hidden), jnp.bfloat16),
            pltpu.VMEM((NZ, tokens, rows // 2), jnp.bfloat16),
            pltpu.SemaphoreType.DMA((NZ,)),
        ],
        compiler_params=pltpu.CompilerParams(vmem_limit_bytes=TILE_VMEM_BYTES),
        cost_estimate=tile_cost(NX * tokens, hidden, rows),
    )(where, grads.reshape(NX * tokens, hidden), near, far)


def sum_kernel(pieces, summed_ref, coords_ref):
    total = jnp.sum(pieces[...].astype(jnp.float32), axis=0)
    width = summed_ref.shape[1]
    summed_ref[...] = total[:, :width]
    coords_ref[...] = total[:, width:].astype(jnp.bfloat16)


def sum_first(pieces, rank):
    tokens, width = pieces.shape[1:]
    return pl.pallas_call(
        sum_kernel,
        out_shape=(
            jax.ShapeDtypeStruct((tokens, width - rank), jnp.float32),
            jax.ShapeDtypeStruct((tokens, rank), jnp.bfloat16),
        ),
        in_specs=whole(1),
        out_specs=tuple(whole(2)),
        compiler_params=pltpu.CompilerParams(vmem_limit_bytes=VMEM_BYTES),
    )(pieces)


def finish_kernel(where_ref, first, second, out_ref):
    parity = where_ref[3]
    width = first.shape[1] // 2
    for j in range(2):
        for mine, at in ((first, parity), (second, 1 - parity)):
            start = pl.multiple_of((2 * j + at) * width, width)
            out_ref[:, pl.ds(start, width)] = mine[:, j * width : (j + 1) * width]


def finish(where, first, second):
    tokens, width = first.shape
    return pl.pallas_call(
        finish_kernel,
        out_shape=jax.ShapeDtypeStruct((tokens, 2 * width), jnp.bfloat16),
        in_specs=[pl.BlockSpec(memory_space=pltpu.SMEM)] + whole(2),
        out_specs=pl.BlockSpec(memory_space=pltpu.VMEM),
        compiler_params=pltpu.CompilerParams(vmem_limit_bytes=VMEM_BYTES),
        cost_estimate=pl.CostEstimate(flops=FINISH_FLOPS, bytes_accessed=0, transcendentals=0),
    )(where, first, second)


def proj_kernel(where_ref, grads, coords, out_ref, proj):
    proj[...] = lax.dot_general(
        grads[...], coords[...], (((0,), (0,)), ((), ())), preferred_element_type=jnp.float32
    )
    parts, share, _ = out_ref.shape
    at = pl.multiple_of(where_ref[0] * (parts * share), parts * share)
    own = proj[pl.ds(at, parts * share), :]
    for k in range(parts):
        out_ref[k] = own[k * share : (k + 1) * share]


def project(where, grads, coords):
    hidden, rank = grads.shape[2], coords.shape[1]
    return pl.pallas_call(
        proj_kernel,
        out_shape=jax.ShapeDtypeStruct((NY * NC, hidden // (NX * NY * NC), rank), jnp.float32),
        in_specs=[pl.BlockSpec(memory_space=pltpu.SMEM)] + whole(2),
        out_specs=pl.BlockSpec(memory_space=pltpu.VMEM),
        scratch_shapes=[pltpu.VMEM((hidden, rank), jnp.float32)],
        compiler_params=pltpu.CompilerParams(vmem_limit_bytes=VMEM_BYTES),
    )(where, grads.reshape(-1, hidden), coords)


def adam_kernel(parts_ref, basis_ref, one_ref, two_ref, new_one_ref, new_two_ref, direction_ref):
    projected = jnp.sum(parts_ref[...], axis=0)
    new_one = beta_one * one_ref[:, 0, :] + (1.0 - beta_one) * projected
    new_two = beta_two * two_ref[:, 0, :] + (1.0 - beta_two) * projected * projected
    new_one_ref[:, 0, :] = new_one
    new_two_ref[:, 0, :] = new_two
    step_dir = new_one / bias_one / (jnp.sqrt(new_two / bias_two) + adam_epsilon)
    direction_ref[:, 0, :] = lax.dot_general(
        step_dir.astype(jnp.bfloat16),
        basis_ref[...],
        (((1,), (1,)), ((), ())),
        preferred_element_type=jnp.float32,
    )


def adam(parts, basis, one, two):
    rows = one.shape[0]
    return pl.pallas_call(
        adam_kernel,
        out_shape=(
            jax.ShapeDtypeStruct(one.shape, jnp.float32),
            jax.ShapeDtypeStruct(one.shape, jnp.float32),
            jax.ShapeDtypeStruct((rows, 1, basis.shape[0]), jnp.float32),
        ),
        in_specs=whole(4),
        out_specs=tuple(whole(3)),
        compiler_params=pltpu.CompilerParams(vmem_limit_bytes=VMEM_BYTES),
    )(parts, basis, one, two)


def body(features, out_grad, weight, basis, moment_one, moment_two):
    dp = lax.axis_index("dp")
    x, y, core = dp // (NY * NC), (dp // NC) % NY, dp % NC
    where = jnp.stack([x, core, lax.axis_index("tensor"), y % 2])

    grads = lax.all_to_all(spread(out_grad), "dp", 0, 0, axis_index_groups=ALONG_X)
    same = lax.all_gather(weight, "dp", axis=0, axis_index_groups=SAME_PARITY)
    same, grads = lax.optimization_barrier((same, grads))

    same_other = lax.ppermute(same, "dp", OTHER_CORE)
    first, near = first_tiles(where, grads, same, same_other, features, basis)
    first = lax.all_to_all(first, "tensor", 0, 0)

    near = lax.ppermute(near, "dp", TO_NEIGHBOUR)
    far = lax.ppermute(near, "dp", OTHER_CORE)
    second = second_tiles(where, grads, near, far)
    first, second = lax.optimization_barrier((first, second))
    second = lax.all_to_all(second, "tensor", 0, 0)
    first, coords = sum_first(first, basis.shape[1])

    coords = lax.all_gather(coords, "dp", axis=0, tiled=True, axis_index_groups=ALONG_X)
    parts = project(where, grads, coords)
    parts, second = lax.optimization_barrier((parts, second))

    summed = jnp.sum(second.astype(jnp.float32), axis=0)
    summed = jnp.concatenate([first, summed], axis=1).astype(jnp.bfloat16)
    summed = lax.ppermute(summed, ("dp", "tensor"), HOME)
    half = summed.shape[1] // 2
    feature_grad = finish(where, summed[:, :half], summed[:, half:])

    parts = lax.all_to_all(parts, "dp", 0, 0, axis_index_groups=ALONG_YC)
    results = adam(parts, basis, *(jnp.swapaxes(m, 0, 1) for m in (moment_one, moment_two)))
    return (feature_grad, *(jnp.swapaxes(r, 0, 1) for r in results))


def solution(mesh):
    in_specs = (
        P("dp", "tensor"),
        P("dp", "tensor"),
        P("dp", "tensor"),
        P(),
        P("tensor", "dp", None),
        P("tensor", "dp", None),
    )
    out_specs = (
        P("dp", "tensor"),
        P("tensor", "dp", None),
        P("tensor", "dp", None),
        P("tensor", "dp", None),
    )
    return jax.shard_map(body, mesh=mesh, in_specs=in_specs, out_specs=out_specs, check_vma=False)
```

time: 364 us -> 122 us (0.34)
  the two profiles are of different devices: /device:TPU:6 before, /device:TPU:5 now
where the time goes in v2:
time: 122 us; the launch traced here: 121 us
  starting transfers between devices  37.9 us (31%)
  waiting for transfers between devices  33.1 us (27%)
  blocking collectives  31.6 us (26%)
  Pallas kernels  16.1 us (13%)
    all_gather x1, blocking collectives, body(): same = lax.all_gather(weight, 'dp', axis=0, axis_index_groups=SAME_PARITY)  21.9 us
    all_gather x1, blocking collectives, body(): lax.all_gather(coords, 'dp', axis=0, tiled=True, axis_index_groups=ALONG_X)  9.72 us
    all_to_all x1, waiting for transfers between devices, body(): first = lax.all_to_all(first, 'tensor', 0, 0)  9.43 us
    all_to_all x1, starting transfers between devices, body(): first = lax.all_to_all(first, 'tensor', 0, 0)  9.25 us
    all_to_all x1, starting transfers between devices, body(): parts = lax.all_to_all(parts, 'dp', 0, 0, axis_index_groups=ALONG_YC)  7.26 us
    all_to_all x1, waiting for transfers between devices, body(): parts = lax.all_to_all(parts, 'dp', 0, 0, axis_index_groups=ALONG_YC)  6.53 us
    all_to_all x1, waiting for transfers between devices, body(): second = lax.all_to_all(second, 'tensor', 0, 0)  6.07 us
    ppermute x1, starting transfers between devices, body(): same_other = lax.ppermute(same, 'dp', OTHER_CORE)  5.29 us
  transfers between devices with their start and end apart: 8, of which 7 were waited for; matrix products, arithmetic and copies ran while one was open for 1% of the time, Pallas kernels for 6%

profile of v2, /device:TPU:5, one launch (start us, length us, event | category | flops | bytes accessed | tf_op | source)
XLA Modules:
  0.0 121.2 jit_solution(16915515296126397267)
XLA Ops:
  0.6 2.3 %shard_map.93 = bf16[4,128,1792]{2,1,0:T(8,128)(2,1)} custom-call(bf16[128,1792]{1,0:T(8,128)(2,1)} %grads.1), custom_call_target="tpu_custom_call" | custom-call | tf_op jit(solution)/shard_map/pallas_call | solution.py:62
  3.0 0.0 copy-start.8
  3.0 4.4 %all-to-all-start = ((bf16[4,128,1792]{2,1,0:T(8,128)(2,1)}), bf16[4,128,1792]{2,1,0:T(8,128)(2,1)S(1)}, u32[]{:S(2)}, u32[]{:S(2)}) async-start(bf16[4,128,1792]{2,1,0:T(8,128)(2,1)} %shard_map.93), calls=%async_computation | async-start | bytes 3670016 | tf_op jit(solution)/shard_map/all_to_all | solution.py:290
  7.4 0.0 copy-done.8
  7.4 21.9 %all-gather = bf16[256,1792]{1,0:T(8,128)(2,1)S(1)} all-gather(bf16[64,1792]{1,0:T(8,128)(2,1)S(1)} %copy-done.8), channel_id=2, replica_groups={{0,32,64,96},{8,40,72,104},{16,48,80,112},{24,56,88,120},{128,160,192,2..., dimensions={0}, use_global_device_ids=true | all-gather | bytes 1146880 | tf_op jit(solution)/shard_map/all_gather | solution.py:291
  29.2 0.0 copy-start.6
  29.2 0.0 all-to-all-done
  29.2 0.0 copy-start
  29.2 0.9 copy-done.6
  30.2 5.3 %collective-permute-start = (bf16[4,64,1792]{2,1,0:T(8,128)(2,1)S(1)}, bf16[4,64,1792]{2,1,0:T(8,128)(2,1)}, u32[]{:S(2)}, u32[]{:S(2)}) collective-permute-start(bf16[4,64,1792]{2,1,0:T(8,128)(2,1)S(1)} %bitcast.16), channel_id=1, source_target_pairs={{0,8},{8,0},{16,24},{24,16},{32,40},{40,32},{48,56},{56,48},{64,72... | collective-permute-start | bytes 2752520 | tf_op jit(solution)/shard_map/ppermute | solution.py:294
  35.5 0.6 pad_add_fusion.where_ref
  36.1 1.5 %collective-permute-done.same_other = bf16[4,64,1792]{2,1,0:T(8,128)(2,1)} collective-permute-done((bf16[4,64,1792]{2,1,0:T(8,128)(2,1)S(1)}, bf16[4,64,1792]{2,1,0:T(8,128)(2,1)}, u32[]{:S(2)}, u32[]{:S(2)}) %collective-permute-start) | collective-permute-done | bytes 917536 | tf_op jit(solution)/shard_map/ppermute | solution.py:294
  37.7 0.0 copy-done
  37.7 5.1 %shard_map.94 = (bf16[8,128,384]{2,1,0:T(8,128)(2,1)}, bf16[2,2,64,1792]{3,2,1,0:T(8,128)(2,1)}) custom-call(s32[4]{0:T(128)} %pad_add_fusion.where_ref, bf16[512,1792]{1,0:T(8,128)(2,1)} %bitcast.11, bf16[4,64,1792]{2,1,0:T(8,128)(2,1)} %bitcast.17, bf16[4,64,1792]{2,1,0:T(8,128)(2,1)} %collective-permute-done.same_other, bf16[128,512]{1,0:T(8,128)(2,1)} %features.1, ...), custom_call_target="tpu_custom_call" | custom-call | flops 939524096 | bytes 4194304 | tf_op jit(solution)/shard_map/pallas_call | solution.py:151
  42.8 1.9 %collective-permute-start.1 = (bf16[2,2,64,1792]{3,2,1,0:T(8,128)(2,1)}, bf16[2,2,64,1792]{3,2,1,0:T(8,128)(2,1)S(1)}, u32[]{:S(2)}, u32[]{:S(2)}) collective-permute-start(bf16[2,2,64,1792]{3,2,1,0:T(8,128)(2,1)} %get-tuple-element.20), channel_id=1, source_target_pairs={{0,16},{8,120},{16,32},{24,8},{32,48},{40,24},{48,64},{56,40},{64,... | collective-permute-start | bytes 2752520 | tf_op jit(solution)/shard_map/ppermute | solution.py:298
  44.8 9.3 %all-to-all-start.1 = ((bf16[8,128,384]{2,1,0:T(8,128)(2,1)}), bf16[8,128,384]{2,1,0:T(8,128)(2,1)S(1)}, u32[]{:S(2)}, u32[]{:S(2)}) async-start(bf16[8,128,384]{2,1,0:T(8,128)(2,1)} %get-tuple-element.19), calls=%async_computation.1 | async-start | bytes 1572864 | tf_op jit(solution)/shard_map/all_to_all | solution.py:296
  54.0 3.5 %collective-permute-done.1.near = bf16[2,2,64,1792]{3,2,1,0:T(8,128)(2,1)S(1)} collective-permute-done((bf16[2,2,64,1792]{3,2,1,0:T(8,128)(2,1)}, bf16[2,2,64,1792]{3,2,1,0:T(8,128)(2,1)S(1)}, u32[]{:S(2)}, u32[]{:S(2)}) %collective-permute-start.1) | collective-permute-done | bytes 917536 | tf_op jit(solution)/shard_map/ppermute | solution.py:298
  57.5 0.0 copy-start.7
  57.5 4.3 %collective-permute-start.2 = (bf16[2,2,64,1792]{3,2,1,0:T(8,128)(2,1)S(1)}, bf16[2,2,64,1792]{3,2,1,0:T(8,128)(2,1)}, u32[]{:S(2)}, u32[]{:S(2)}) collective-permute-start(bf16[2,2,64,1792]{3,2,1,0:T(8,128)(2,1)S(1)} %collective-permute-done.1.near), channel_id=1, source_target_pairs={{0,8},{8,0},{16,24},{24,16},{32,40},{40,32},{48,56},{56,48},{64,72... | collective-permute-start | bytes 2752520 | tf_op jit(solution)/shard_map/ppermute | solution.py:299
  61.8 2.2 %collective-permute-done.2.far = bf16[2,2,64,1792]{3,2,1,0:T(8,128)(2,1)} collective-permute-done((bf16[2,2,64,1792]{3,2,1,0:T(8,128)(2,1)S(1)}, bf16[2,2,64,1792]{3,2,1,0:T(8,128)(2,1)}, u32[]{:S(2)}, u32[]{:S(2)}) %collective-permute-start.2) | collective-permute-done | bytes 917536 | tf_op jit(solution)/shard_map/ppermute | solution.py:299
  64.0 0.0 copy-done.7
  64.0 4.1 %shard_map.95 = bf16[8,128,256]{2,1,0:T(8,128)(2,1)} custom-call(s32[4]{0:T(128)} %pad_add_fusion.where_ref, bf16[512,1792]{1,0:T(8,128)(2,1)} %bitcast.12, bf16[2,2,64,1792]{3,2,1,0:T(8,128)(2,1)} %copy-done.7, bf16[2,2,64,1792]{3,2,1,0:T(8,128)(2,1)} %collective-permute-done.2.far), custom_call_target="tpu_custom_call" | custom-call | flops 939524096 | bytes 4194304 | tf_op jit(solution)/shard_map/pallas_call | solution.py:175
  68.1 0.0 copy-start.1
  68.1 0.0 copy-start.5
  68.2 9.4 %all-to-all-done.1.pieces = bf16[8,128,384]{2,1,0:T(8,128)(2,1)S(1)} async-done(((bf16[8,128,384]{2,1,0:T(8,128)(2,1)}), bf16[8,128,384]{2,1,0:T(8,128)(2,1)S(1)}, u32[]{:S(2)}, u32[]{:S(2)}) %all-to-all-start.1) | async-done | bytes 786464 | tf_op jit(solution)/shard_map/all_to_all | solution.py:296
  77.6 3.5 %all-to-all-start.2 = ((bf16[8,128,256]{2,1,0:T(8,128)(2,1)}), bf16[8,128,256]{2,1,0:T(8,128)(2,1)S(1)}, u32[]{:S(2)}, u32[]{:S(2)}) async-start(bf16[8,128,256]{2,1,0:T(8,128)(2,1)} %shard_map.95), calls=%async_computation.2 | async-start | bytes 1048576 | tf_op jit(solution)/shard_map/all_to_all | solution.py:302
  81.1 0.1 shard_map.96
  81.2 9.7 %all_gather.11.coords = bf16[512,128]{1,0:T(8,128)(2,1)S(1)} all-gather(bf16[128,128]{1,0:T(8,128)(2,1)S(1)} %get-tuple-element.23), channel_id=1, replica_groups={{0,128,256,384},{8,136,264,392},{16,144,272,400},{24,152,280,408},{32,1..., dimensions={0}, use_global_device_ids=true | all-gather | bytes 163840 | tf_op jit(solution)/shard_map/all_gather | solution.py:305
  90.9 0.0 copy-done.1
  90.9 0.0 copy-done.5
  90.9 2.0 %shard_map.97 = f32[16,28,128]{2,1,0:T(8,128)} custom-call(s32[4]{0:T(128)S(1)} %copy-done.5, bf16[512,1792]{1,0:T(8,128)(2,1)S(1)} %bitcast.13, bf16[512,128]{1,0:T(8,128)(2,1)S(1)} %all_gather.11.coords), custom_call_target="tpu_custom_call" | custom-call | tf_op jit(solution)/shard_map/pallas_call | solution.py:245
  92.9 6.1 %all-to-all-done.2 = bf16[8,128,256]{2,1,0:T(8,128)(2,1)S(1)} async-done(((bf16[8,128,256]{2,1,0:T(8,128)(2,1)}), bf16[8,128,256]{2,1,0:T(8,128)(2,1)S(1)}, u32[]{:S(2)}, u32[]{:S(2)}) %all-to-all-start.2) | async-done | bytes 524320 | tf_op jit(solution)/shard_map/all_to_all | solution.py:302
  99.0 0.1 reduce
  99.1 1.9 %collective-permute-start.3 = (bf16[128,512]{1,0:T(8,128)(2,1)S(1)}, bf16[128,512]{1,0:T(8,128)(2,1)S(1)}, u32[]{:S(2)}, u32[]{:S(2)}) collective-permute-start(bf16[128,512]{1,0:T(8,128)(2,1)S(1)} %pad_maximum_fusion), channel_id=1, source_target_pairs={{0,0},{1,1},{2,128},{3,129},{4,256},{5,257},{6,384},{7,385},{8,8},... | collective-permute-start | bytes 393224 | tf_op jit(solution)/shard_map/ppermute | solution.py:311
  101.0 7.3 %all-to-all-start.3 = ((f32[16,28,128]{2,1,0:T(8,128)}), f32[16,28,128]{2,1,0:T(8,128)S(1)}, u32[]{:S(2)}, u32[]{:S(2)}) async-start(f32[16,28,128]{2,1,0:T(8,128)} %shard_map.97), calls=%async_computation.3 | async-start | bytes 524288 | tf_op jit(solution)/shard_map/all_to_all | solution.py:315
  108.2 3.9 %collective-permute-done.3 = bf16[128,512]{1,0:T(8,128)(2,1)S(1)} collective-permute-done((bf16[128,512]{1,0:T(8,128)(2,1)S(1)}, bf16[128,512]{1,0:T(8,128)(2,1)S(1)}, u32[]{:S(2)}, u32[]{:S(2)}) %collective-permute-start.3) | collective-permute-done | bytes 131104 | tf_op jit(solution)/shard_map/ppermute | solution.py:311
  112.2 0.0 copy-start.2
  112.2 0.0 copy-start.3
  112.2 0.0 copy-start.4
  112.2 1.2 %shard_map.98 = bf16[128,512]{1,0:T(8,128)(2,1)} custom-call(s32[4]{0:T(128)S(1)} %copy-done.5, bf16[128,256]{1,0:T(8,128)(2,1)S(1)} %get-tuple-element.31.first, bf16[128,256]{1,0:T(8,128)(2,1)S(1)} %get-tuple-element.30.second), custom_call_target="tpu_custom_call" | custom-call | flops 4000000000 | tf_op jit(solution)/shard_map/pallas_call | solution.py:222
  113.4 6.5 %all-to-all-done.3.parts_ref = f32[16,28,128]{2,1,0:T(8,128)S(1)} async-done(((f32[16,28,128]{2,1,0:T(8,128)}), f32[16,28,128]{2,1,0:T(8,128)S(1)}, u32[]{:S(2)}, u32[]{:S(2)}) %all-to-all-start.3) | async-done | bytes 229408 | tf_op jit(solution)/shard_map/all_to_all | solution.py:315
  120.0 0.0 copy-done.2
  120.0 0.0 copy-done.3
  120.0 0.0 copy-done.4
  120.0 1.3 %shard_map.99 = (f32[28,1,128]{2,1,0:T(1,128)}, f32[28,1,128]{2,1,0:T(1,128)}, f32[28,1,4096]{2,1,0:T(1,128)}) custom-call(f32[16,28,128]{2,1,0:T(8,128)S(1)} %all-to-all-done.3.parts_ref, bf16[4096,128]{1,0:T(8,128)(2,1)S(1)} %copy-done.2, f32[28,1,128]{2,1,0:T(1,128)S(1)} %bitcast.14, f32[28,1,128]{2,1,0:T(1,128)S(1)} %bitcast.15), custom_call_target="tpu_custom_call" | custom-call | tf_op jit(solution)/shard_map/pallas_call | solution.py:272
  (3 shorter events, 0.0 us)
Async XLA Ops:
  3.0 4.4 %copy-start.8 = (bf16[64,1792]{1,0:T(8,128)(2,1)S(1)}, bf16[64,1792]{1,0:T(8,128)(2,1)}, u32[]{:S(2)}) copy-start(bf16[64,1792]{1,0:T(8,128)(2,1)} %param.8) | copy-start | bytes 688132
  3.0 26.3 %all-to-all-start = ((bf16[4,128,1792]{2,1,0:T(8,128)(2,1)}), bf16[4,128,1792]{2,1,0:T(8,128)(2,1)S(1)}, u32[]{:S(2)}, u32[]{:S(2)}) async-start(bf16[4,128,1792]{2,1,0:T(8,128)(2,1)} %shard_map.93), calls=%async_computation | async-start | bytes 3670016 | tf_op jit(solution)/shard_map/all_to_all | solution.py:290
  29.2 0.9 copy-start.6
  29.2 8.4 %copy-start = (bf16[4,128,1792]{2,1,0:T(8,128)(2,1)}, bf16[4,128,1792]{2,1,0:T(8,128)(2,1)S(1)}, u32[]{:S(2)}) copy-start(bf16[4,128,1792]{2,1,0:T(8,128)(2,1)S(1)} %all-to-all-done) | copy-start | bytes 5505028
  30.2 7.5 %collective-permute-start = (bf16[4,64,1792]{2,1,0:T(8,128)(2,1)S(1)}, bf16[4,64,1792]{2,1,0:T(8,128)(2,1)}, u32[]{:S(2)}, u32[]{:S(2)}) collective-permute-start(bf16[4,64,1792]{2,1,0:T(8,128)(2,1)S(1)} %bitcast.16), channel_id=1, source_target_pairs={{0,8},{8,0},{16,24},{24,16},{32,40},{40,32},{48,56},{56,48},{64,72... | collective-permute-start | bytes 2752520 | tf_op jit(solution)/shard_map/ppermute | solution.py:294
  42.8 14.6 %collective-permute-start.1 = (bf16[2,2,64,1792]{3,2,1,0:T(8,128)(2,1)}, bf16[2,2,64,1792]{3,2,1,0:T(8,128)(2,1)S(1)}, u32[]{:S(2)}, u32[]{:S(2)}) collective-permute-start(bf16[2,2,64,1792]{3,2,1,0:T(8,128)(2,1)} %get-tuple-element.20), channel_id=1, source_target_pairs={{0,16},{8,120},{16,32},{24,8},{32,48},{40,24},{48,64},{56,40},{64,... | collective-permute-start | bytes 2752520 | tf_op jit(solution)/shard_map/ppermute | solution.py:298
  44.8 32.8 %all-to-all-start.1 = ((bf16[8,128,384]{2,1,0:T(8,128)(2,1)}), bf16[8,128,384]{2,1,0:T(8,128)(2,1)S(1)}, u32[]{:S(2)}, u32[]{:S(2)}) async-start(bf16[8,128,384]{2,1,0:T(8,128)(2,1)} %get-tuple-element.19), calls=%async_computation.1 | async-start | bytes 1572864 | tf_op jit(solution)/shard_map/all_to_all | solution.py:296
  57.5 6.6 %copy-start.7 = (bf16[2,2,64,1792]{3,2,1,0:T(8,128)(2,1)}, bf16[2,2,64,1792]{3,2,1,0:T(8,128)(2,1)S(1)}, u32[]{:S(2)}) copy-start(bf16[2,2,64,1792]{3,2,1,0:T(8,128)(2,1)S(1)} %collective-permute-done.1.near) | copy-start | bytes 2752516
  57.5 6.6 %collective-permute-start.2 = (bf16[2,2,64,1792]{3,2,1,0:T(8,128)(2,1)S(1)}, bf16[2,2,64,1792]{3,2,1,0:T(8,128)(2,1)}, u32[]{:S(2)}, u32[]{:S(2)}) collective-permute-start(bf16[2,2,64,1792]{3,2,1,0:T(8,128)(2,1)S(1)} %collective-permute-done.1.near), channel_id=1, source_target_pairs={{0,8},{8,0},{16,24},{24,16},{32,40},{40,32},{48,56},{56,48},{64,72... | collective-permute-start | bytes 2752520 | tf_op jit(solution)/shard_map/ppermute | solution.py:299
  68.1 22.8 %copy-start.1 = (bf16[4,128,1792]{2,1,0:T(8,128)(2,1)S(1)}, bf16[4,128,1792]{2,1,0:T(8,128)(2,1)}, u32[]{:S(2)}) copy-start(bf16[4,128,1792]{2,1,0:T(8,128)(2,1)} %copy-done) | copy-start | bytes 5505028
  68.1 22.8 %copy-start.5 = (s32[4]{0:T(128)S(1)}, s32[4]{0:T(128)}, u32[]{:S(2)}) copy-start(s32[4]{0:T(128)} %pad_add_fusion.where_ref) | copy-start | bytes 52
  77.6 21.4 %all-to-all-start.2 = ((bf16[8,128,256]{2,1,0:T(8,128)(2,1)}), bf16[8,128,256]{2,1,0:T(8,128)(2,1)S(1)}, u32[]{:S(2)}, u32[]{:S(2)}) async-start(bf16[8,128,256]{2,1,0:T(8,128)(2,1)} %shard_map.95), calls=%async_computation.2 | async-start | bytes 1048576 | tf_op jit(solution)/shard_map/all_to_all | solution.py:302
  99.1 13.1 %collective-permute-start.3 = (bf16[128,512]{1,0:T(8,128)(2,1)S(1)}, bf16[128,512]{1,0:T(8,128)(2,1)S(1)}, u32[]{:S(2)}, u32[]{:S(2)}) collective-permute-start(bf16[128,512]{1,0:T(8,128)(2,1)S(1)} %pad_maximum_fusion), channel_id=1, source_target_pairs={{0,0},{1,1},{2,128},{3,129},{4,256},{5,257},{6,384},{7,385},{8,8},... | collective-permute-start | bytes 393224 | tf_op jit(solution)/shard_map/ppermute | solution.py:311
  101.0 19.0 %all-to-all-start.3 = ((f32[16,28,128]{2,1,0:T(8,128)}), f32[16,28,128]{2,1,0:T(8,128)S(1)}, u32[]{:S(2)}, u32[]{:S(2)}) async-start(f32[16,28,128]{2,1,0:T(8,128)} %shard_map.97), calls=%async_computation.3 | async-start | bytes 524288 | tf_op jit(solution)/shard_map/all_to_all | solution.py:315
  112.2 7.8 %copy-start.2 = (bf16[4096,128]{1,0:T(8,128)(2,1)S(1)}, bf16[4096,128]{1,0:T(8,128)(2,1)}, u32[]{:S(2)}) copy-start(bf16[4096,128]{1,0:T(8,128)(2,1)} %basis_ref.1) | copy-start | bytes 3145732
  112.2 7.8 %copy-start.3 = (f32[1,28,128]{2,0,1:T(1,128)S(1)}, f32[1,28,128]{2,0,1:T(1,128)}, u32[]{:S(2)}) copy-start(f32[1,28,128]{2,0,1:T(1,128)} %param.10) | copy-start | bytes 43012
  112.2 7.8 %copy-start.4 = (f32[1,28,128]{2,0,1:T(1,128)S(1)}, f32[1,28,128]{2,0,1:T(1,128)}, u32[]{:S(2)}) copy-start(f32[1,28,128]{2,0,1:T(1,128)} %param.11) | copy-start | bytes 43012

commit v3 on v2

--- a/solution.py
+++ b/solution.py
@@ -18,9 +18,15 @@
     return (x * NY + y) * NC + c
 
 
+def here():
+    dp = lax.axis_index("dp")
+    y = lax.rem(lax.div(dp, NC), NY)
+    return lax.div(dp, NY * NC), y, lax.rem(dp, NC), lax.axis_index("tensor")
+
+
 CHIPS = [(x, y, c) for x in range(NX) for y in range(NY) for c in range(NC)]
 ALONG_X = [[dp_of(x, y, c) for x in range(NX)] for y in range(NY) for c in range(NC)]
-ALONG_YC = [[dp_of(x, y, c) for y in range(NY) for c in range(NC)] for x in range(NX)]
+ALONG_Y = [[dp_of(x, y, c) for y in range(NY)] for x in range(NX) for c in range(NC)]
 SAME_PARITY = [
     [dp_of(x, p + 2 * j, c) for j in range(NY // 2)]
     for x in range(NX)
@@ -38,8 +44,11 @@
 ]
 
 FINISH_FLOPS = int(4e9)
+FIRST_FLOPS = int(1e9)
+SECOND_FLOPS = int(1e9)
 VMEM_BYTES = 24 * 1024 * 1024
-TILE_VMEM_BYTES = 62 * 1024 * 1024
+FIRST_VMEM = 53_000_000
+SECOND_VMEM = 24_000_000
 
 
 def whole(count):
@@ -96,10 +105,10 @@
 
 
 def first_kernel(
-    where_ref, left, same, same_other, features, basis, out_ref, near_ref, right, part, buffer,
+    left, same, same_other, features, basis, out_ref, near_ref, right, part, buffer,
     sems, near_sems, sem
 ):
-    x, core, z = where_ref[0], where_ref[1], where_ref[2]
+    x, _, core, z = here()
     height, width = same.shape[1], features.shape[1]
     start = pl.multiple_of(z * width, width)
     copy = pltpu.make_async_copy(basis.at[pl.ds(start, width), :], part, sem)
@@ -125,8 +134,8 @@
         piece.wait()
 
 
-def second_kernel(where_ref, left, near, far, out_ref, right, buffer, sems):
-    x, core = where_ref[0], where_ref[1]
+def second_kernel(left, near, far, out_ref, right, buffer, sems):
+    x, _, core, _ = here()
     height = near.shape[2]
     for j in range(NY // 4):
         place(right, height, NY // 4 * core + j, core, near[0, j], near[1, j])
@@ -135,15 +144,7 @@
         piece.wait()
 
 
-def tile_cost(tokens, hidden, rows):
-    return pl.CostEstimate(
-        flops=2 * tokens * hidden * rows,
-        bytes_accessed=2 * (tokens * hidden + rows * hidden + tokens * rows),
-        transcendentals=0,
-    )
-
-
-def first_tiles(where, grads, same, same_other, features, basis):
+def first_tiles(grads, same, same_other, features, basis):
     tokens, hidden = grads.shape[1:]
     count, height = same.shape[:2]
     width, rank = features.shape[1], basis.shape[1]
@@ -154,7 +155,7 @@
             jax.ShapeDtypeStruct((NZ, tokens, rows // 2 + rank), jnp.bfloat16),
             jax.ShapeDtypeStruct((2, count // 2, height, hidden), jnp.bfloat16),
         ),
-        in_specs=[pl.BlockSpec(memory_space=pltpu.SMEM)] + whole(4) + in_hbm(1),
+        in_specs=whole(4) + in_hbm(1),
         out_specs=tuple(in_hbm(2)),
         scratch_shapes=[
             pltpu.VMEM((rows, hidden), jnp.bfloat16),
@@ -164,27 +165,27 @@
             pltpu.SemaphoreType.DMA((2,)),
             pltpu.SemaphoreType.DMA,
         ],
-        compiler_params=pltpu.CompilerParams(vmem_limit_bytes=TILE_VMEM_BYTES),
-        cost_estimate=tile_cost(NX * tokens, hidden, rows),
-    )(where, grads.reshape(NX * tokens, hidden), same, same_other, features, basis)
-
-
-def second_tiles(where, grads, near, far):
+        compiler_params=pltpu.CompilerParams(vmem_limit_bytes=FIRST_VMEM),
+        cost_estimate=pl.CostEstimate(flops=FIRST_FLOPS, bytes_accessed=0, transcendentals=0),
+    )(grads.reshape(NX * tokens, hidden), same, same_other, features, basis)
+
+
+def second_tiles(grads, near, far):
     tokens, hidden = grads.shape[1:]
     rows = (near.size + far.size) // hidden
     return pl.pallas_call(
         second_kernel,
         out_shape=jax.ShapeDtypeStruct((NZ, tokens, rows // 2), jnp.bfloat16),
-        in_specs=[pl.BlockSpec(memory_space=pltpu.SMEM)] + whole(3),
+        in_specs=whole(3),
         out_specs=in_hbm(1)[0],
         scratch_shapes=[
             pltpu.VMEM((rows, hidden), jnp.bfloat16),
             pltpu.VMEM((NZ, tokens, rows // 2), jnp.bfloat16),
             pltpu.SemaphoreType.DMA((NZ,)),
         ],
-        compiler_params=pltpu.CompilerParams(vmem_limit_bytes=TILE_VMEM_BYTES),
-        cost_estimate=tile_cost(NX * tokens, hidden, rows),
-    )(where, grads.reshape(NX * tokens, hidden), near, far)
+        compiler_params=pltpu.CompilerParams(vmem_limit_bytes=SECOND_VMEM),
+        cost_estimate=pl.CostEstimate(flops=SECOND_FLOPS, bytes_accessed=0, transcendentals=0),
+    )(grads.reshape(NX * tokens, hidden), near, far)
 
 
 def sum_kernel(pieces, summed_ref, coords_ref):
@@ -208,8 +209,8 @@
     )(pieces)
 
 
-def finish_kernel(where_ref, first, second, out_ref):
-    parity = where_ref[3]
+def finish_kernel(first, second, out_ref):
+    parity = lax.rem(here()[1], 2)
     width = first.shape[1] // 2
     for j in range(2):
         for mine, at in ((first, parity), (second, 1 - parity)):
@@ -217,39 +218,45 @@
             out_ref[:, pl.ds(start, width)] = mine[:, j * width : (j + 1) * width]
 
 
-def finish(where, first, second):
+def finish(first, second):
     tokens, width = first.shape
     return pl.pallas_call(
         finish_kernel,
         out_shape=jax.ShapeDtypeStruct((tokens, 2 * width), jnp.bfloat16),
-        in_specs=[pl.BlockSpec(memory_space=pltpu.SMEM)] + whole(2),
+        in_specs=whole(2),
         out_specs=pl.BlockSpec(memory_space=pltpu.VMEM),
         compiler_params=pltpu.CompilerParams(vmem_limit_bytes=VMEM_BYTES),
         cost_estimate=pl.CostEstimate(flops=FINISH_FLOPS, bytes_accessed=0, transcendentals=0),
-    )(where, first, second)
-
-
-def proj_kernel(where_ref, grads, coords, out_ref, proj):
+    )(first, second)
+
+
+def proj_kernel(grads, coords, mine_ref, other_ref, proj):
     proj[...] = lax.dot_general(
         grads[...], coords[...], (((0,), (0,)), ((), ())), preferred_element_type=jnp.float32
     )
-    parts, share, _ = out_ref.shape
-    at = pl.multiple_of(where_ref[0] * (parts * share), parts * share)
-    own = proj[pl.ds(at, parts * share), :]
+    x, _, core, _ = here()
+    parts, share, _ = mine_ref.shape
+    rows = parts * NC * share
+    own = proj[pl.ds(pl.multiple_of(x * rows, rows), rows), :]
+    first_core = core == 0
     for k in range(parts):
-        out_ref[k] = own[k * share : (k + 1) * share]
-
-
-def project(where, grads, coords):
+        at = NC * k * share
+        zero, one = own[at : at + share], own[at + share : at + NC * share]
+        mine_ref[k] = jnp.where(first_core, zero, one)
+        other_ref[k] = jnp.where(first_core, one, zero)
+
+
+def project(grads, coords):
     hidden, rank = grads.shape[2], coords.shape[1]
+    part = jax.ShapeDtypeStruct((NY, hidden // (NX * NY * NC), rank), jnp.float32)
     return pl.pallas_call(
         proj_kernel,
-        out_shape=jax.ShapeDtypeStruct((NY * NC, hidden // (NX * NY * NC), rank), jnp.float32),
-        in_specs=[pl.BlockSpec(memory_space=pltpu.SMEM)] + whole(2),
-        out_specs=pl.BlockSpec(memory_space=pltpu.VMEM),
+        out_shape=(part, part),
+        in_specs=whole(2),
+        out_specs=tuple(whole(2)),
         scratch_shapes=[pltpu.VMEM((hidden, rank), jnp.float32)],
         compiler_params=pltpu.CompilerParams(vmem_limit_bytes=VMEM_BYTES),
-    )(where, grads.reshape(-1, hidden), coords)
+    )(grads.reshape(-1, hidden), coords)
 
 
 def adam_kernel(parts_ref, basis_ref, one_ref, two_ref, new_one_ref, new_two_ref, direction_ref):
@@ -283,36 +290,32 @@
 
 
 def body(features, out_grad, weight, basis, moment_one, moment_two):
-    dp = lax.axis_index("dp")
-    x, y, core = dp // (NY * NC), (dp // NC) % NY, dp % NC
-    where = jnp.stack([x, core, lax.axis_index("tensor"), y % 2])
-
     grads = lax.all_to_all(spread(out_grad), "dp", 0, 0, axis_index_groups=ALONG_X)
     same = lax.all_gather(weight, "dp", axis=0, axis_index_groups=SAME_PARITY)
-    same, grads = lax.optimization_barrier((same, grads))
 
     same_other = lax.ppermute(same, "dp", OTHER_CORE)
-    first, near = first_tiles(where, grads, same, same_other, features, basis)
+    first, near = first_tiles(grads, same, same_other, features, basis)
     first = lax.all_to_all(first, "tensor", 0, 0)
 
     near = lax.ppermute(near, "dp", TO_NEIGHBOUR)
     far = lax.ppermute(near, "dp", OTHER_CORE)
-    second = second_tiles(where, grads, near, far)
+    second = second_tiles(grads, near, far)
     first, second = lax.optimization_barrier((first, second))
     second = lax.all_to_all(second, "tensor", 0, 0)
     first, coords = sum_first(first, basis.shape[1])
 
     coords = lax.all_gather(coords, "dp", axis=0, tiled=True, axis_index_groups=ALONG_X)
-    parts = project(where, grads, coords)
+    parts, other = project(grads, coords)
+    parts = parts + lax.ppermute(other, "dp", OTHER_CORE)
     parts, second = lax.optimization_barrier((parts, second))
 
     summed = jnp.sum(second.astype(jnp.float32), axis=0)
     summed = jnp.concatenate([first, summed], axis=1).astype(jnp.bfloat16)
     summed = lax.ppermute(summed, ("dp", "tensor"), HOME)
     half = summed.shape[1] // 2
-    feature_grad = finish(where, summed[:, :half], summed[:, half:])
-
-    parts = lax.all_to_all(parts, "dp", 0, 0, axis_index_groups=ALONG_YC)
+    feature_grad = finish(summed[:, :half], summed[:, half:])
+
+    parts = lax.all_to_all(parts, "dp", 0, 0, axis_index_groups=ALONG_Y)
     results = adam(parts, basis, *(jnp.swapaxes(m, 0, 1) for m in (moment_one, moment_two)))
     return (feature_grad, *(jnp.swapaxes(r, 0, 1) for r in results))
 

time: 122 us -> 120 us (0.984)
  the two profiles are of different devices: /device:TPU:5 before, /device:TPU:6 now
where the time goes in v3:
time: 120 us; the launch traced here: 119 us
  starting transfers between devices  40 us (33%)
  blocking collectives  31.6 us (26%)
  waiting for transfers between devices  31.2 us (26%)
  Pallas kernels  12 us (10%)
  local copies, waits for them, and re-layouts  2.82 us (2%)
    all_gather x1, blocking collectives, body(): same = lax.all_gather(weight, 'dp', axis=0, axis_index_groups=SAME_PARITY)  19.7 us
    all_gather x1, blocking collectives, body(): lax.all_gather(coords, 'dp', axis=0, tiled=True, axis_index_groups=ALONG_X)  12 us
    all_to_all x1, waiting for transfers between devices, body(): first = lax.all_to_all(first, 'tensor', 0, 0)  9.97 us
    all_to_all x1, starting transfers between devices, body(): lax.all_to_all(spread(out_grad), 'dp', 0, 0, axis_index_groups=ALONG_X)  9.55 us
    all_to_all x1, starting transfers between devices, body(): first = lax.all_to_all(first, 'tensor', 0, 0)  9.41 us
    ppermute x1, waiting for transfers between devices, body(): near = lax.ppermute(near, 'dp', TO_NEIGHBOUR)  5.37 us
    ppermute x1, starting transfers between devices, body(): summed = lax.ppermute(summed, ('dp', 'tensor'), HOME)  5.01 us
    all_to_all x1, starting transfers between devices, body(): parts = lax.all_to_all(parts, 'dp', 0, 0, axis_index_groups=ALONG_Y)  4.92 us
  transfers between devices with their start and end apart: 9, of which 8 were waited for; matrix products, arithmetic and copies ran while one was open for 1% of the time, Pallas kernels for 3%

profile of v3, /device:TPU:6, one launch (start us, length us, event | category | flops | bytes accessed | tf_op | source)
XLA Modules:
  0.0 119.2 jit_solution(123033985102854415)
XLA Ops:
  0.6 2.3 %shard_map.93 = bf16[4,128,1792]{2,1,0:T(8,128)(2,1)} custom-call(bf16[128,1792]{1,0:T(8,128)(2,1)} %grads.1), custom_call_target="tpu_custom_call" | custom-call | tf_op jit(solution)/shard_map/pallas_call | solution.py:71
  3.0 0.0 copy-start.7
  3.0 0.0 copy-start.4
  3.0 9.6 %all-to-all-start = ((bf16[4,128,1792]{2,1,0:T(8,128)(2,1)}), bf16[4,128,1792]{2,1,0:T(8,128)(2,1)S(1)}, u32[]{:S(2)}, u32[]{:S(2)}) async-start(bf16[4,128,1792]{2,1,0:T(8,128)(2,1)} %shard_map.93), calls=%async_computation | async-start | bytes 3670016 | tf_op jit(solution)/shard_map/all_to_all | solution.py:293
  12.5 0.0 copy-done.7
  12.5 19.7 %all-gather = bf16[256,1792]{1,0:T(8,128)(2,1)S(1)} all-gather(bf16[64,1792]{1,0:T(8,128)(2,1)S(1)} %copy-done.7), channel_id=2, replica_groups={{0,32,64,96},{8,40,72,104},{16,48,80,112},{24,56,88,120},{128,160,192,2..., dimensions={0}, use_global_device_ids=true | all-gather | bytes 1146880 | tf_op jit(solution)/shard_map/all_gather | solution.py:294
  32.2 1.9 %collective-permute-start = (bf16[4,64,1792]{2,1,0:T(8,128)(2,1)S(1)}, bf16[4,64,1792]{2,1,0:T(8,128)(2,1)}, u32[]{:S(2)}, u32[]{:S(2)}) collective-permute-start(bf16[4,64,1792]{2,1,0:T(8,128)(2,1)S(1)} %bitcast.10), channel_id=1, source_target_pairs={{0,8},{8,0},{16,24},{24,16},{32,40},{40,32},{48,56},{56,48},{64,72... | collective-permute-start | bytes 2752520 | tf_op jit(solution)/shard_map/ppermute | solution.py:296
  34.1 2.6 %collective-permute-done.same_other = bf16[4,64,1792]{2,1,0:T(8,128)(2,1)} collective-permute-done((bf16[4,64,1792]{2,1,0:T(8,128)(2,1)S(1)}, bf16[4,64,1792]{2,1,0:T(8,128)(2,1)}, u32[]{:S(2)}, u32[]{:S(2)}) %collective-permute-start) | collective-permute-done | bytes 917536 | tf_op jit(solution)/shard_map/ppermute | solution.py:296
  36.7 0.0 all-to-all-done
  36.7 0.0 copy-start
  36.7 1.3 %copy-done = bf16[4,128,1792]{2,1,0:T(8,128)(2,1)} copy-done((bf16[4,128,1792]{2,1,0:T(8,128)(2,1)}, bf16[4,128,1792]{2,1,0:T(8,128)(2,1)S(1)}, u32[]{:S(2)}) %copy-start) | copy-done | bytes 1835032
  38.0 0.0 copy-done.4
  38.0 4.8 %shard_map.94 = (bf16[8,128,384]{2,1,0:T(8,128)(2,1)}, bf16[2,2,64,1792]{3,2,1,0:T(8,128)(2,1)}) custom-call(bf16[512,1792]{1,0:T(8,128)(2,1)} %bitcast.7, bf16[4,64,1792]{2,1,0:T(8,128)(2,1)S(1)} %bitcast.11, bf16[4,64,1792]{2,1,0:T(8,128)(2,1)} %collective-permute-done.same_other, bf16[128,512]{1,0:T(8,128)(2,1)S(1)} %copy-done.4, bf16[4096,128]{1,0:T(8,128)(2,1)} %basis_ref.1), custom_call_target="tpu_custom_call" | custom-call | flops 1000000000 | tf_op jit(solution)/shard_map/pallas_call | solution.py:152
  42.8 1.9 %collective-permute-start.1 = (bf16[2,2,64,1792]{3,2,1,0:T(8,128)(2,1)}, bf16[2,2,64,1792]{3,2,1,0:T(8,128)(2,1)S(1)}, u32[]{:S(2)}, u32[]{:S(2)}) collective-permute-start(bf16[2,2,64,1792]{3,2,1,0:T(8,128)(2,1)} %get-tuple-element.18), channel_id=1, source_target_pairs={{0,16},{8,120},{16,32},{24,8},{32,48},{40,24},{48,64},{56,40},{64,... | collective-permute-start | bytes 2752520 | tf_op jit(solution)/shard_map/ppermute | solution.py:300
  44.7 9.4 %all-to-all-start.1 = ((bf16[8,128,384]{2,1,0:T(8,128)(2,1)}), bf16[8,128,384]{2,1,0:T(8,128)(2,1)S(1)}, u32[]{:S(2)}, u32[]{:S(2)}) async-start(bf16[8,128,384]{2,1,0:T(8,128)(2,1)} %get-tuple-element.17), calls=%async_computation.1 | async-start | bytes 1572864 | tf_op jit(solution)/shard_map/all_to_all | solution.py:298
  54.1 5.4 %collective-permute-done.1.near = bf16[2,2,64,1792]{3,2,1,0:T(8,128)(2,1)S(1)} collective-permute-done((bf16[2,2,64,1792]{3,2,1,0:T(8,128)(2,1)}, bf16[2,2,64,1792]{3,2,1,0:T(8,128)(2,1)S(1)}, u32[]{:S(2)}, u32[]{:S(2)}) %collective-permute-start.1) | collective-permute-done | bytes 917536 | tf_op jit(solution)/shard_map/ppermute | solution.py:300
  59.5 1.9 %collective-permute-start.2 = (bf16[2,2,64,1792]{3,2,1,0:T(8,128)(2,1)S(1)}, bf16[2,2,64,1792]{3,2,1,0:T(8,128)(2,1)S(1)}, u32[]{:S(2)}, u32[]{:S(2)}) collective-permute-start(bf16[2,2,64,1792]{3,2,1,0:T(8,128)(2,1)S(1)} %collective-permute-done.1.near), channel_id=1, source_target_pairs={{0,8},{8,0},{16,24},{24,16},{32,40},{40,32},{48,56},{56,48},{64,72... | collective-permute-start | bytes 2752520 | tf_op jit(solution)/shard_map/ppermute | solution.py:301
  61.4 2.4 %collective-permute-done.2.far = bf16[2,2,64,1792]{3,2,1,0:T(8,128)(2,1)S(1)} collective-permute-done((bf16[2,2,64,1792]{3,2,1,0:T(8,128)(2,1)S(1)}, bf16[2,2,64,1792]{3,2,1,0:T(8,128)(2,1)S(1)}, u32[]{:S(2)}, u32[]{:S(2)}) %collective-permute-start.2) | collective-permute-done | bytes 917536 | tf_op jit(solution)/shard_map/ppermute | solution.py:301
  63.9 0.0 copy-start.1
  63.9 1.5 %copy-done.1 = bf16[4,128,1792]{2,1,0:T(8,128)(2,1)S(1)} copy-done((bf16[4,128,1792]{2,1,0:T(8,128)(2,1)S(1)}, bf16[4,128,1792]{2,1,0:T(8,128)(2,1)}, u32[]{:S(2)}) %copy-start.1) | copy-done | bytes 1835032
  65.4 2.1 %shard_map.95 = bf16[8,128,256]{2,1,0:T(8,128)(2,1)} custom-call(bf16[512,1792]{1,0:T(8,128)(2,1)S(1)} %bitcast.8, bf16[2,2,64,1792]{3,2,1,0:T(8,128)(2,1)S(1)} %collective-permute-done.1.near, bf16[2,2,64,1792]{3,2,1,0:T(8,128)(2,1)S(1)} %collective-permute-done.2.far), custom_call_target="tpu_custom_call" | custom-call | flops 1000000000 | tf_op jit(solution)/shard_map/pallas_call | solution.py:176
  67.4 0.0 copy-start.2
  67.5 10.0 %all-to-all-done.1.pieces = bf16[8,128,384]{2,1,0:T(8,128)(2,1)S(1)} async-done(((bf16[8,128,384]{2,1,0:T(8,128)(2,1)}), bf16[8,128,384]{2,1,0:T(8,128)(2,1)S(1)}, u32[]{:S(2)}, u32[]{:S(2)}) %all-to-all-start.1) | async-done | bytes 786464 | tf_op jit(solution)/shard_map/all_to_all | solution.py:298
  77.4 3.5 %all-to-all-start.2 = ((bf16[8,128,256]{2,1,0:T(8,128)(2,1)}), bf16[8,128,256]{2,1,0:T(8,128)(2,1)S(1)}, u32[]{:S(2)}, u32[]{:S(2)}) async-start(bf16[8,128,256]{2,1,0:T(8,128)(2,1)} %shard_map.95), calls=%async_computation.2 | async-start | bytes 1048576 | tf_op jit(solution)/shard_map/all_to_all | solution.py:304
  80.9 0.1 shard_map.96
  81.0 12.0 %all_gather.11.coords = bf16[512,128]{1,0:T(8,128)(2,1)S(1)} all-gather(bf16[128,128]{1,0:T(8,128)(2,1)S(1)} %get-tuple-element.21), channel_id=1, replica_groups={{0,128,256,384},{8,136,264,392},{16,144,272,400},{24,152,280,408},{32,1..., dimensions={0}, use_global_device_ids=true | all-gather | bytes 163840 | tf_op jit(solution)/shard_map/all_gather | solution.py:307
  93.0 0.0 copy-done.2
  93.0 0.7 shard_map.97
  93.8 1.9 %collective-permute-start.3 = (f32[8,28,128]{2,1,0:T(8,128)S(1)}, f32[8,28,128]{2,1,0:T(8,128)S(1)}, u32[]{:S(2)}, u32[]{:S(2)}) collective-permute-start(f32[8,28,128]{2,1,0:T(8,128)S(1)} %get-tuple-element.23), channel_id=1, source_target_pairs={{0,8},{8,0},{16,24},{24,16},{32,40},{40,32},{48,56},{56,48},{64,72... | collective-permute-start | bytes 344072 | tf_op jit(solution)/shard_map/ppermute | solution.py:309
  95.7 1.3 %collective-permute-done.3 = f32[8,28,128]{2,1,0:T(8,128)S(1)} collective-permute-done((f32[8,28,128]{2,1,0:T(8,128)S(1)}, f32[8,28,128]{2,1,0:T(8,128)S(1)}, u32[]{:S(2)}, u32[]{:S(2)}) %collective-permute-start.3) | collective-permute-done | bytes 114720 | tf_op jit(solution)/shard_map/ppermute | solution.py:309
  97.0 0.7 add.3
  97.7 1.1 all-to-all-done.2
  98.8 0.1 reduce
  98.9 5.0 %collective-permute-start.4 = (bf16[128,512]{1,0:T(8,128)(2,1)S(1)}, bf16[128,512]{1,0:T(8,128)(2,1)S(1)}, u32[]{:S(2)}, u32[]{:S(2)}) collective-permute-start(bf16[128,512]{1,0:T(8,128)(2,1)S(1)} %pad_maximum_fusion), channel_id=1, source_target_pairs={{0,0},{1,1},{2,128},{3,129},{4,256},{5,257},{6,384},{7,385},{8,8},... | collective-permute-start | bytes 393224 | tf_op jit(solution)/shard_map/ppermute | solution.py:314
  103.9 4.9 %all-to-all-start.3 = ((f32[8,28,128]{2,1,0:T(8,128)}), f32[8,28,128]{2,1,0:T(8,128)S(1)}, u32[]{:S(2)}, u32[]{:S(2)}) async-start(f32[8,28,128]{2,1,0:T(8,128)} %add.3), calls=%async_computation.3 | async-start | bytes 262144 | tf_op jit(solution)/shard_map/all_to_all | solution.py:318
  108.8 4.6 %collective-permute-done.4 = bf16[128,512]{1,0:T(8,128)(2,1)S(1)} collective-permute-done((bf16[128,512]{1,0:T(8,128)(2,1)S(1)}, bf16[128,512]{1,0:T(8,128)(2,1)S(1)}, u32[]{:S(2)}, u32[]{:S(2)}) %collective-permute-start.4) | collective-permute-done | bytes 131104 | tf_op jit(solution)/shard_map/ppermute | solution.py:314
  113.5 0.0 copy-start.3
  113.5 0.0 copy-start.5
  113.5 0.0 copy-start.6
  113.5 0.7 shard_map.98
  114.2 3.8 %all-to-all-done.3.parts_ref = f32[8,28,128]{2,1,0:T(8,128)S(1)} async-done(((f32[8,28,128]{2,1,0:T(8,128)}), f32[8,28,128]{2,1,0:T(8,128)S(1)}, u32[]{:S(2)}, u32[]{:S(2)}) %all-to-all-start.3) | async-done | bytes 114720 | tf_op jit(solution)/shard_map/all_to_all | solution.py:318
  118.0 0.0 copy-done.3
  118.0 0.0 copy-done.5
  118.0 0.0 copy-done.6
  118.0 1.3 %shard_map.99 = (f32[28,1,128]{2,1,0:T(1,128)}, f32[28,1,128]{2,1,0:T(1,128)}, f32[28,1,4096]{2,1,0:T(1,128)}) custom-call(f32[8,28,128]{2,1,0:T(8,128)S(1)} %all-to-all-done.3.parts_ref, bf16[4096,128]{1,0:T(8,128)(2,1)S(1)} %copy-done.3, f32[28,1,128]{2,1,0:T(1,128)S(1)} %bitcast.12, f32[28,1,128]{2,1,0:T(1,128)S(1)} %bitcast.13), custom_call_target="tpu_custom_call" | custom-call | tf_op jit(solution)/shard_map/pallas_call | solution.py:279
  (3 shorter events, 0.0 us)
Async XLA Ops:
  3.0 9.6 %copy-start.7 = (bf16[64,1792]{1,0:T(8,128)(2,1)S(1)}, bf16[64,1792]{1,0:T(8,128)(2,1)}, u32[]{:S(2)}) copy-start(bf16[64,1792]{1,0:T(8,128)(2,1)} %param.8) | copy-start | bytes 688132
  3.0 35.0 %copy-start.4 = (bf16[128,512]{1,0:T(8,128)(2,1)S(1)}, bf16[128,512]{1,0:T(8,128)(2,1)}, u32[]{:S(2)}) copy-start(bf16[128,512]{1,0:T(8,128)(2,1)} %features.1) | copy-start | bytes 393220
  3.0 33.7 %all-to-all-start = ((bf16[4,128,1792]{2,1,0:T(8,128)(2,1)}), bf16[4,128,1792]{2,1,0:T(8,128)(2,1)S(1)}, u32[]{:S(2)}, u32[]{:S(2)}) async-start(bf16[4,128,1792]{2,1,0:T(8,128)(2,1)} %shard_map.93), calls=%async_computation | async-start | bytes 3670016 | tf_op jit(solution)/shard_map/all_to_all | solution.py:293
  32.2 4.5 %collective-permute-start = (bf16[4,64,1792]{2,1,0:T(8,128)(2,1)S(1)}, bf16[4,64,1792]{2,1,0:T(8,128)(2,1)}, u32[]{:S(2)}, u32[]{:S(2)}) collective-permute-start(bf16[4,64,1792]{2,1,0:T(8,128)(2,1)S(1)} %bitcast.10), channel_id=1, source_target_pairs={{0,8},{8,0},{16,24},{24,16},{32,40},{40,32},{48,56},{56,48},{64,72... | collective-permute-start | bytes 2752520 | tf_op jit(solution)/shard_map/ppermute | solution.py:296
  36.7 1.3 %copy-start = (bf16[4,128,1792]{2,1,0:T(8,128)(2,1)}, bf16[4,128,1792]{2,1,0:T(8,128)(2,1)S(1)}, u32[]{:S(2)}) copy-start(bf16[4,128,1792]{2,1,0:T(8,128)(2,1)S(1)} %all-to-all-done) | copy-start | bytes 5505028
  42.8 16.7 %collective-permute-start.1 = (bf16[2,2,64,1792]{3,2,1,0:T(8,128)(2,1)}, bf16[2,2,64,1792]{3,2,1,0:T(8,128)(2,1)S(1)}, u32[]{:S(2)}, u32[]{:S(2)}) collective-permute-start(bf16[2,2,64,1792]{3,2,1,0:T(8,128)(2,1)} %get-tuple-element.18), channel_id=1, source_target_pairs={{0,16},{8,120},{16,32},{24,8},{32,48},{40,24},{48,64},{56,40},{64,... | collective-permute-start | bytes 2752520 | tf_op jit(solution)/shard_map/ppermute | solution.py:300
  44.7 32.7 %all-to-all-start.1 = ((bf16[8,128,384]{2,1,0:T(8,128)(2,1)}), bf16[8,128,384]{2,1,0:T(8,128)(2,1)S(1)}, u32[]{:S(2)}, u32[]{:S(2)}) async-start(bf16[8,128,384]{2,1,0:T(8,128)(2,1)} %get-tuple-element.17), calls=%async_computation.1 | async-start | bytes 1572864 | tf_op jit(solution)/shard_map/all_to_all | solution.py:298
  59.5 4.4 %collective-permute-start.2 = (bf16[2,2,64,1792]{3,2,1,0:T(8,128)(2,1)S(1)}, bf16[2,2,64,1792]{3,2,1,0:T(8,128)(2,1)S(1)}, u32[]{:S(2)}, u32[]{:S(2)}) collective-permute-start(bf16[2,2,64,1792]{3,2,1,0:T(8,128)(2,1)S(1)} %collective-permute-done.1.near), channel_id=1, source_target_pairs={{0,8},{8,0},{16,24},{24,16},{32,40},{40,32},{48,56},{56,48},{64,72... | collective-permute-start | bytes 2752520 | tf_op jit(solution)/shard_map/ppermute | solution.py:301
  63.9 1.5 %copy-start.1 = (bf16[4,128,1792]{2,1,0:T(8,128)(2,1)S(1)}, bf16[4,128,1792]{2,1,0:T(8,128)(2,1)}, u32[]{:S(2)}) copy-start(bf16[4,128,1792]{2,1,0:T(8,128)(2,1)} %copy-done) | copy-start | bytes 5505028
  67.4 25.6 %copy-start.2 = (bf16[4,128,1792]{2,1,0:T(8,128)(2,1)S(1)}, bf16[4,128,1792]{2,1,0:T(8,128)(2,1)}, u32[]{:S(2)}) copy-start(bf16[4,128,1792]{2,1,0:T(8,128)(2,1)} %copy-done) | copy-start | bytes 5505028
  77.4 21.4 %all-to-all-start.2 = ((bf16[8,128,256]{2,1,0:T(8,128)(2,1)}), bf16[8,128,256]{2,1,0:T(8,128)(2,1)S(1)}, u32[]{:S(2)}, u32[]{:S(2)}) async-start(bf16[8,128,256]{2,1,0:T(8,128)(2,1)} %shard_map.95), calls=%async_computation.2 | async-start | bytes 1048576 | tf_op jit(solution)/shard_map/all_to_all | solution.py:304
  93.8 3.2 %collective-permute-start.3 = (f32[8,28,128]{2,1,0:T(8,128)S(1)}, f32[8,28,128]{2,1,0:T(8,128)S(1)}, u32[]{:S(2)}, u32[]{:S(2)}) collective-permute-start(f32[8,28,128]{2,1,0:T(8,128)S(1)} %get-tuple-element.23), channel_id=1, source_target_pairs={{0,8},{8,0},{16,24},{24,16},{32,40},{40,32},{48,56},{56,48},{64,72... | collective-permute-start | bytes 344072 | tf_op jit(solution)/shard_map/ppermute | solution.py:309
  98.9 14.6 %collective-permute-start.4 = (bf16[128,512]{1,0:T(8,128)(2,1)S(1)}, bf16[128,512]{1,0:T(8,128)(2,1)S(1)}, u32[]{:S(2)}, u32[]{:S(2)}) collective-permute-start(bf16[128,512]{1,0:T(8,128)(2,1)S(1)} %pad_maximum_fusion), channel_id=1, source_target_pairs={{0,0},{1,1},{2,128},{3,129},{4,256},{5,257},{6,384},{7,385},{8,8},... | collective-permute-start | bytes 393224 | tf_op jit(solution)/shard_map/ppermute | solution.py:314
  103.9 14.1 %all-to-all-start.3 = ((f32[8,28,128]{2,1,0:T(8,128)}), f32[8,28,128]{2,1,0:T(8,128)S(1)}, u32[]{:S(2)}, u32[]{:S(2)}) async-start(f32[8,28,128]{2,1,0:T(8,128)} %add.3), calls=%async_computation.3 | async-start | bytes 262144 | tf_op jit(solution)/shard_map/all_to_all | solution.py:318
  113.5 4.5 %copy-start.3 = (bf16[4096,128]{1,0:T(8,128)(2,1)S(1)}, bf16[4096,128]{1,0:T(8,128)(2,1)}, u32[]{:S(2)}) copy-start(bf16[4096,128]{1,0:T(8,128)(2,1)} %basis_ref.1) | copy-start | bytes 3145732
  113.5 4.5 %copy-start.5 = (f32[1,28,128]{2,0,1:T(1,128)S(1)}, f32[1,28,128]{2,0,1:T(1,128)}, u32[]{:S(2)}) copy-start(f32[1,28,128]{2,0,1:T(1,128)} %param.10) | copy-start | bytes 43012
  113.5 4.5 %copy-start.6 = (f32[1,28,128]{2,0,1:T(1,128)S(1)}, f32[1,28,128]{2,0,1:T(1,128)}, u32[]{:S(2)}) copy-start(f32[1,28,128]{2,0,1:T(1,128)} %param.11) | copy-start | bytes 43012

commit v4 on v3

--- a/solution.py
+++ b/solution.py
@@ -46,9 +46,11 @@
 FINISH_FLOPS = int(4e9)
 FIRST_FLOPS = int(1e9)
 SECOND_FLOPS = int(1e9)
+NEAR_FLOPS = int(1e9)
+NEAR_VMEM = 24_000_000
 VMEM_BYTES = 24 * 1024 * 1024
 FIRST_VMEM = 53_000_000
-SECOND_VMEM = 24_000_000
+SECOND_VMEM = 53_000_000
 
 
 def whole(count):
@@ -77,130 +79,171 @@
     )(grads)
 
 
-def products(left, right, x, out_ref, buffer, sems):
-    tokens = out_ref.shape[1]
-    half = right.shape[0] // 2
+FOLD = 4
+
+
+def folded(block):
+    step = block.shape[0] // FOLD
+    return jnp.concatenate([block[k * step : (k + 1) * step] for k in range(FOLD)], axis=1)
+
+
+def unfolded(block):
+    step = block.shape[1] // FOLD
+    return jnp.concatenate([block[:, k * step : (k + 1) * step] for k in range(FOLD)], axis=0)
+
+
+def times(left, rows):
+    return lax.dot_general(
+        left[...], rows, (((1,), (1,)), ((), ())), preferred_element_type=jnp.float32
+    ).astype(jnp.bfloat16)
+
+
+def other_rows(same_other, k):
+    height = same_other.shape[0] // (NY // 2)
+    return jnp.concatenate(
+        [same_other[(2 * h + k) * height : (2 * h + k + 1) * height, :] for h in range(2)], axis=0
+    )
+
+
+def fill(buffer, at, tokens, product):
+    width = product.shape[1] // 2
+    for block in range(NX):
+        for h in range(2):
+            part = product[block * tokens : (block + 1) * tokens, h * width : (h + 1) * width]
+            if at is None:
+                buffer[2 * block + h, tokens:, :] = folded(part)
+            else:
+                buffer[2 * block + h, :tokens, at : at + width] = part
+
+
+def send(buffer, out_ref, x, sems):
     copies = []
-    for h in range(2):
-        product = lax.dot_general(
-            left[...],
-            right[h * half : (h + 1) * half, :],
-            (((1,), (1,)), ((), ())),
-            preferred_element_type=jnp.float32,
-        ).astype(jnp.bfloat16)
-        for block in range(NX):
+    for block in range(NX):
+        for h in range(2):
             k = 2 * block + h
-            buffer[k, :, :half] = product[block * tokens : (block + 1) * tokens]
             piece = 2 * lax.rem(block - x + NX, NX) + h
-            copies.append(
-                pltpu.make_async_copy(buffer.at[k], out_ref.at[piece], sems.at[k])
-            )
+            copies.append(pltpu.make_async_copy(buffer.at[k], out_ref.at[piece], sems.at[k]))
             copies[-1].start()
-    return copies
-
-
-def place(right, height, j, core, mine, other):
-    right[pl.ds(pl.multiple_of((NC * j + core) * height, height), height), :] = mine
-    right[pl.ds(pl.multiple_of((NC * j + 1 - core) * height, height), height), :] = other
-
-
-def first_kernel(
-    left, same, same_other, features, basis, out_ref, near_ref, right, part, buffer,
-    sems, near_sems, sem
-):
-    x, _, core, z = here()
-    height, width = same.shape[1], features.shape[1]
+    for copy in copies:
+        copy.wait()
+
+
+def first_kernel(left, same, same_other, features, basis, out_ref, part, buffer, sems, sem):
+    x, _, _, z = here()
+    tokens, width = features.shape
+    rank = basis.shape[1]
     start = pl.multiple_of(z * width, width)
     copy = pltpu.make_async_copy(basis.at[pl.ds(start, width), :], part, sem)
     copy.start()
-    copies = [
-        pltpu.make_async_copy(
-            rows.at[pl.ds(NY // 4 * core, NY // 4)], near_ref.at[k], near_sems.at[k]
-        )
-        for k, rows in enumerate((same, same_other))
-    ]
-    for near in copies:
-        near.start()
-    for j in range(NY // 2):
-        place(right, height, j, core, same[j], same_other[j])
+    fill(buffer, 0, tokens, times(left, same[...]))
+    fill(buffer, None, tokens, times(left, other_rows(same_other, 0)))
     copy.wait()
     coords = jnp.dot(features[...], part[...], preferred_element_type=jnp.float32).astype(
         jnp.bfloat16
     )
     for k in range(NZ):
-        buffer[k, :, right.shape[0] // 2 :] = coords
-    copies += products(left, right, x, out_ref, buffer, sems)
-    for piece in copies:
-        piece.wait()
-
-
-def second_kernel(left, near, far, out_ref, right, buffer, sems):
+        buffer[k, :tokens, buffer.shape[2] - rank :] = coords
+    send(buffer, out_ref, x, sems)
+
+
+def near_kernel(same, same_other, near_ref):
+    _, _, core, _ = here()
+    for k, rows in enumerate((same, same_other)):
+        for j in range(NY // 4):
+            near_ref[k, j] = rows[NY // 4 * core + j]
+
+
+def rest_kernel(left, same_other, near, far, out_ref, right, buffer, sems):
     x, _, core, _ = here()
     height = near.shape[2]
+    tokens = left.shape[0] // NX
+
+    def place(j, c, rows):
+        at = pl.multiple_of((NC * j + c) * height, height)
+        right[pl.ds(at, height), :] = rows
+
     for j in range(NY // 4):
-        place(right, height, NY // 4 * core + j, core, near[0, j], near[1, j])
-        place(right, height, NY // 4 * (1 - core) + j, 1 - core, far[0, j], far[1, j])
-    for piece in products(left, right, x, out_ref, buffer, sems):
-        piece.wait()
+        for source, half in ((near, core), (far, 1 - core)):
+            place(NY // 4 * half + j, half, source[0, j])
+            place(NY // 4 * half + j, 1 - half, source[1, j])
+    fill(buffer, None, tokens, times(left, other_rows(same_other, 1)))
+    fill(buffer, 0, tokens, times(left, right[...]))
+    send(buffer, out_ref, x, sems)
+
+
+def flat(rows):
+    return rows.reshape(-1, rows.shape[-1])
 
 
 def first_tiles(grads, same, same_other, features, basis):
-    tokens, hidden = grads.shape[1:]
-    count, height = same.shape[:2]
-    width, rank = features.shape[1], basis.shape[1]
-    rows = 2 * count * height
+    tokens, width = features.shape
+    rank = basis.shape[1]
+    same, same_other = flat(same), flat(same_other)
+    shape = (NZ, tokens + tokens // FOLD, same.shape[0] // 2 + rank)
     return pl.pallas_call(
         first_kernel,
-        out_shape=(
-            jax.ShapeDtypeStruct((NZ, tokens, rows // 2 + rank), jnp.bfloat16),
-            jax.ShapeDtypeStruct((2, count // 2, height, hidden), jnp.bfloat16),
-        ),
+        out_shape=jax.ShapeDtypeStruct(shape, jnp.bfloat16),
         in_specs=whole(4) + in_hbm(1),
-        out_specs=tuple(in_hbm(2)),
+        out_specs=in_hbm(1)[0],
         scratch_shapes=[
-            pltpu.VMEM((rows, hidden), jnp.bfloat16),
             pltpu.VMEM((width, rank), jnp.bfloat16),
-            pltpu.VMEM((NZ, tokens, rows // 2 + rank), jnp.bfloat16),
+            pltpu.VMEM(shape, jnp.bfloat16),
             pltpu.SemaphoreType.DMA((NZ,)),
-            pltpu.SemaphoreType.DMA((2,)),
             pltpu.SemaphoreType.DMA,
         ],
         compiler_params=pltpu.CompilerParams(vmem_limit_bytes=FIRST_VMEM),
         cost_estimate=pl.CostEstimate(flops=FIRST_FLOPS, bytes_accessed=0, transcendentals=0),
-    )(grads.reshape(NX * tokens, hidden), same, same_other, features, basis)
-
-
-def second_tiles(grads, near, far):
+    )(flat(grads), same, same_other, features, basis)
+
+
+def neighbour_rows(same, same_other):
+    count, height, hidden = same.shape
+    return pl.pallas_call(
+        near_kernel,
+        out_shape=jax.ShapeDtypeStruct((2, count // 2, height, hidden), jnp.bfloat16),
+        in_specs=whole(2),
+        out_specs=whole(1)[0],
+        compiler_params=pltpu.CompilerParams(vmem_limit_bytes=NEAR_VMEM),
+        cost_estimate=pl.CostEstimate(flops=NEAR_FLOPS, bytes_accessed=0, transcendentals=0),
+    )(same, same_other)
+
+
+def rest_tiles(grads, same_other, near, far):
     tokens, hidden = grads.shape[1:]
+    same_other = flat(same_other)
     rows = (near.size + far.size) // hidden
-    return pl.pallas_call(
-        second_kernel,
-        out_shape=jax.ShapeDtypeStruct((NZ, tokens, rows // 2), jnp.bfloat16),
-        in_specs=whole(3),
+    shape = (NZ, tokens + tokens // FOLD, rows // 2)
+    return pl.pallas_call(
+        rest_kernel,
+        out_shape=jax.ShapeDtypeStruct(shape, jnp.bfloat16),
+        in_specs=whole(4),
         out_specs=in_hbm(1)[0],
         scratch_shapes=[
             pltpu.VMEM((rows, hidden), jnp.bfloat16),
-            pltpu.VMEM((NZ, tokens, rows // 2), jnp.bfloat16),
+            pltpu.VMEM(shape, jnp.bfloat16),
             pltpu.SemaphoreType.DMA((NZ,)),
         ],
         compiler_params=pltpu.CompilerParams(vmem_limit_bytes=SECOND_VMEM),
         cost_estimate=pl.CostEstimate(flops=SECOND_FLOPS, bytes_accessed=0, transcendentals=0),
-    )(grads.reshape(NX * tokens, hidden), near, far)
+    )(flat(grads), same_other, near, far)
 
 
 def sum_kernel(pieces, summed_ref, coords_ref):
     total = jnp.sum(pieces[...].astype(jnp.float32), axis=0)
-    width = summed_ref.shape[1]
-    summed_ref[...] = total[:, :width]
-    coords_ref[...] = total[:, width:].astype(jnp.bfloat16)
+    tokens, rank = coords_ref.shape
+    width = total.shape[1] - rank
+    summed_ref[:, :width] = total[:tokens, :width]
+    summed_ref[:, width:] = unfolded(total[tokens:])
+    coords_ref[...] = total[:tokens, width:].astype(jnp.bfloat16)
 
 
 def sum_first(pieces, rank):
-    tokens, width = pieces.shape[1:]
+    tokens = pieces.shape[1] * FOLD // (FOLD + 1)
+    width = pieces.shape[2]
     return pl.pallas_call(
         sum_kernel,
         out_shape=(
-            jax.ShapeDtypeStruct((tokens, width - rank), jnp.float32),
+            jax.ShapeDtypeStruct((tokens, width - rank + width // FOLD), jnp.float32),
             jax.ShapeDtypeStruct((tokens, rank), jnp.bfloat16),
         ),
         in_specs=whole(1),
@@ -209,25 +252,52 @@
     )(pieces)
 
 
-def finish_kernel(first, second, out_ref):
-    parity = lax.rem(here()[1], 2)
-    width = first.shape[1] // 2
-    for j in range(2):
-        for mine, at in ((first, parity), (second, 1 - parity)):
-            start = pl.multiple_of((2 * j + at) * width, width)
-            out_ref[:, pl.ds(start, width)] = mine[:, j * width : (j + 1) * width]
-
-
-def finish(first, second):
+def join_kernel(first, pieces, out_ref):
+    total = jnp.sum(pieces[...].astype(jnp.float32), axis=0)
     tokens, width = first.shape
+    out_ref[:, :width] = first[...].astype(jnp.bfloat16)
+    rest = unfolded(total[tokens:])
+    out_ref[:, width : width + rest.shape[1]] = rest.astype(jnp.bfloat16)
+    out_ref[:, width + rest.shape[1] :] = total[:tokens].astype(jnp.bfloat16)
+
+
+def join(first, pieces):
+    tokens, width = first.shape
+    columns = width + pieces.shape[2] // FOLD + pieces.shape[2]
+    return pl.pallas_call(
+        join_kernel,
+        out_shape=jax.ShapeDtypeStruct((tokens, columns), jnp.bfloat16),
+        in_specs=whole(2),
+        out_specs=whole(1)[0],
+        compiler_params=pltpu.CompilerParams(vmem_limit_bytes=VMEM_BYTES),
+    )(first, pieces)
+
+
+def finish_kernel(parts, out_ref):
+    _, y, core, _ = here()
+    parity = lax.rem(y, 2)
+    width = out_ref.shape[1] // (NY // 2 * NC)
+    for k in range(2):
+        mine = parts[:, k * width : (k + 1) * width]
+        other = parts[:, (2 + k) * width : (3 + k) * width]
+        for odd in range(2):
+            for c in range(NC):
+                crossed = parts[:, (4 + NC * k + c) * width : (5 + NC * k + c) * width]
+                at = ((2 * k + odd) * NC + c) * width
+                out_ref[:, at : at + width] = jnp.where(
+                    parity == odd, jnp.where(core == c, mine, other), crossed
+                )
+
+
+def finish(parts):
     return pl.pallas_call(
         finish_kernel,
-        out_shape=jax.ShapeDtypeStruct((tokens, 2 * width), jnp.bfloat16),
-        in_specs=whole(2),
+        out_shape=jax.ShapeDtypeStruct(parts.shape, jnp.bfloat16),
+        in_specs=whole(1),
         out_specs=pl.BlockSpec(memory_space=pltpu.VMEM),
         compiler_params=pltpu.CompilerParams(vmem_limit_bytes=VMEM_BYTES),
         cost_estimate=pl.CostEstimate(flops=FINISH_FLOPS, bytes_accessed=0, transcendentals=0),
-    )(first, second)
+    )(parts)
 
 
 def proj_kernel(grads, coords, mine_ref, other_ref, proj):
@@ -294,12 +364,13 @@
     same = lax.all_gather(weight, "dp", axis=0, axis_index_groups=SAME_PARITY)
 
     same_other = lax.ppermute(same, "dp", OTHER_CORE)
-    first, near = first_tiles(grads, same, same_other, features, basis)
+    first = first_tiles(grads, same, same_other, features, basis)
+    first, same, same_other = lax.optimization_barrier((first, same, same_other))
     first = lax.all_to_all(first, "tensor", 0, 0)
 
-    near = lax.ppermute(near, "dp", TO_NEIGHBOUR)
+    near = lax.ppermute(neighbour_rows(same, same_other), "dp", TO_NEIGHBOUR)
     far = lax.ppermute(near, "dp", OTHER_CORE)
-    second = second_tiles(grads, near, far)
+    second = rest_tiles(grads, same_other, near, far)
     first, second = lax.optimization_barrier((first, second))
     second = lax.all_to_all(second, "tensor", 0, 0)
     first, coords = sum_first(first, basis.shape[1])
@@ -309,11 +380,8 @@
     parts = parts + lax.ppermute(other, "dp", OTHER_CORE)
     parts, second = lax.optimization_barrier((parts, second))
 
-    summed = jnp.sum(second.astype(jnp.float32), axis=0)
-    summed = jnp.concatenate([first, summed], axis=1).astype(jnp.bfloat16)
-    summed = lax.ppermute(summed, ("dp", "tensor"), HOME)
-    half = summed.shape[1] // 2
-    feature_grad = finish(summed[:, :half], summed[:, half:])
+    summed = lax.ppermute(join(first, second), ("dp", "tensor"), HOME)
+    feature_grad = finish(summed)
 
     parts = lax.all_to_all(parts, "dp", 0, 0, axis_index_groups=ALONG_Y)
     results = adam(parts, basis, *(jnp.swapaxes(m, 0, 1) for m in (moment_one, moment_two)))

time: 120 us -> 118 us (0.983)
  starting transfers between devices: 40 us -> 37.6 us
  Pallas kernels: 12 us -> 14 us
  waiting for transfers between devices: 31.2 us -> 29.3 us
    all_to_all x1, waiting for transfers between devices: 9.97 us -> 6.88 us  [body(): first = lax.all_to_all(first, 'tensor', 0, 0)]
    all_to_all x1, waiting for transfers between devices: 3.76 us -> 0.9 us  [body(): parts = lax.all_to_all(parts, 'dp', 0, 0, axis_index_groups=ALONG_Y)]
    all_to_all x1, waiting for transfers between devices: 1.13 us -> 3.87 us  [body(): second = lax.all_to_all(second, 'tensor', 0, 0)]
    ppermute x2, starting transfers between devices: 6.93 us -> 4.29 us  [the longest x1 2.37 us: body(): summed = lax.ppermute(join(first, second), ('dp', 'tensor'), HOME)]
    ppermute x2, waiting for transfers between devices: 10 us -> 12.4 us  [the longest x1 7.23 us: body(): summed = lax.ppermute(join(first, second), ('dp', 'tensor'), HOME)]
    pallas_call x3 -> x5, Pallas kernels: 7.6 us -> 9.5 us  [the longest x1 4.25 us: first_tiles(): pl.pallas_call(first_kernel, out_shape=jax.ShapeDtypeStruct(shape, jnp.bf...]
    unnamed x16 -> x18, local copies, waits for them, and re-layouts: 2.81 us -> 3.42 us
  transfers between devices with their start and end apart: 9 -> 9, of which waited for: 8 -> 8; matrix products, arithmetic and copies ran while one was open for 1% -> 1% of each run, Pallas kernels for 3% -> 5%
where the time goes in v4:
time: 118 us; the launch traced here: 117 us
  starting transfers between devices  37.6 us (32%)
  blocking collectives  31.6 us (27%)
  waiting for transfers between devices  29.3 us (25%)
  Pallas kernels  14 us (12%)
  local copies, waits for them, and re-layouts  3.42 us (3%)
    all_gather x1, blocking collectives, body(): same = lax.all_gather(weight, 'dp', axis=0, axis_index_groups=SAME_PARITY)  19.7 us
    all_gather x1, blocking collectives, body(): lax.all_gather(coords, 'dp', axis=0, tiled=True, axis_index_groups=ALONG_X)  12 us
    all_to_all x1, starting transfers between devices, body(): lax.all_to_all(spread(out_grad), 'dp', 0, 0, axis_index_groups=ALONG_X)  9.55 us
    all_to_all x1, starting transfers between devices, body(): first = lax.all_to_all(first, 'tensor', 0, 0)  9.41 us
    ppermute x1, waiting for transfers between devices, body(): summed = lax.ppermute(join(first, second), ('dp', 'tensor'), HOME)  7.23 us
    all_to_all x1, waiting for transfers between devices, body(): first = lax.all_to_all(first, 'tensor', 0, 0)  6.88 us
    ppermute x1, waiting for transfers between devices, body(): near = lax.ppermute(neighbour_rows(same, same_other), 'dp', TO_NEIGHBOUR)  5.16 us
    all_to_all x1, starting transfers between devices, body(): parts = lax.all_to_all(parts, 'dp', 0, 0, axis_index_groups=ALONG_Y)  5.08 us
  transfers between devices with their start and end apart: 9, of which 8 were waited for; matrix products, arithmetic and copies ran while one was open for 1% of the time, Pallas kernels for 5%

profile of v4, /device:TPU:6, one launch (start us, length us, event | category | flops | bytes accessed | tf_op | source)
XLA Modules:
  0.0 117.4 jit_solution(13204385799166767686)
XLA Ops:
  0.6 2.3 %shard_map.93 = bf16[4,128,1792]{2,1,0:T(8,128)(2,1)} custom-call(bf16[128,1792]{1,0:T(8,128)(2,1)} %grads.1), custom_call_target="tpu_custom_call" | custom-call | tf_op jit(solution)/shard_map/pallas_call | solution.py:73
  3.0 0.0 copy-start.8
  3.0 0.0 copy-start.5
  3.0 9.6 %all-to-all-start = ((bf16[4,128,1792]{2,1,0:T(8,128)(2,1)}), bf16[4,128,1792]{2,1,0:T(8,128)(2,1)S(1)}, u32[]{:S(2)}, u32[]{:S(2)}) async-start(bf16[4,128,1792]{2,1,0:T(8,128)(2,1)} %shard_map.93), calls=%async_computation | async-start | bytes 3670016 | tf_op jit(solution)/shard_map/all_to_all | solution.py:363
  12.5 0.0 copy-done.8
  12.5 19.7 %all-gather.same = bf16[256,1792]{1,0:T(8,128)(2,1)S(1)} all-gather(bf16[64,1792]{1,0:T(8,128)(2,1)S(1)} %copy-done.8), channel_id=2, replica_groups={{0,32,64,96},{8,40,72,104},{16,48,80,112},{24,56,88,120},{128,160,192,2..., dimensions={0}, use_global_device_ids=true | all-gather | bytes 1146880 | tf_op jit(solution)/shard_map/all_gather | solution.py:364
  32.2 1.9 %collective-permute-start = (bf16[4,64,1792]{2,1,0:T(8,128)(2,1)S(1)}, bf16[4,64,1792]{2,1,0:T(8,128)(2,1)S(1)}, u32[]{:S(2)}, u32[]{:S(2)}) collective-permute-start(bf16[4,64,1792]{2,1,0:T(8,128)(2,1)S(1)} %bitcast.14), channel_id=1, source_target_pairs={{0,8},{8,0},{16,24},{24,16},{32,40},{40,32},{48,56},{56,48},{64,72... | collective-permute-start | bytes 2752520 | tf_op jit(solution)/shard_map/ppermute | solution.py:366
  34.1 0.0 copy-start.3
  34.1 0.9 copy-done.3
  35.1 1.5 %collective-permute-done.same_other = bf16[4,64,1792]{2,1,0:T(8,128)(2,1)S(1)} collective-permute-done((bf16[4,64,1792]{2,1,0:T(8,128)(2,1)S(1)}, bf16[4,64,1792]{2,1,0:T(8,128)(2,1)S(1)}, u32[]{:S(2)}, u32[]{:S(2)}) %collective-permute-start) | collective-permute-done | bytes 917536 | tf_op jit(solution)/shard_map/ppermute | solution.py:366
  36.5 0.0 all-to-all-done
  36.6 0.0 copy-start
  36.6 1.3 %copy-done = bf16[4,128,1792]{2,1,0:T(8,128)(2,1)} copy-done((bf16[4,128,1792]{2,1,0:T(8,128)(2,1)}, bf16[4,128,1792]{2,1,0:T(8,128)(2,1)S(1)}, u32[]{:S(2)}) %copy-start) | copy-done | bytes 1835032
  37.8 0.0 copy-done.5
  37.8 0.0 copy-start.4
  37.8 1.2 %copy-done.4 = bf16[256,1792]{1,0:T(8,128)(2,1)S(1)} copy-done((bf16[256,1792]{1,0:T(8,128)(2,1)S(1)}, bf16[256,1792]{1,0:T(8,128)(2,1)}, u32[]{:S(2)}) %copy-start.4) | copy-done | bytes 917528
  39.0 4.3 %shard_map.94 = bf16[8,160,256]{2,1,0:T(8,128)(2,1)} custom-call(bf16[512,1792]{1,0:T(8,128)(2,1)} %bitcast.9, bf16[256,1792]{1,0:T(8,128)(2,1)S(1)} %copy-done.4, bf16[256,1792]{1,0:T(8,128)(2,1)S(1)} %bitcast.12, bf16[128,512]{1,0:T(8,128)(2,1)S(1)} %copy-done.5, bf16[4096,128]{1,0:T(8,128)(2,1)} %basis_ref.1), custom_call_target="tpu_custom_call" | custom-call | flops 1000000000 | tf_op jit(solution)/shard_map/pallas_call | solution.py:183
  43.3 0.1 shard_map.95
  43.3 1.9 %collective-permute-start.1 = (bf16[2,2,64,1792]{3,2,1,0:T(8,128)(2,1)S(1)}, bf16[2,2,64,1792]{3,2,1,0:T(8,128)(2,1)S(1)}, u32[]{:S(2)}, u32[]{:S(2)}) collective-permute-start(bf16[2,2,64,1792]{3,2,1,0:T(8,128)(2,1)S(1)} %shard_map.95), channel_id=1, source_target_pairs={{0,16},{8,120},{16,32},{24,8},{32,48},{40,24},{48,64},{56,40},{64,... | collective-permute-start | bytes 2752520 | tf_op jit(solution)/shard_map/ppermute | solution.py:371
  45.3 9.4 %all-to-all-start.1 = ((bf16[8,160,256]{2,1,0:T(8,128)(2,1)}), bf16[8,160,256]{2,1,0:T(8,128)(2,1)S(1)}, u32[]{:S(2)}, u32[]{:S(2)}) async-start(bf16[8,160,256]{2,1,0:T(8,128)(2,1)} %shard_map.94), calls=%async_computation.1 | async-start | bytes 1310720 | tf_op jit(solution)/shard_map/all_to_all | solution.py:369
  54.7 5.2 %collective-permute-done.1.near = bf16[2,2,64,1792]{3,2,1,0:T(8,128)(2,1)S(1)} collective-permute-done((bf16[2,2,64,1792]{3,2,1,0:T(8,128)(2,1)S(1)}, bf16[2,2,64,1792]{3,2,1,0:T(8,128)(2,1)S(1)}, u32[]{:S(2)}, u32[]{:S(2)}) %collective-permute-start.1) | collective-permute-done | bytes 917536 | tf_op jit(solution)/shard_map/ppermute | solution.py:371
  59.8 1.9 %collective-permute-start.2 = (bf16[2,2,64,1792]{3,2,1,0:T(8,128)(2,1)S(1)}, bf16[2,2,64,1792]{3,2,1,0:T(8,128)(2,1)S(1)}, u32[]{:S(2)}, u32[]{:S(2)}) collective-permute-start(bf16[2,2,64,1792]{3,2,1,0:T(8,128)(2,1)S(1)} %collective-permute-done.1.near), channel_id=1, source_target_pairs={{0,8},{8,0},{16,24},{24,16},{32,40},{40,32},{48,56},{56,48},{64,72... | collective-permute-start | bytes 2752520 | tf_op jit(solution)/shard_map/ppermute | solution.py:372
  61.8 2.4 %collective-permute-done.2.far = bf16[2,2,64,1792]{3,2,1,0:T(8,128)(2,1)S(1)} collective-permute-done((bf16[2,2,64,1792]{3,2,1,0:T(8,128)(2,1)S(1)}, bf16[2,2,64,1792]{3,2,1,0:T(8,128)(2,1)S(1)}, u32[]{:S(2)}, u32[]{:S(2)}) %collective-permute-start.2) | collective-permute-done | bytes 917536 | tf_op jit(solution)/shard_map/ppermute | solution.py:372
  64.2 4.1 %shard_map.96 = bf16[8,160,256]{2,1,0:T(8,128)(2,1)} custom-call(bf16[512,1792]{1,0:T(8,128)(2,1)} %bitcast.10, bf16[256,1792]{1,0:T(8,128)(2,1)S(1)} %bitcast.13, bf16[2,2,64,1792]{3,2,1,0:T(8,128)(2,1)S(1)} %collective-permute-done.1.near, bf16[2,2,64,1792]{3,2,1,0:T(8,128)(2,1)S(1)} %collective-permute-done.2.far), custom_call_target="tpu_custom_call" | custom-call | flops 1000000000 | tf_op jit(solution)/shard_map/pallas_call | solution.py:216
  68.3 0.0 copy-start.1
  68.3 6.9 %all-to-all-done.1.pieces = bf16[8,160,256]{2,1,0:T(8,128)(2,1)S(1)} async-done(((bf16[8,160,256]{2,1,0:T(8,128)(2,1)}), bf16[8,160,256]{2,1,0:T(8,128)(2,1)S(1)}, u32[]{:S(2)}, u32[]{:S(2)}) %all-to-all-start.1) | async-done | bytes 655392 | tf_op jit(solution)/shard_map/all_to_all | solution.py:369
  75.2 3.5 %all-to-all-start.2 = ((bf16[8,160,256]{2,1,0:T(8,128)(2,1)}), bf16[8,160,256]{2,1,0:T(8,128)(2,1)S(1)}, u32[]{:S(2)}, u32[]{:S(2)}) async-start(bf16[8,160,256]{2,1,0:T(8,128)(2,1)} %shard_map.96), calls=%async_computation.2 | async-start | bytes 1310720 | tf_op jit(solution)/shard_map/all_to_all | solution.py:375
  78.7 0.2 shard_map.97
  78.9 12.0 %all_gather.11.coords = bf16[512,128]{1,0:T(8,128)(2,1)S(1)} all-gather(bf16[128,128]{1,0:T(8,128)(2,1)S(1)} %get-tuple-element.23), channel_id=1, replica_groups={{0,128,256,384},{8,136,264,392},{16,144,272,400},{24,152,280,408},{32,1..., dimensions={0}, use_global_device_ids=true | all-gather | bytes 163840 | tf_op jit(solution)/shard_map/all_gather | solution.py:378
  90.9 0.0 copy-done.1
  90.9 0.7 shard_map.98
  91.6 1.9 %collective-permute-start.3 = (f32[8,28,128]{2,1,0:T(8,128)S(1)}, f32[8,28,128]{2,1,0:T(8,128)S(1)}, u32[]{:S(2)}, u32[]{:S(2)}) collective-permute-start(f32[8,28,128]{2,1,0:T(8,128)S(1)} %get-tuple-element.25), channel_id=1, source_target_pairs={{0,8},{8,0},{16,24},{24,16},{32,40},{40,32},{48,56},{56,48},{64,72... | collective-permute-start | bytes 344072 | tf_op jit(solution)/shard_map/ppermute | solution.py:380
  93.5 1.3 %collective-permute-done.3 = f32[8,28,128]{2,1,0:T(8,128)S(1)} collective-permute-done((f32[8,28,128]{2,1,0:T(8,128)S(1)}, f32[8,28,128]{2,1,0:T(8,128)S(1)}, u32[]{:S(2)}, u32[]{:S(2)}) %collective-permute-start.3) | collective-permute-done | bytes 114720 | tf_op jit(solution)/shard_map/ppermute | solution.py:380
  94.9 0.7 add.3
  95.5 3.9 %all-to-all-done.2.pieces = bf16[8,160,256]{2,1,0:T(8,128)(2,1)S(1)} async-done(((bf16[8,160,256]{2,1,0:T(8,128)(2,1)}), bf16[8,160,256]{2,1,0:T(8,128)(2,1)S(1)}, u32[]{:S(2)}, u32[]{:S(2)}) %all-to-all-start.2) | async-done | bytes 655392 | tf_op jit(solution)/shard_map/all_to_all | solution.py:375
  99.4 0.2 shard_map.99
  99.6 2.4 %collective-permute-start.4 = (bf16[128,512]{1,0:T(8,128)(2,1)S(1)}, bf16[128,512]{1,0:T(8,128)(2,1)S(1)}, u32[]{:S(2)}, u32[]{:S(2)}) collective-permute-start(bf16[128,512]{1,0:T(8,128)(2,1)S(1)} %shard_map.99), channel_id=1, source_target_pairs={{0,0},{1,1},{2,128},{3,129},{4,256},{5,257},{6,384},{7,385},{8,8},... | collective-permute-start | bytes 393224 | tf_op jit(solution)/shard_map/ppermute | solution.py:383
  102.0 5.1 %all-to-all-start.3 = ((f32[8,28,128]{2,1,0:T(8,128)}), f32[8,28,128]{2,1,0:T(8,128)S(1)}, u32[]{:S(2)}, u32[]{:S(2)}) async-start(f32[8,28,128]{2,1,0:T(8,128)} %add.3), calls=%async_computation.3 | async-start | bytes 262144 | tf_op jit(solution)/shard_map/all_to_all | solution.py:386
  107.0 0.0 copy-start.2
  107.0 0.0 copy-start.6
  107.1 0.0 copy-start.7
  107.1 7.2 %collective-permute-done.4.parts = bf16[128,512]{1,0:T(8,128)(2,1)S(1)} collective-permute-done((bf16[128,512]{1,0:T(8,128)(2,1)S(1)}, bf16[128,512]{1,0:T(8,128)(2,1)S(1)}, u32[]{:S(2)}, u32[]{:S(2)}) %collective-permute-start.4) | collective-permute-done | bytes 131104 | tf_op jit(solution)/shard_map/ppermute | solution.py:383
  114.3 0.9 shard_map.100
  115.2 0.9 all-to-all-done.3.parts_ref
  116.1 0.0 copy-done.2
  116.1 0.0 copy-done.6
  116.1 0.0 copy-done.7
  116.1 1.3 %shard_map.101 = (f32[28,1,128]{2,1,0:T(1,128)}, f32[28,1,128]{2,1,0:T(1,128)}, f32[28,1,4096]{2,1,0:T(1,128)}) custom-call(f32[8,28,128]{2,1,0:T(8,128)S(1)} %all-to-all-done.3.parts_ref, bf16[4096,128]{1,0:T(8,128)(2,1)S(1)} %copy-done.2, f32[28,1,128]{2,1,0:T(1,128)S(1)} %bitcast.16, f32[28,1,128]{2,1,0:T(1,128)S(1)} %bitcast.17), custom_call_target="tpu_custom_call" | custom-call | tf_op jit(solution)/shard_map/pallas_call | solution.py:349
Async XLA Ops:
  3.0 9.6 %copy-start.8 = (bf16[64,1792]{1,0:T(8,128)(2,1)S(1)}, bf16[64,1792]{1,0:T(8,128)(2,1)}, u32[]{:S(2)}) copy-start(bf16[64,1792]{1,0:T(8,128)(2,1)} %param.8) | copy-start | bytes 688132
  3.0 34.9 %copy-start.5 = (bf16[128,512]{1,0:T(8,128)(2,1)S(1)}, bf16[128,512]{1,0:T(8,128)(2,1)}, u32[]{:S(2)}) copy-start(bf16[128,512]{1,0:T(8,128)(2,1)} %features.1) | copy-start | bytes 393220
  3.0 33.6 %all-to-all-start = ((bf16[4,128,1792]{2,1,0:T(8,128)(2,1)}), bf16[4,128,1792]{2,1,0:T(8,128)(2,1)S(1)}, u32[]{:S(2)}, u32[]{:S(2)}) async-start(bf16[4,128,1792]{2,1,0:T(8,128)(2,1)} %shard_map.93), calls=%async_computation | async-start | bytes 3670016 | tf_op jit(solution)/shard_map/all_to_all | solution.py:363
  32.2 4.4 %collective-permute-start = (bf16[4,64,1792]{2,1,0:T(8,128)(2,1)S(1)}, bf16[4,64,1792]{2,1,0:T(8,128)(2,1)S(1)}, u32[]{:S(2)}, u32[]{:S(2)}) collective-permute-start(bf16[4,64,1792]{2,1,0:T(8,128)(2,1)S(1)} %bitcast.14), channel_id=1, source_target_pairs={{0,8},{8,0},{16,24},{24,16},{32,40},{40,32},{48,56},{56,48},{64,72... | collective-permute-start | bytes 2752520 | tf_op jit(solution)/shard_map/ppermute | solution.py:366
  34.1 0.9 copy-start.3
  36.6 1.3 %copy-start = (bf16[4,128,1792]{2,1,0:T(8,128)(2,1)}, bf16[4,128,1792]{2,1,0:T(8,128)(2,1)S(1)}, u32[]{:S(2)}) copy-start(bf16[4,128,1792]{2,1,0:T(8,128)(2,1)S(1)} %all-to-all-done) | copy-start | bytes 5505028
  37.8 1.2 %copy-start.4 = (bf16[256,1792]{1,0:T(8,128)(2,1)S(1)}, bf16[256,1792]{1,0:T(8,128)(2,1)}, u32[]{:S(2)}) copy-start(bf16[256,1792]{1,0:T(8,128)(2,1)} %copy-done.3) | copy-start | bytes 2752516
  43.3 16.5 %collective-permute-start.1 = (bf16[2,2,64,1792]{3,2,1,0:T(8,128)(2,1)S(1)}, bf16[2,2,64,1792]{3,2,1,0:T(8,128)(2,1)S(1)}, u32[]{:S(2)}, u32[]{:S(2)}) collective-permute-start(bf16[2,2,64,1792]{3,2,1,0:T(8,128)(2,1)S(1)} %shard_map.95), channel_id=1, source_target_pairs={{0,16},{8,120},{16,32},{24,8},{32,48},{40,24},{48,64},{56,40},{64,... | collective-permute-start | bytes 2752520 | tf_op jit(solution)/shard_map/ppermute | solution.py:371
  45.3 29.9 %all-to-all-start.1 = ((bf16[8,160,256]{2,1,0:T(8,128)(2,1)}), bf16[8,160,256]{2,1,0:T(8,128)(2,1)S(1)}, u32[]{:S(2)}, u32[]{:S(2)}) async-start(bf16[8,160,256]{2,1,0:T(8,128)(2,1)} %shard_map.94), calls=%async_computation.1 | async-start | bytes 1310720 | tf_op jit(solution)/shard_map/all_to_all | solution.py:369
  59.8 4.4 %collective-permute-start.2 = (bf16[2,2,64,1792]{3,2,1,0:T(8,128)(2,1)S(1)}, bf16[2,2,64,1792]{3,2,1,0:T(8,128)(2,1)S(1)}, u32[]{:S(2)}, u32[]{:S(2)}) collective-permute-start(bf16[2,2,64,1792]{3,2,1,0:T(8,128)(2,1)S(1)} %collective-permute-done.1.near), channel_id=1, source_target_pairs={{0,8},{8,0},{16,24},{24,16},{32,40},{40,32},{48,56},{56,48},{64,72... | collective-permute-start | bytes 2752520 | tf_op jit(solution)/shard_map/ppermute | solution.py:372
  68.3 22.6 %copy-start.1 = (bf16[4,128,1792]{2,1,0:T(8,128)(2,1)S(1)}, bf16[4,128,1792]{2,1,0:T(8,128)(2,1)}, u32[]{:S(2)}) copy-start(bf16[4,128,1792]{2,1,0:T(8,128)(2,1)} %copy-done) | copy-start | bytes 5505028
  75.2 24.2 %all-to-all-start.2 = ((bf16[8,160,256]{2,1,0:T(8,128)(2,1)}), bf16[8,160,256]{2,1,0:T(8,128)(2,1)S(1)}, u32[]{:S(2)}, u32[]{:S(2)}) async-start(bf16[8,160,256]{2,1,0:T(8,128)(2,1)} %shard_map.96), calls=%async_computation.2 | async-start | bytes 1310720 | tf_op jit(solution)/shard_map/all_to_all | solution.py:375
  91.6 3.2 %collective-permute-start.3 = (f32[8,28,128]{2,1,0:T(8,128)S(1)}, f32[8,28,128]{2,1,0:T(8,128)S(1)}, u32[]{:S(2)}, u32[]{:S(2)}) collective-permute-start(f32[8,28,128]{2,1,0:T(8,128)S(1)} %get-tuple-element.25), channel_id=1, source_target_pairs={{0,8},{8,0},{16,24},{24,16},{32,40},{40,32},{48,56},{56,48},{64,72... | collective-permute-start | bytes 344072 | tf_op jit(solution)/shard_map/ppermute | solution.py:380
  99.6 14.7 %collective-permute-start.4 = (bf16[128,512]{1,0:T(8,128)(2,1)S(1)}, bf16[128,512]{1,0:T(8,128)(2,1)S(1)}, u32[]{:S(2)}, u32[]{:S(2)}) collective-permute-start(bf16[128,512]{1,0:T(8,128)(2,1)S(1)} %shard_map.99), channel_id=1, source_target_pairs={{0,0},{1,1},{2,128},{3,129},{4,256},{5,257},{6,384},{7,385},{8,8},... | collective-permute-start | bytes 393224 | tf_op jit(solution)/shard_map/ppermute | solution.py:383
  102.0 14.2 %all-to-all-start.3 = ((f32[8,28,128]{2,1,0:T(8,128)}), f32[8,28,128]{2,1,0:T(8,128)S(1)}, u32[]{:S(2)}, u32[]{:S(2)}) async-start(f32[8,28,128]{2,1,0:T(8,128)} %add.3), calls=%async_computation.3 | async-start | bytes 262144 | tf_op jit(solution)/shard_map/all_to_all | solution.py:386
  107.0 9.1 %copy-start.2 = (bf16[4096,128]{1,0:T(8,128)(2,1)S(1)}, bf16[4096,128]{1,0:T(8,128)(2,1)}, u32[]{:S(2)}) copy-start(bf16[4096,128]{1,0:T(8,128)(2,1)} %basis_ref.1) | copy-start | bytes 3145732
  107.0 9.1 %copy-start.6 = (f32[1,28,128]{2,0,1:T(1,128)S(1)}, f32[1,28,128]{2,0,1:T(1,128)}, u32[]{:S(2)}) copy-start(f32[1,28,128]{2,0,1:T(1,128)} %param.10) | copy-start | bytes 43012
  107.1 9.1 %copy-start.7 = (f32[1,28,128]{2,0,1:T(1,128)S(1)}, f32[1,28,128]{2,0,1:T(1,128)}, u32[]{:S(2)}) copy-start(f32[1,28,128]{2,0,1:T(1,128)} %param.11) | copy-start | bytes 43012

commit v5 on v4

--- a/solution.py
+++ b/solution.py
@@ -26,7 +26,8 @@
 
 CHIPS = [(x, y, c) for x in range(NX) for y in range(NY) for c in range(NC)]
 ALONG_X = [[dp_of(x, y, c) for x in range(NX)] for y in range(NY) for c in range(NC)]
-ALONG_Y = [[dp_of(x, y, c) for y in range(NY)] for x in range(NX) for c in range(NC)]
+Y_ORDER = [0, 4, 1, 5, 2, 6, 3, 7]
+ALONG_Y = [[dp_of(x, y, c) for y in Y_ORDER] for x in range(NX) for c in range(NC)]
 SAME_PARITY = [
     [dp_of(x, p + 2 * j, c) for j in range(NY // 2)]
     for x in range(NX)
@@ -48,6 +49,9 @@
 SECOND_FLOPS = int(1e9)
 NEAR_FLOPS = int(1e9)
 NEAR_VMEM = 24_000_000
+Z_ORDER = [0, 4, 1, 5, 2, 6, 3, 7]
+ALONG_Z = [Z_ORDER]
+
 VMEM_BYTES = 24 * 1024 * 1024
 FIRST_VMEM = 53_000_000
 SECOND_VMEM = 53_000_000
@@ -116,12 +120,19 @@
                 buffer[2 * block + h, :tokens, at : at + width] = part
 
 
+def slot_of(q, h):
+    slot = Z_ORDER.index(h)
+    for k in range(1, NX):
+        slot = jnp.where(q == k, Z_ORDER.index(2 * k + h), slot)
+    return slot
+
+
 def send(buffer, out_ref, x, sems):
     copies = []
     for block in range(NX):
         for h in range(2):
             k = 2 * block + h
-            piece = 2 * lax.rem(block - x + NX, NX) + h
+            piece = slot_of(lax.rem(block - x + NX, NX), h)
             copies.append(pltpu.make_async_copy(buffer.at[k], out_ref.at[piece], sems.at[k]))
             copies[-1].start()
     for copy in copies:
@@ -312,8 +323,8 @@
     for k in range(parts):
         at = NC * k * share
         zero, one = own[at : at + share], own[at + share : at + NC * share]
-        mine_ref[k] = jnp.where(first_core, zero, one)
-        other_ref[k] = jnp.where(first_core, one, zero)
+        mine_ref[Y_ORDER.index(k)] = jnp.where(first_core, zero, one)
+        other_ref[Y_ORDER.index(k)] = jnp.where(first_core, one, zero)
 
 
 def project(grads, coords):
@@ -366,13 +377,13 @@
     same_other = lax.ppermute(same, "dp", OTHER_CORE)
     first = first_tiles(grads, same, same_other, features, basis)
     first, same, same_other = lax.optimization_barrier((first, same, same_other))
-    first = lax.all_to_all(first, "tensor", 0, 0)
+    first = lax.all_to_all(first, "tensor", 0, 0, axis_index_groups=ALONG_Z)
 
     near = lax.ppermute(neighbour_rows(same, same_other), "dp", TO_NEIGHBOUR)
     far = lax.ppermute(near, "dp", OTHER_CORE)
     second = rest_tiles(grads, same_other, near, far)
     first, second = lax.optimization_barrier((first, second))
-    second = lax.all_to_all(second, "tensor", 0, 0)
+    second = lax.all_to_all(second, "tensor", 0, 0, axis_index_groups=ALONG_Z)
     first, coords = sum_first(first, basis.shape[1])
 
     coords = lax.all_gather(coords, "dp", axis=0, tiled=True, axis_index_groups=ALONG_X)

time: 118 us -> 116 us (0.983)
  waiting for transfers between devices: 29.3 us -> 20.6 us
  starting transfers between devices: 37.6 us -> 43.7 us
    all_to_all x2, waiting for transfers between devices: 10.8 us -> 3.15 us  [the longest x1 3.15 us: body(): first = lax.all_to_all(first, 'tensor', 0, 0, axis_index_groups=ALONG_Z)]
    ppermute x1, starting transfers between devices: 2.37 us -> 6.04 us  [body(): summed = lax.ppermute(join(first, second), ('dp', 'tensor'), HOME)]
    ppermute x1, waiting for transfers between devices: 7.23 us -> 3.87 us  [body(): summed = lax.ppermute(join(first, second), ('dp', 'tensor'), HOME)]
    all_to_all x2, starting transfers between devices: 13 us -> 15.7 us  [the longest x1 9.41 us: body(): first = lax.all_to_all(first, 'tensor', 0, 0, axis_index_groups=ALONG_Z)]
    all_to_all x1, waiting for transfers between devices: 0.9 us -> 3.15 us  [body(): parts = lax.all_to_all(parts, 'dp', 0, 0, axis_index_groups=ALONG_Y)]
  transfers between devices with their start and end apart: 9 -> 9, of which waited for: 8 -> 7; matrix products, arithmetic and copies ran while one was open for 1% -> 1% of each run, Pallas kernels for 5% -> 5%
where the time goes in v5:
time: 116 us; the launch traced here: 115 us
  starting transfers between devices  43.7 us (38%)
  blocking collectives  31.6 us (27%)
  waiting for transfers between devices  20.6 us (18%)
  Pallas kernels  14 us (12%)
  local copies, waits for them, and re-layouts  3.42 us (3%)
    all_gather x1, blocking collectives, body(): same = lax.all_gather(weight, 'dp', axis=0, axis_index_groups=SAME_PARITY)  19.7 us
    all_gather x1, blocking collectives, body(): lax.all_gather(coords, 'dp', axis=0, tiled=True, axis_index_groups=ALONG_X)  12 us
    all_to_all x1, starting transfers between devices, body(): lax.all_to_all(spread(out_grad), 'dp', 0, 0, axis_index_groups=ALONG_X)  9.55 us
    all_to_all x1, starting transfers between devices, body(): first = lax.all_to_all(first, 'tensor', 0, 0, axis_index_groups=ALONG_Z)  9.41 us
    all_to_all x1, starting transfers between devices, body(): second = lax.all_to_all(second, 'tensor', 0, 0, axis_index_groups=ALONG_Z)  6.29 us
    ppermute x1, starting transfers between devices, body(): summed = lax.ppermute(join(first, second), ('dp', 'tensor'), HOME)  6.04 us
    ppermute x1, waiting for transfers between devices, body(): near = lax.ppermute(neighbour_rows(same, same_other), 'dp', TO_NEIGHBOUR)  5.16 us
    all_to_all x1, starting transfers between devices, body(): parts = lax.all_to_all(parts, 'dp', 0, 0, axis_index_groups=ALONG_Y)  4.77 us
  transfers between devices with their start and end apart: 9, of which 7 were waited for; matrix products, arithmetic and copies ran while one was open for 1% of the time, Pallas kernels for 5%

profile of v5, /device:TPU:6, one launch (start us, length us, event | category | flops | bytes accessed | tf_op | source)
XLA Modules:
  0.0 114.8 jit_solution(4275677812512865640)
XLA Ops:
  0.6 2.3 %shard_map.93 = bf16[4,128,1792]{2,1,0:T(8,128)(2,1)} custom-call(bf16[128,1792]{1,0:T(8,128)(2,1)} %grads.1), custom_call_target="tpu_custom_call" | custom-call | tf_op jit(solution)/shard_map/pallas_call | solution.py:77
  3.0 0.0 copy-start.8
  3.0 0.0 copy-start.5
  3.0 9.6 %all-to-all-start = ((bf16[4,128,1792]{2,1,0:T(8,128)(2,1)}), bf16[4,128,1792]{2,1,0:T(8,128)(2,1)S(1)}, u32[]{:S(2)}, u32[]{:S(2)}) async-start(bf16[4,128,1792]{2,1,0:T(8,128)(2,1)} %shard_map.93), calls=%async_computation | async-start | bytes 3670016 | tf_op jit(solution)/shard_map/all_to_all | solution.py:374
  12.5 0.0 copy-done.8
  12.5 19.7 %all-gather.same = bf16[256,1792]{1,0:T(8,128)(2,1)S(1)} all-gather(bf16[64,1792]{1,0:T(8,128)(2,1)S(1)} %copy-done.8), channel_id=2, replica_groups={{0,32,64,96},{8,40,72,104},{16,48,80,112},{24,56,88,120},{128,160,192,2..., dimensions={0}, use_global_device_ids=true | all-gather | bytes 1146880 | tf_op jit(solution)/shard_map/all_gather | solution.py:375
  32.2 1.9 %collective-permute-start = (bf16[4,64,1792]{2,1,0:T(8,128)(2,1)S(1)}, bf16[4,64,1792]{2,1,0:T(8,128)(2,1)S(1)}, u32[]{:S(2)}, u32[]{:S(2)}) collective-permute-start(bf16[4,64,1792]{2,1,0:T(8,128)(2,1)S(1)} %bitcast.14), channel_id=1, source_target_pairs={{0,8},{8,0},{16,24},{24,16},{32,40},{40,32},{48,56},{56,48},{64,72... | collective-permute-start | bytes 2752520 | tf_op jit(solution)/shard_map/ppermute | solution.py:377
  34.1 0.0 copy-start.3
  34.1 0.9 copy-done.3
  35.1 1.5 %collective-permute-done.same_other = bf16[4,64,1792]{2,1,0:T(8,128)(2,1)S(1)} collective-permute-done((bf16[4,64,1792]{2,1,0:T(8,128)(2,1)S(1)}, bf16[4,64,1792]{2,1,0:T(8,128)(2,1)S(1)}, u32[]{:S(2)}, u32[]{:S(2)}) %collective-permute-start) | collective-permute-done | bytes 917536 | tf_op jit(solution)/shard_map/ppermute | solution.py:377
  36.5 0.0 all-to-all-done
  36.6 0.0 copy-start
  36.6 1.3 %copy-done = bf16[4,128,1792]{2,1,0:T(8,128)(2,1)} copy-done((bf16[4,128,1792]{2,1,0:T(8,128)(2,1)}, bf16[4,128,1792]{2,1,0:T(8,128)(2,1)S(1)}, u32[]{:S(2)}) %copy-start) | copy-done | bytes 1835032
  37.8 0.0 copy-done.5
  37.8 0.0 copy-start.4
  37.8 1.2 %copy-done.4 = bf16[256,1792]{1,0:T(8,128)(2,1)S(1)} copy-done((bf16[256,1792]{1,0:T(8,128)(2,1)S(1)}, bf16[256,1792]{1,0:T(8,128)(2,1)}, u32[]{:S(2)}) %copy-start.4) | copy-done | bytes 917528
  39.0 4.3 %shard_map.94 = bf16[8,160,256]{2,1,0:T(8,128)(2,1)} custom-call(bf16[512,1792]{1,0:T(8,128)(2,1)} %bitcast.9, bf16[256,1792]{1,0:T(8,128)(2,1)S(1)} %copy-done.4, bf16[256,1792]{1,0:T(8,128)(2,1)S(1)} %bitcast.12, bf16[128,512]{1,0:T(8,128)(2,1)S(1)} %copy-done.5, bf16[4096,128]{1,0:T(8,128)(2,1)} %basis_ref.1), custom_call_target="tpu_custom_call" | custom-call | flops 1000000000 | tf_op jit(solution)/shard_map/pallas_call | solution.py:194
  43.3 0.1 shard_map.95
  43.4 1.9 %collective-permute-start.1 = (bf16[2,2,64,1792]{3,2,1,0:T(8,128)(2,1)S(1)}, bf16[2,2,64,1792]{3,2,1,0:T(8,128)(2,1)S(1)}, u32[]{:S(2)}, u32[]{:S(2)}) collective-permute-start(bf16[2,2,64,1792]{3,2,1,0:T(8,128)(2,1)S(1)} %shard_map.95), channel_id=1, source_target_pairs={{0,16},{8,120},{16,32},{24,8},{32,48},{40,24},{48,64},{56,40},{64,... | collective-permute-start | bytes 2752520 | tf_op jit(solution)/shard_map/ppermute | solution.py:382
  45.3 9.4 %all-to-all-start.1 = ((bf16[8,160,256]{2,1,0:T(8,128)(2,1)}), bf16[8,160,256]{2,1,0:T(8,128)(2,1)S(1)}, u32[]{:S(2)}, u32[]{:S(2)}) async-start(bf16[8,160,256]{2,1,0:T(8,128)(2,1)} %shard_map.94), calls=%async_computation.1 | async-start | bytes 1310720 | tf_op jit(solution)/shard_map/all_to_all | solution.py:380
  54.7 5.2 %collective-permute-done.1.near = bf16[2,2,64,1792]{3,2,1,0:T(8,128)(2,1)S(1)} collective-permute-done((bf16[2,2,64,1792]{3,2,1,0:T(8,128)(2,1)S(1)}, bf16[2,2,64,1792]{3,2,1,0:T(8,128)(2,1)S(1)}, u32[]{:S(2)}, u32[]{:S(2)}) %collective-permute-start.1) | collective-permute-done | bytes 917536 | tf_op jit(solution)/shard_map/ppermute | solution.py:382
  59.9 1.9 %collective-permute-start.2 = (bf16[2,2,64,1792]{3,2,1,0:T(8,128)(2,1)S(1)}, bf16[2,2,64,1792]{3,2,1,0:T(8,128)(2,1)S(1)}, u32[]{:S(2)}, u32[]{:S(2)}) collective-permute-start(bf16[2,2,64,1792]{3,2,1,0:T(8,128)(2,1)S(1)} %collective-permute-done.1.near), channel_id=1, source_target_pairs={{0,8},{8,0},{16,24},{24,16},{32,40},{40,32},{48,56},{56,48},{64,72... | collective-permute-start | bytes 2752520 | tf_op jit(solution)/shard_map/ppermute | solution.py:383
  61.8 2.4 %collective-permute-done.2.far = bf16[2,2,64,1792]{3,2,1,0:T(8,128)(2,1)S(1)} collective-permute-done((bf16[2,2,64,1792]{3,2,1,0:T(8,128)(2,1)S(1)}, bf16[2,2,64,1792]{3,2,1,0:T(8,128)(2,1)S(1)}, u32[]{:S(2)}, u32[]{:S(2)}) %collective-permute-start.2) | collective-permute-done | bytes 917536 | tf_op jit(solution)/shard_map/ppermute | solution.py:383
  64.2 4.1 %shard_map.96 = bf16[8,160,256]{2,1,0:T(8,128)(2,1)} custom-call(bf16[512,1792]{1,0:T(8,128)(2,1)} %bitcast.10, bf16[256,1792]{1,0:T(8,128)(2,1)S(1)} %bitcast.13, bf16[2,2,64,1792]{3,2,1,0:T(8,128)(2,1)S(1)} %collective-permute-done.1.near, bf16[2,2,64,1792]{3,2,1,0:T(8,128)(2,1)S(1)} %collective-permute-done.2.far), custom_call_target="tpu_custom_call" | custom-call | flops 1000000000 | tf_op jit(solution)/shard_map/pallas_call | solution.py:227
  68.3 0.0 copy-start.1
  68.3 3.2 %all-to-all-done.1.pieces = bf16[8,160,256]{2,1,0:T(8,128)(2,1)S(1)} async-done(((bf16[8,160,256]{2,1,0:T(8,128)(2,1)}), bf16[8,160,256]{2,1,0:T(8,128)(2,1)S(1)}, u32[]{:S(2)}, u32[]{:S(2)}) %all-to-all-start.1) | async-done | bytes 655392 | tf_op jit(solution)/shard_map/all_to_all | solution.py:380
  71.5 6.3 %all-to-all-start.2 = ((bf16[8,160,256]{2,1,0:T(8,128)(2,1)}), bf16[8,160,256]{2,1,0:T(8,128)(2,1)S(1)}, u32[]{:S(2)}, u32[]{:S(2)}) async-start(bf16[8,160,256]{2,1,0:T(8,128)(2,1)} %shard_map.96), calls=%async_computation.2 | async-start | bytes 1310720 | tf_op jit(solution)/shard_map/all_to_all | solution.py:386
  77.8 0.2 shard_map.97
  77.9 12.0 %all_gather.11.coords = bf16[512,128]{1,0:T(8,128)(2,1)S(1)} all-gather(bf16[128,128]{1,0:T(8,128)(2,1)S(1)} %get-tuple-element.23), channel_id=1, replica_groups={{0,128,256,384},{8,136,264,392},{16,144,272,400},{24,152,280,408},{32,1..., dimensions={0}, use_global_device_ids=true | all-gather | bytes 163840 | tf_op jit(solution)/shard_map/all_gather | solution.py:389
  89.9 0.0 copy-done.1
  89.9 0.7 shard_map.98
  90.6 1.9 %collective-permute-start.3 = (f32[8,28,128]{2,1,0:T(8,128)S(1)}, f32[8,28,128]{2,1,0:T(8,128)S(1)}, u32[]{:S(2)}, u32[]{:S(2)}) collective-permute-start(f32[8,28,128]{2,1,0:T(8,128)S(1)} %get-tuple-element.25), channel_id=1, source_target_pairs={{0,8},{8,0},{16,24},{24,16},{32,40},{40,32},{48,56},{56,48},{64,72... | collective-permute-start | bytes 344072 | tf_op jit(solution)/shard_map/ppermute | solution.py:391
  92.6 1.3 %collective-permute-done.3 = f32[8,28,128]{2,1,0:T(8,128)S(1)} collective-permute-done((f32[8,28,128]{2,1,0:T(8,128)S(1)}, f32[8,28,128]{2,1,0:T(8,128)S(1)}, u32[]{:S(2)}, u32[]{:S(2)}) %collective-permute-start.3) | collective-permute-done | bytes 114720 | tf_op jit(solution)/shard_map/ppermute | solution.py:391
  93.9 0.7 add.3
  94.6 0.0 all-to-all-done.2.pieces
  94.6 0.2 shard_map.99
  94.7 6.0 %collective-permute-start.4 = (bf16[128,512]{1,0:T(8,128)(2,1)S(1)}, bf16[128,512]{1,0:T(8,128)(2,1)S(1)}, u32[]{:S(2)}, u32[]{:S(2)}) collective-permute-start(bf16[128,512]{1,0:T(8,128)(2,1)S(1)} %shard_map.99), channel_id=1, source_target_pairs={{0,0},{1,1},{2,128},{3,129},{4,256},{5,257},{6,384},{7,385},{8,8},... | collective-permute-start | bytes 393224 | tf_op jit(solution)/shard_map/ppermute | solution.py:394
  100.8 4.8 %all-to-all-start.3 = ((f32[8,28,128]{2,1,0:T(8,128)}), f32[8,28,128]{2,1,0:T(8,128)S(1)}, u32[]{:S(2)}, u32[]{:S(2)}) async-start(f32[8,28,128]{2,1,0:T(8,128)} %add.3), calls=%async_computation.3 | async-start | bytes 262144 | tf_op jit(solution)/shard_map/all_to_all | solution.py:397
  105.5 0.0 copy-start.2
  105.6 0.0 copy-start.6
  105.6 0.0 copy-start.7
  105.6 3.9 %collective-permute-done.4.parts = bf16[128,512]{1,0:T(8,128)(2,1)S(1)} collective-permute-done((bf16[128,512]{1,0:T(8,128)(2,1)S(1)}, bf16[128,512]{1,0:T(8,128)(2,1)S(1)}, u32[]{:S(2)}, u32[]{:S(2)}) %collective-permute-start.4) | collective-permute-done | bytes 131104 | tf_op jit(solution)/shard_map/ppermute | solution.py:394
  109.5 0.9 shard_map.100
  110.4 3.1 %all-to-all-done.3.parts_ref = f32[8,28,128]{2,1,0:T(8,128)S(1)} async-done(((f32[8,28,128]{2,1,0:T(8,128)}), f32[8,28,128]{2,1,0:T(8,128)S(1)}, u32[]{:S(2)}, u32[]{:S(2)}) %all-to-all-start.3) | async-done | bytes 114720 | tf_op jit(solution)/shard_map/all_to_all | solution.py:397
  113.5 0.0 copy-done.2
  113.5 0.0 copy-done.6
  113.5 0.0 copy-done.7
  113.5 1.3 %shard_map.101 = (f32[28,1,128]{2,1,0:T(1,128)}, f32[28,1,128]{2,1,0:T(1,128)}, f32[28,1,4096]{2,1,0:T(1,128)}) custom-call(f32[8,28,128]{2,1,0:T(8,128)S(1)} %all-to-all-done.3.parts_ref, bf16[4096,128]{1,0:T(8,128)(2,1)S(1)} %copy-done.2, f32[28,1,128]{2,1,0:T(1,128)S(1)} %bitcast.16, f32[28,1,128]{2,1,0:T(1,128)S(1)} %bitcast.17), custom_call_target="tpu_custom_call" | custom-call | tf_op jit(solution)/shard_map/pallas_call | solution.py:360
Async XLA Ops:
  3.0 9.6 %copy-start.8 = (bf16[64,1792]{1,0:T(8,128)(2,1)S(1)}, bf16[64,1792]{1,0:T(8,128)(2,1)}, u32[]{:S(2)}) copy-start(bf16[64,1792]{1,0:T(8,128)(2,1)} %param.8) | copy-start | bytes 688132
  3.0 34.9 %copy-start.5 = (bf16[128,512]{1,0:T(8,128)(2,1)S(1)}, bf16[128,512]{1,0:T(8,128)(2,1)}, u32[]{:S(2)}) copy-start(bf16[128,512]{1,0:T(8,128)(2,1)} %features.1) | copy-start | bytes 393220
  3.0 33.6 %all-to-all-start = ((bf16[4,128,1792]{2,1,0:T(8,128)(2,1)}), bf16[4,128,1792]{2,1,0:T(8,128)(2,1)S(1)}, u32[]{:S(2)}, u32[]{:S(2)}) async-start(bf16[4,128,1792]{2,1,0:T(8,128)(2,1)} %shard_map.93), calls=%async_computation | async-start | bytes 3670016 | tf_op jit(solution)/shard_map/all_to_all | solution.py:374
  32.2 4.4 %collective-permute-start = (bf16[4,64,1792]{2,1,0:T(8,128)(2,1)S(1)}, bf16[4,64,1792]{2,1,0:T(8,128)(2,1)S(1)}, u32[]{:S(2)}, u32[]{:S(2)}) collective-permute-start(bf16[4,64,1792]{2,1,0:T(8,128)(2,1)S(1)} %bitcast.14), channel_id=1, source_target_pairs={{0,8},{8,0},{16,24},{24,16},{32,40},{40,32},{48,56},{56,48},{64,72... | collective-permute-start | bytes 2752520 | tf_op jit(solution)/shard_map/ppermute | solution.py:377
  34.1 0.9 copy-start.3
  36.6 1.3 %copy-start = (bf16[4,128,1792]{2,1,0:T(8,128)(2,1)}, bf16[4,128,1792]{2,1,0:T(8,128)(2,1)S(1)}, u32[]{:S(2)}) copy-start(bf16[4,128,1792]{2,1,0:T(8,128)(2,1)S(1)} %all-to-all-done) | copy-start | bytes 5505028
  37.8 1.2 %copy-start.4 = (bf16[256,1792]{1,0:T(8,128)(2,1)S(1)}, bf16[256,1792]{1,0:T(8,128)(2,1)}, u32[]{:S(2)}) copy-start(bf16[256,1792]{1,0:T(8,128)(2,1)} %copy-done.3) | copy-start | bytes 2752516
  43.4 16.5 %collective-permute-start.1 = (bf16[2,2,64,1792]{3,2,1,0:T(8,128)(2,1)S(1)}, bf16[2,2,64,1792]{3,2,1,0:T(8,128)(2,1)S(1)}, u32[]{:S(2)}, u32[]{:S(2)}) collective-permute-start(bf16[2,2,64,1792]{3,2,1,0:T(8,128)(2,1)S(1)} %shard_map.95), channel_id=1, source_target_pairs={{0,16},{8,120},{16,32},{24,8},{32,48},{40,24},{48,64},{56,40},{64,... | collective-permute-start | bytes 2752520 | tf_op jit(solution)/shard_map/ppermute | solution.py:382
  45.3 26.2 %all-to-all-start.1 = ((bf16[8,160,256]{2,1,0:T(8,128)(2,1)}), bf16[8,160,256]{2,1,0:T(8,128)(2,1)S(1)}, u32[]{:S(2)}, u32[]{:S(2)}) async-start(bf16[8,160,256]{2,1,0:T(8,128)(2,1)} %shard_map.94), calls=%async_computation.1 | async-start | bytes 1310720 | tf_op jit(solution)/shard_map/all_to_all | solution.py:380
  59.9 4.4 %collective-permute-start.2 = (bf16[2,2,64,1792]{3,2,1,0:T(8,128)(2,1)S(1)}, bf16[2,2,64,1792]{3,2,1,0:T(8,128)(2,1)S(1)}, u32[]{:S(2)}, u32[]{:S(2)}) collective-permute-start(bf16[2,2,64,1792]{3,2,1,0:T(8,128)(2,1)S(1)} %collective-permute-done.1.near), channel_id=1, source_target_pairs={{0,8},{8,0},{16,24},{24,16},{32,40},{40,32},{48,56},{56,48},{64,72... | collective-permute-start | bytes 2752520 | tf_op jit(solution)/shard_map/ppermute | solution.py:383
  68.3 21.6 %copy-start.1 = (bf16[4,128,1792]{2,1,0:T(8,128)(2,1)S(1)}, bf16[4,128,1792]{2,1,0:T(8,128)(2,1)}, u32[]{:S(2)}) copy-start(bf16[4,128,1792]{2,1,0:T(8,128)(2,1)} %copy-done) | copy-start | bytes 5505028
  71.5 23.1 %all-to-all-start.2 = ((bf16[8,160,256]{2,1,0:T(8,128)(2,1)}), bf16[8,160,256]{2,1,0:T(8,128)(2,1)S(1)}, u32[]{:S(2)}, u32[]{:S(2)}) async-start(bf16[8,160,256]{2,1,0:T(8,128)(2,1)} %shard_map.96), calls=%async_computation.2 | async-start | bytes 1310720 | tf_op jit(solution)/shard_map/all_to_all | solution.py:386
  90.6 3.2 %collective-permute-start.3 = (f32[8,28,128]{2,1,0:T(8,128)S(1)}, f32[8,28,128]{2,1,0:T(8,128)S(1)}, u32[]{:S(2)}, u32[]{:S(2)}) collective-permute-start(f32[8,28,128]{2,1,0:T(8,128)S(1)} %get-tuple-element.25), channel_id=1, source_target_pairs={{0,8},{8,0},{16,24},{24,16},{32,40},{40,32},{48,56},{56,48},{64,72... | collective-permute-start | bytes 344072 | tf_op jit(solution)/shard_map/ppermute | solution.py:391
  94.7 14.7 %collective-permute-start.4 = (bf16[128,512]{1,0:T(8,128)(2,1)S(1)}, bf16[128,512]{1,0:T(8,128)(2,1)S(1)}, u32[]{:S(2)}, u32[]{:S(2)}) collective-permute-start(bf16[128,512]{1,0:T(8,128)(2,1)S(1)} %shard_map.99), channel_id=1, source_target_pairs={{0,0},{1,1},{2,128},{3,129},{4,256},{5,257},{6,384},{7,385},{8,8},... | collective-permute-start | bytes 393224 | tf_op jit(solution)/shard_map/ppermute | solution.py:394
  100.8 12.7 %all-to-all-start.3 = ((f32[8,28,128]{2,1,0:T(8,128)}), f32[8,28,128]{2,1,0:T(8,128)S(1)}, u32[]{:S(2)}, u32[]{:S(2)}) async-start(f32[8,28,128]{2,1,0:T(8,128)} %add.3), calls=%async_computation.3 | async-start | bytes 262144 | tf_op jit(solution)/shard_map/all_to_all | solution.py:397
  105.5 8.0 %copy-start.2 = (bf16[4096,128]{1,0:T(8,128)(2,1)S(1)}, bf16[4096,128]{1,0:T(8,128)(2,1)}, u32[]{:S(2)}) copy-start(bf16[4096,128]{1,0:T(8,128)(2,1)} %basis_ref.1) | copy-start | bytes 3145732
  105.6 8.0 %copy-start.6 = (f32[1,28,128]{2,0,1:T(1,128)S(1)}, f32[1,28,128]{2,0,1:T(1,128)}, u32[]{:S(2)}) copy-start(f32[1,28,128]{2,0,1:T(1,128)} %param.10) | copy-start | bytes 43012
  105.6 8.0 %copy-start.7 = (f32[1,28,128]{2,0,1:T(1,128)S(1)}, f32[1,28,128]{2,0,1:T(1,128)}, u32[]{:S(2)}) copy-start(f32[1,28,128]{2,0,1:T(1,128)} %param.11) | copy-start | bytes 43012

commit v6 on v5

--- a/solution.py
+++ b/solution.py
@@ -47,8 +47,6 @@
 FINISH_FLOPS = int(4e9)
 FIRST_FLOPS = int(1e9)
 SECOND_FLOPS = int(1e9)
-NEAR_FLOPS = int(1e9)
-NEAR_VMEM = 24_000_000
 Z_ORDER = [0, 4, 1, 5, 2, 6, 3, 7]
 ALONG_Z = [Z_ORDER]
 
@@ -139,8 +137,21 @@
         copy.wait()
 
 
-def first_kernel(left, same, same_other, features, basis, out_ref, part, buffer, sems, sem):
-    x, _, _, z = here()
+def first_kernel(
+    left, same, same_other, features, basis, out_ref, near_ref, part, buffer, sems, near_sems, sem
+):
+    x, _, core, z = here()
+    _, count, height, _ = near_ref.shape
+    nears = []
+    for k, rows in enumerate((same, same_other)):
+        for j in range(count):
+            at = pl.multiple_of((count * core + j) * height, height)
+            nears.append(
+                pltpu.make_async_copy(
+                    rows.at[pl.ds(at, height)], near_ref.at[k, j], near_sems.at[k, j]
+                )
+            )
+            nears[-1].start()
     tokens, width = features.shape
     rank = basis.shape[1]
     start = pl.multiple_of(z * width, width)
@@ -155,13 +166,8 @@
     for k in range(NZ):
         buffer[k, :tokens, buffer.shape[2] - rank :] = coords
     send(buffer, out_ref, x, sems)
-
-
-def near_kernel(same, same_other, near_ref):
-    _, _, core, _ = here()
-    for k, rows in enumerate((same, same_other)):
-        for j in range(NY // 4):
-            near_ref[k, j] = rows[NY // 4 * core + j]
+    for near in nears:
+        near.wait()
 
 
 def rest_kernel(left, same_other, near, far, out_ref, right, buffer, sems):
@@ -189,34 +195,27 @@
 def first_tiles(grads, same, same_other, features, basis):
     tokens, width = features.shape
     rank = basis.shape[1]
+    count, height, hidden = same.shape
     same, same_other = flat(same), flat(same_other)
     shape = (NZ, tokens + tokens // FOLD, same.shape[0] // 2 + rank)
     return pl.pallas_call(
         first_kernel,
-        out_shape=jax.ShapeDtypeStruct(shape, jnp.bfloat16),
+        out_shape=(
+            jax.ShapeDtypeStruct(shape, jnp.bfloat16),
+            jax.ShapeDtypeStruct((2, count // 2, height, hidden), jnp.bfloat16),
+        ),
         in_specs=whole(4) + in_hbm(1),
-        out_specs=in_hbm(1)[0],
+        out_specs=tuple(in_hbm(2)),
         scratch_shapes=[
             pltpu.VMEM((width, rank), jnp.bfloat16),
             pltpu.VMEM(shape, jnp.bfloat16),
             pltpu.SemaphoreType.DMA((NZ,)),
+            pltpu.SemaphoreType.DMA((2, count // 2)),
             pltpu.SemaphoreType.DMA,
         ],
         compiler_params=pltpu.CompilerParams(vmem_limit_bytes=FIRST_VMEM),
         cost_estimate=pl.CostEstimate(flops=FIRST_FLOPS, bytes_accessed=0, transcendentals=0),
     )(flat(grads), same, same_other, features, basis)
-
-
-def neighbour_rows(same, same_other):
-    count, height, hidden = same.shape
-    return pl.pallas_call(
-        near_kernel,
-        out_shape=jax.ShapeDtypeStruct((2, count // 2, height, hidden), jnp.bfloat16),
-        in_specs=whole(2),
-        out_specs=whole(1)[0],
-        compiler_params=pltpu.CompilerParams(vmem_limit_bytes=NEAR_VMEM),
-        cost_estimate=pl.CostEstimate(flops=NEAR_FLOPS, bytes_accessed=0, transcendentals=0),
-    )(same, same_other)
 
 
 def rest_tiles(grads, same_other, near, far):
@@ -375,11 +374,10 @@
     same = lax.all_gather(weight, "dp", axis=0, axis_index_groups=SAME_PARITY)
 
     same_other = lax.ppermute(same, "dp", OTHER_CORE)
-    first = first_tiles(grads, same, same_other, features, basis)
-    first, same, same_other = lax.optimization_barrier((first, same, same_other))
+    first, near = first_tiles(grads, same, same_other, features, basis)
     first = lax.all_to_all(first, "tensor", 0, 0, axis_index_groups=ALONG_Z)
 
-    near = lax.ppermute(neighbour_rows(same, same_other), "dp", TO_NEIGHBOUR)
+    near = lax.ppermute(near, "dp", TO_NEIGHBOUR)
     far = lax.ppermute(near, "dp", OTHER_CORE)
     second = rest_tiles(grads, same_other, near, far)
     first, second = lax.optimization_barrier((first, second))

time: 116 us -> 116 us (level)
    pallas_call x2 -> x1, Pallas kernels: 4.34 us -> 4.46 us  [first_tiles(): pl.pallas_call(first_kernel, out_shape=(jax.ShapeDtypeStruct(shape, jnp.b...]
where the time goes in v6:
time: 116 us; the launch traced here: 115 us
  starting transfers between devices  43.9 us (38%)
  blocking collectives  31.6 us (27%)
  waiting for transfers between devices  20.6 us (18%)
  Pallas kernels  14.1 us (12%)
  local copies, waits for them, and re-layouts  3.41 us (3%)
    all_gather x1, blocking collectives, body(): same = lax.all_gather(weight, 'dp', axis=0, axis_index_groups=SAME_PARITY)  19.7 us
    all_gather x1, blocking collectives, body(): lax.all_gather(coords, 'dp', axis=0, tiled=True, axis_index_groups=ALONG_X)  12 us
    all_to_all x1, starting transfers between devices, body(): lax.all_to_all(spread(out_grad), 'dp', 0, 0, axis_index_groups=ALONG_X)  9.55 us
    all_to_all x1, starting transfers between devices, body(): first = lax.all_to_all(first, 'tensor', 0, 0, axis_index_groups=ALONG_Z)  9.41 us
    all_to_all x1, starting transfers between devices, body(): second = lax.all_to_all(second, 'tensor', 0, 0, axis_index_groups=ALONG_Z)  6.5 us
    ppermute x1, starting transfers between devices, body(): summed = lax.ppermute(join(first, second), ('dp', 'tensor'), HOME)  6.06 us
    ppermute x1, waiting for transfers between devices, body(): near = lax.ppermute(near, 'dp', TO_NEIGHBOUR)  5.37 us
    all_to_all x1, starting transfers between devices, body(): parts = lax.all_to_all(parts, 'dp', 0, 0, axis_index_groups=ALONG_Y)  4.76 us
  transfers between devices with their start and end apart: 9, of which 7 were waited for; matrix products, arithmetic and copies ran while one was open for 1% of the time, Pallas kernels for 5%

profile of v6, /device:TPU:6, one launch (start us, length us, event | category | flops | bytes accessed | tf_op | source)
XLA Modules:
  0.0 115.1 jit_solution(8832384292072676186)
XLA Ops:
  0.6 2.3 %shard_map.93 = bf16[4,128,1792]{2,1,0:T(8,128)(2,1)} custom-call(bf16[128,1792]{1,0:T(8,128)(2,1)} %grads.1), custom_call_target="tpu_custom_call" | custom-call | tf_op jit(solution)/shard_map/pallas_call | solution.py:75
  3.0 0.0 copy-start.8
  3.0 0.0 copy-start.5
  3.0 9.6 %all-to-all-start = ((bf16[4,128,1792]{2,1,0:T(8,128)(2,1)}), bf16[4,128,1792]{2,1,0:T(8,128)(2,1)S(1)}, u32[]{:S(2)}, u32[]{:S(2)}) async-start(bf16[4,128,1792]{2,1,0:T(8,128)(2,1)} %shard_map.93), calls=%async_computation | async-start | bytes 3670016 | tf_op jit(solution)/shard_map/all_to_all | solution.py:373
  12.5 0.0 copy-done.8
  12.5 19.7 %all-gather.same = bf16[256,1792]{1,0:T(8,128)(2,1)S(1)} all-gather(bf16[64,1792]{1,0:T(8,128)(2,1)S(1)} %copy-done.8), channel_id=2, replica_groups={{0,32,64,96},{8,40,72,104},{16,48,80,112},{24,56,88,120},{128,160,192,2..., dimensions={0}, use_global_device_ids=true | all-gather | bytes 1146880 | tf_op jit(solution)/shard_map/all_gather | solution.py:374
  32.2 1.9 %collective-permute-start = (bf16[4,64,1792]{2,1,0:T(8,128)(2,1)S(1)}, bf16[4,64,1792]{2,1,0:T(8,128)(2,1)S(1)}, u32[]{:S(2)}, u32[]{:S(2)}) collective-permute-start(bf16[4,64,1792]{2,1,0:T(8,128)(2,1)S(1)} %bitcast.13), channel_id=1, source_target_pairs={{0,8},{8,0},{16,24},{24,16},{32,40},{40,32},{48,56},{56,48},{64,72... | collective-permute-start | bytes 2752520 | tf_op jit(solution)/shard_map/ppermute | solution.py:376
  34.1 0.0 copy-start.3
  34.1 0.9 copy-done.3
  35.0 1.5 %collective-permute-done = bf16[4,64,1792]{2,1,0:T(8,128)(2,1)S(1)} collective-permute-done((bf16[4,64,1792]{2,1,0:T(8,128)(2,1)S(1)}, bf16[4,64,1792]{2,1,0:T(8,128)(2,1)S(1)}, u32[]{:S(2)}, u32[]{:S(2)}) %collective-permute-start) | collective-permute-done | bytes 917536 | tf_op jit(solution)/shard_map/ppermute | solution.py:376
  36.5 0.0 all-to-all-done
  36.5 0.0 copy-start
  36.5 1.3 %copy-done = bf16[4,128,1792]{2,1,0:T(8,128)(2,1)} copy-done((bf16[4,128,1792]{2,1,0:T(8,128)(2,1)}, bf16[4,128,1792]{2,1,0:T(8,128)(2,1)S(1)}, u32[]{:S(2)}) %copy-start) | copy-done | bytes 1835032
  37.8 0.0 copy-done.5
  37.8 0.0 copy-start.4
  37.8 1.2 %copy-done.4 = bf16[256,1792]{1,0:T(8,128)(2,1)S(1)} copy-done((bf16[256,1792]{1,0:T(8,128)(2,1)S(1)}, bf16[256,1792]{1,0:T(8,128)(2,1)}, u32[]{:S(2)}) %copy-start.4) | copy-done | bytes 917528
  39.0 4.5 %shard_map.94 = (bf16[8,160,256]{2,1,0:T(8,128)(2,1)}, bf16[2,2,64,1792]{3,2,1,0:T(8,128)(2,1)}) custom-call(bf16[512,1792]{1,0:T(8,128)(2,1)} %bitcast.8, bf16[256,1792]{1,0:T(8,128)(2,1)S(1)} %copy-done.4, bf16[256,1792]{1,0:T(8,128)(2,1)S(1)} %bitcast.11, bf16[128,512]{1,0:T(8,128)(2,1)S(1)} %copy-done.5, bf16[4096,128]{1,0:T(8,128)(2,1)} %basis_ref.1), custom_call_target="tpu_custom_call" | custom-call | flops 1000000000 | tf_op jit(solution)/shard_map/pallas_call | solution.py:201
  43.5 1.9 %collective-permute-start.1 = (bf16[2,2,64,1792]{3,2,1,0:T(8,128)(2,1)}, bf16[2,2,64,1792]{3,2,1,0:T(8,128)(2,1)S(1)}, u32[]{:S(2)}, u32[]{:S(2)}) collective-permute-start(bf16[2,2,64,1792]{3,2,1,0:T(8,128)(2,1)} %get-tuple-element.18), channel_id=1, source_target_pairs={{0,16},{8,120},{16,32},{24,8},{32,48},{40,24},{48,64},{56,40},{64,... | collective-permute-start | bytes 2752520 | tf_op jit(solution)/shard_map/ppermute | solution.py:380
  45.4 9.4 %all-to-all-start.1 = ((bf16[8,160,256]{2,1,0:T(8,128)(2,1)}), bf16[8,160,256]{2,1,0:T(8,128)(2,1)S(1)}, u32[]{:S(2)}, u32[]{:S(2)}) async-start(bf16[8,160,256]{2,1,0:T(8,128)(2,1)} %get-tuple-element.17), calls=%async_computation.1 | async-start | bytes 1310720 | tf_op jit(solution)/shard_map/all_to_all | solution.py:378
  54.8 5.4 %collective-permute-done.1.near = bf16[2,2,64,1792]{3,2,1,0:T(8,128)(2,1)S(1)} collective-permute-done((bf16[2,2,64,1792]{3,2,1,0:T(8,128)(2,1)}, bf16[2,2,64,1792]{3,2,1,0:T(8,128)(2,1)S(1)}, u32[]{:S(2)}, u32[]{:S(2)}) %collective-permute-start.1) | collective-permute-done | bytes 917536 | tf_op jit(solution)/shard_map/ppermute | solution.py:380
  60.2 1.9 %collective-permute-start.2 = (bf16[2,2,64,1792]{3,2,1,0:T(8,128)(2,1)S(1)}, bf16[2,2,64,1792]{3,2,1,0:T(8,128)(2,1)S(1)}, u32[]{:S(2)}, u32[]{:S(2)}) collective-permute-start(bf16[2,2,64,1792]{3,2,1,0:T(8,128)(2,1)S(1)} %collective-permute-done.1.near), channel_id=1, source_target_pairs={{0,8},{8,0},{16,24},{24,16},{32,40},{40,32},{48,56},{56,48},{64,72... | collective-permute-start | bytes 2752520 | tf_op jit(solution)/shard_map/ppermute | solution.py:381
  62.1 2.4 %collective-permute-done.2.far = bf16[2,2,64,1792]{3,2,1,0:T(8,128)(2,1)S(1)} collective-permute-done((bf16[2,2,64,1792]{3,2,1,0:T(8,128)(2,1)S(1)}, bf16[2,2,64,1792]{3,2,1,0:T(8,128)(2,1)S(1)}, u32[]{:S(2)}, u32[]{:S(2)}) %collective-permute-start.2) | collective-permute-done | bytes 917536 | tf_op jit(solution)/shard_map/ppermute | solution.py:381
  64.5 4.1 %shard_map.95 = bf16[8,160,256]{2,1,0:T(8,128)(2,1)} custom-call(bf16[512,1792]{1,0:T(8,128)(2,1)} %bitcast.9, bf16[256,1792]{1,0:T(8,128)(2,1)S(1)} %bitcast.12, bf16[2,2,64,1792]{3,2,1,0:T(8,128)(2,1)S(1)} %collective-permute-done.1.near, bf16[2,2,64,1792]{3,2,1,0:T(8,128)(2,1)S(1)} %collective-permute-done.2.far), custom_call_target="tpu_custom_call" | custom-call | flops 1000000000 | tf_op jit(solution)/shard_map/pallas_call | solution.py:226
  68.6 0.0 copy-start.1
  68.6 2.9 %all-to-all-done.1.pieces = bf16[8,160,256]{2,1,0:T(8,128)(2,1)S(1)} async-done(((bf16[8,160,256]{2,1,0:T(8,128)(2,1)}), bf16[8,160,256]{2,1,0:T(8,128)(2,1)S(1)}, u32[]{:S(2)}, u32[]{:S(2)}) %all-to-all-start.1) | async-done | bytes 655392 | tf_op jit(solution)/shard_map/all_to_all | solution.py:378
  71.6 6.5 %all-to-all-start.2 = ((bf16[8,160,256]{2,1,0:T(8,128)(2,1)}), bf16[8,160,256]{2,1,0:T(8,128)(2,1)S(1)}, u32[]{:S(2)}, u32[]{:S(2)}) async-start(bf16[8,160,256]{2,1,0:T(8,128)(2,1)} %shard_map.95), calls=%async_computation.2 | async-start | bytes 1310720 | tf_op jit(solution)/shard_map/all_to_all | solution.py:384
  78.1 0.2 shard_map.96
  78.3 12.0 %all_gather.11.coords = bf16[512,128]{1,0:T(8,128)(2,1)S(1)} all-gather(bf16[128,128]{1,0:T(8,128)(2,1)S(1)} %get-tuple-element.21), channel_id=1, replica_groups={{0,128,256,384},{8,136,264,392},{16,144,272,400},{24,152,280,408},{32,1..., dimensions={0}, use_global_device_ids=true | all-gather | bytes 163840 | tf_op jit(solution)/shard_map/all_gather | solution.py:387
  90.2 0.0 copy-done.1
  90.2 0.7 shard_map.97
  91.0 1.9 %collective-permute-start.3 = (f32[8,28,128]{2,1,0:T(8,128)S(1)}, f32[8,28,128]{2,1,0:T(8,128)S(1)}, u32[]{:S(2)}, u32[]{:S(2)}) collective-permute-start(f32[8,28,128]{2,1,0:T(8,128)S(1)} %get-tuple-element.23), channel_id=1, source_target_pairs={{0,8},{8,0},{16,24},{24,16},{32,40},{40,32},{48,56},{56,48},{64,72... | collective-permute-start | bytes 344072 | tf_op jit(solution)/shard_map/ppermute | solution.py:389
  92.9 1.3 %collective-permute-done.3 = f32[8,28,128]{2,1,0:T(8,128)S(1)} collective-permute-done((f32[8,28,128]{2,1,0:T(8,128)S(1)}, f32[8,28,128]{2,1,0:T(8,128)S(1)}, u32[]{:S(2)}, u32[]{:S(2)}) %collective-permute-start.3) | collective-permute-done | bytes 114720 | tf_op jit(solution)/shard_map/ppermute | solution.py:389
  94.2 0.7 add.3
  94.9 0.0 all-to-all-done.2.pieces
  94.9 0.2 shard_map.98
  95.0 6.1 %collective-permute-start.4 = (bf16[128,512]{1,0:T(8,128)(2,1)S(1)}, bf16[128,512]{1,0:T(8,128)(2,1)S(1)}, u32[]{:S(2)}, u32[]{:S(2)}) collective-permute-start(bf16[128,512]{1,0:T(8,128)(2,1)S(1)} %shard_map.98), channel_id=1, source_target_pairs={{0,0},{1,1},{2,128},{3,129},{4,256},{5,257},{6,384},{7,385},{8,8},... | collective-permute-start | bytes 393224 | tf_op jit(solution)/shard_map/ppermute | solution.py:392
  101.1 4.8 %all-to-all-start.3 = ((f32[8,28,128]{2,1,0:T(8,128)}), f32[8,28,128]{2,1,0:T(8,128)S(1)}, u32[]{:S(2)}, u32[]{:S(2)}) async-start(f32[8,28,128]{2,1,0:T(8,128)} %add.3), calls=%async_computation.3 | async-start | bytes 262144 | tf_op jit(solution)/shard_map/all_to_all | solution.py:395
  105.9 0.0 copy-start.2
  105.9 0.0 copy-start.6
  105.9 0.0 copy-start.7
  105.9 3.9 %collective-permute-done.4.parts = bf16[128,512]{1,0:T(8,128)(2,1)S(1)} collective-permute-done((bf16[128,512]{1,0:T(8,128)(2,1)S(1)}, bf16[128,512]{1,0:T(8,128)(2,1)S(1)}, u32[]{:S(2)}, u32[]{:S(2)}) %collective-permute-start.4) | collective-permute-done | bytes 131104 | tf_op jit(solution)/shard_map/ppermute | solution.py:392
  109.8 0.9 shard_map.99
  110.7 3.1 %all-to-all-done.3.parts_ref = f32[8,28,128]{2,1,0:T(8,128)S(1)} async-done(((f32[8,28,128]{2,1,0:T(8,128)}), f32[8,28,128]{2,1,0:T(8,128)S(1)}, u32[]{:S(2)}, u32[]{:S(2)}) %all-to-all-start.3) | async-done | bytes 114720 | tf_op jit(solution)/shard_map/all_to_all | solution.py:395
  113.8 0.0 copy-done.2
  113.8 0.0 copy-done.6
  113.8 0.0 copy-done.7
  113.8 1.3 %shard_map.100 = (f32[28,1,128]{2,1,0:T(1,128)}, f32[28,1,128]{2,1,0:T(1,128)}, f32[28,1,4096]{2,1,0:T(1,128)}) custom-call(f32[8,28,128]{2,1,0:T(8,128)S(1)} %all-to-all-done.3.parts_ref, bf16[4096,128]{1,0:T(8,128)(2,1)S(1)} %copy-done.2, f32[28,1,128]{2,1,0:T(1,128)S(1)} %bitcast.14, f32[28,1,128]{2,1,0:T(1,128)S(1)} %bitcast.15), custom_call_target="tpu_custom_call" | custom-call | tf_op jit(solution)/shard_map/pallas_call | solution.py:359
Async XLA Ops:
  3.0 9.6 %copy-start.8 = (bf16[64,1792]{1,0:T(8,128)(2,1)S(1)}, bf16[64,1792]{1,0:T(8,128)(2,1)}, u32[]{:S(2)}) copy-start(bf16[64,1792]{1,0:T(8,128)(2,1)} %param.8) | copy-start | bytes 688132
  3.0 34.8 %copy-start.5 = (bf16[128,512]{1,0:T(8,128)(2,1)S(1)}, bf16[128,512]{1,0:T(8,128)(2,1)}, u32[]{:S(2)}) copy-start(bf16[128,512]{1,0:T(8,128)(2,1)} %features.1) | copy-start | bytes 393220
  3.0 33.6 %all-to-all-start = ((bf16[4,128,1792]{2,1,0:T(8,128)(2,1)}), bf16[4,128,1792]{2,1,0:T(8,128)(2,1)S(1)}, u32[]{:S(2)}, u32[]{:S(2)}) async-start(bf16[4,128,1792]{2,1,0:T(8,128)(2,1)} %shard_map.93), calls=%async_computation | async-start | bytes 3670016 | tf_op jit(solution)/shard_map/all_to_all | solution.py:373
  32.2 4.4 %collective-permute-start = (bf16[4,64,1792]{2,1,0:T(8,128)(2,1)S(1)}, bf16[4,64,1792]{2,1,0:T(8,128)(2,1)S(1)}, u32[]{:S(2)}, u32[]{:S(2)}) collective-permute-start(bf16[4,64,1792]{2,1,0:T(8,128)(2,1)S(1)} %bitcast.13), channel_id=1, source_target_pairs={{0,8},{8,0},{16,24},{24,16},{32,40},{40,32},{48,56},{56,48},{64,72... | collective-permute-start | bytes 2752520 | tf_op jit(solution)/shard_map/ppermute | solution.py:376
  34.1 0.9 copy-start.3
  36.5 1.3 %copy-start = (bf16[4,128,1792]{2,1,0:T(8,128)(2,1)}, bf16[4,128,1792]{2,1,0:T(8,128)(2,1)S(1)}, u32[]{:S(2)}) copy-start(bf16[4,128,1792]{2,1,0:T(8,128)(2,1)S(1)} %all-to-all-done) | copy-start | bytes 5505028
  37.8 1.2 %copy-start.4 = (bf16[256,1792]{1,0:T(8,128)(2,1)S(1)}, bf16[256,1792]{1,0:T(8,128)(2,1)}, u32[]{:S(2)}) copy-start(bf16[256,1792]{1,0:T(8,128)(2,1)} %copy-done.3) | copy-start | bytes 2752516
  43.5 16.7 %collective-permute-start.1 = (bf16[2,2,64,1792]{3,2,1,0:T(8,128)(2,1)}, bf16[2,2,64,1792]{3,2,1,0:T(8,128)(2,1)S(1)}, u32[]{:S(2)}, u32[]{:S(2)}) collective-permute-start(bf16[2,2,64,1792]{3,2,1,0:T(8,128)(2,1)} %get-tuple-element.18), channel_id=1, source_target_pairs={{0,16},{8,120},{16,32},{24,8},{32,48},{40,24},{48,64},{56,40},{64,... | collective-permute-start | bytes 2752520 | tf_op jit(solution)/shard_map/ppermute | solution.py:380
  45.4 26.2 %all-to-all-start.1 = ((bf16[8,160,256]{2,1,0:T(8,128)(2,1)}), bf16[8,160,256]{2,1,0:T(8,128)(2,1)S(1)}, u32[]{:S(2)}, u32[]{:S(2)}) async-start(bf16[8,160,256]{2,1,0:T(8,128)(2,1)} %get-tuple-element.17), calls=%async_computation.1 | async-start | bytes 1310720 | tf_op jit(solution)/shard_map/all_to_all | solution.py:378
  60.2 4.4 %collective-permute-start.2 = (bf16[2,2,64,1792]{3,2,1,0:T(8,128)(2,1)S(1)}, bf16[2,2,64,1792]{3,2,1,0:T(8,128)(2,1)S(1)}, u32[]{:S(2)}, u32[]{:S(2)}) collective-permute-start(bf16[2,2,64,1792]{3,2,1,0:T(8,128)(2,1)S(1)} %collective-permute-done.1.near), channel_id=1, source_target_pairs={{0,8},{8,0},{16,24},{24,16},{32,40},{40,32},{48,56},{56,48},{64,72... | collective-permute-start | bytes 2752520 | tf_op jit(solution)/shard_map/ppermute | solution.py:381
  68.6 21.6 %copy-start.1 = (bf16[4,128,1792]{2,1,0:T(8,128)(2,1)S(1)}, bf16[4,128,1792]{2,1,0:T(8,128)(2,1)}, u32[]{:S(2)}) copy-start(bf16[4,128,1792]{2,1,0:T(8,128)(2,1)} %copy-done) | copy-start | bytes 5505028
  71.6 23.3 %all-to-all-start.2 = ((bf16[8,160,256]{2,1,0:T(8,128)(2,1)}), bf16[8,160,256]{2,1,0:T(8,128)(2,1)S(1)}, u32[]{:S(2)}, u32[]{:S(2)}) async-start(bf16[8,160,256]{2,1,0:T(8,128)(2,1)} %shard_map.95), calls=%async_computation.2 | async-start | bytes 1310720 | tf_op jit(solution)/shard_map/all_to_all | solution.py:384
  91.0 3.2 %collective-permute-start.3 = (f32[8,28,128]{2,1,0:T(8,128)S(1)}, f32[8,28,128]{2,1,0:T(8,128)S(1)}, u32[]{:S(2)}, u32[]{:S(2)}) collective-permute-start(f32[8,28,128]{2,1,0:T(8,128)S(1)} %get-tuple-element.23), channel_id=1, source_target_pairs={{0,8},{8,0},{16,24},{24,16},{32,40},{40,32},{48,56},{56,48},{64,72... | collective-permute-start | bytes 344072 | tf_op jit(solution)/shard_map/ppermute | solution.py:389
  95.0 14.7 %collective-permute-start.4 = (bf16[128,512]{1,0:T(8,128)(2,1)S(1)}, bf16[128,512]{1,0:T(8,128)(2,1)S(1)}, u32[]{:S(2)}, u32[]{:S(2)}) collective-permute-start(bf16[128,512]{1,0:T(8,128)(2,1)S(1)} %shard_map.98), channel_id=1, source_target_pairs={{0,0},{1,1},{2,128},{3,129},{4,256},{5,257},{6,384},{7,385},{8,8},... | collective-permute-start | bytes 393224 | tf_op jit(solution)/shard_map/ppermute | solution.py:392
  101.1 12.7 %all-to-all-start.3 = ((f32[8,28,128]{2,1,0:T(8,128)}), f32[8,28,128]{2,1,0:T(8,128)S(1)}, u32[]{:S(2)}, u32[]{:S(2)}) async-start(f32[8,28,128]{2,1,0:T(8,128)} %add.3), calls=%async_computation.3 | async-start | bytes 262144 | tf_op jit(solution)/shard_map/all_to_all | solution.py:395
  105.9 8.0 %copy-start.2 = (bf16[4096,128]{1,0:T(8,128)(2,1)S(1)}, bf16[4096,128]{1,0:T(8,128)(2,1)}, u32[]{:S(2)}) copy-start(bf16[4096,128]{1,0:T(8,128)(2,1)} %basis_ref.1) | copy-start | bytes 3145732
  105.9 8.0 %copy-start.6 = (f32[1,28,128]{2,0,1:T(1,128)S(1)}, f32[1,28,128]{2,0,1:T(1,128)}, u32[]{:S(2)}) copy-start(f32[1,28,128]{2,0,1:T(1,128)} %param.10) | copy-start | bytes 43012
  105.9 8.0 %copy-start.7 = (f32[1,28,128]{2,0,1:T(1,128)S(1)}, f32[1,28,128]{2,0,1:T(1,128)}, u32[]{:S(2)}) copy-start(f32[1,28,128]{2,0,1:T(1,128)} %param.11) | copy-start | bytes 43012

commit v7 on v6

--- a/solution.py
+++ b/solution.py
@@ -51,7 +51,7 @@
 ALONG_Z = [Z_ORDER]
 
 VMEM_BYTES = 24 * 1024 * 1024
-FIRST_VMEM = 53_000_000
+FIRST_VMEM = 53_600_000
 SECOND_VMEM = 53_000_000
 
 
@@ -81,17 +81,20 @@
     )(grads)
 
 
-FOLD = 4
-
-
-def folded(block):
-    step = block.shape[0] // FOLD
-    return jnp.concatenate([block[k * step : (k + 1) * step] for k in range(FOLD)], axis=1)
-
-
-def unfolded(block):
-    step = block.shape[1] // FOLD
-    return jnp.concatenate([block[:, k * step : (k + 1) * step] for k in range(FOLD)], axis=0)
+EARLY = 32
+
+
+def folded(block, width):
+    step = block.shape[0] * block.shape[1] // width
+    return jnp.concatenate(
+        [block[k * step : (k + 1) * step] for k in range(block.shape[0] // step)], axis=1
+    )
+
+
+def unfolded(block, columns):
+    return jnp.concatenate(
+        [block[:, k : k + columns] for k in range(0, block.shape[1], columns)], axis=0
+    )
 
 
 def times(left, rows):
@@ -100,22 +103,34 @@
     ).astype(jnp.bfloat16)
 
 
-def other_rows(same_other, k):
-    height = same_other.shape[0] // (NY // 2)
+def other_rows(same_other, start, stop):
+    half = same_other.shape[0] // 2
     return jnp.concatenate(
-        [same_other[(2 * h + k) * height : (2 * h + k + 1) * height, :] for h in range(2)], axis=0
-    )
-
-
-def fill(buffer, at, tokens, product):
+        [same_other[h * half + start : h * half + stop, :] for h in range(2)], axis=0
+    )
+
+
+def fill(buffer, tokens, product):
     width = product.shape[1] // 2
     for block in range(NX):
         for h in range(2):
+            buffer[2 * block + h, :tokens, :width] = product[
+                block * tokens : (block + 1) * tokens, h * width : (h + 1) * width
+            ]
+
+
+def fill_below(buffer, tokens, product):
+    width = product.shape[1] // 2
+    columns = buffer.shape[2]
+    for block in range(NX):
+        for h in range(2):
             part = product[block * tokens : (block + 1) * tokens, h * width : (h + 1) * width]
-            if at is None:
-                buffer[2 * block + h, tokens:, :] = folded(part)
-            else:
-                buffer[2 * block + h, :tokens, at : at + width] = part
+            at = tokens
+            for start, stop in ((0, EARLY), (EARLY, width)):
+                if start < stop:
+                    below = folded(part[:, start:stop], columns)
+                    buffer[2 * block + h, at : at + below.shape[0], :] = below
+                    at += below.shape[0]
 
 
 def slot_of(q, h):
@@ -157,8 +172,8 @@
     start = pl.multiple_of(z * width, width)
     copy = pltpu.make_async_copy(basis.at[pl.ds(start, width), :], part, sem)
     copy.start()
-    fill(buffer, 0, tokens, times(left, same[...]))
-    fill(buffer, None, tokens, times(left, other_rows(same_other, 0)))
+    fill(buffer, tokens, times(left, same[...]))
+    fill_below(buffer, tokens, times(left, other_rows(same_other, 0, EARLY)))
     copy.wait()
     coords = jnp.dot(features[...], part[...], preferred_element_type=jnp.float32).astype(
         jnp.bfloat16
@@ -183,8 +198,8 @@
         for source, half in ((near, core), (far, 1 - core)):
             place(NY // 4 * half + j, half, source[0, j])
             place(NY // 4 * half + j, 1 - half, source[1, j])
-    fill(buffer, None, tokens, times(left, other_rows(same_other, 1)))
-    fill(buffer, 0, tokens, times(left, right[...]))
+    fill_below(buffer, tokens, times(left, other_rows(same_other, EARLY, same_other.shape[0] // 2)))
+    fill(buffer, tokens, times(left, right[...]))
     send(buffer, out_ref, x, sems)
 
 
@@ -197,7 +212,8 @@
     rank = basis.shape[1]
     count, height, hidden = same.shape
     same, same_other = flat(same), flat(same_other)
-    shape = (NZ, tokens + tokens // FOLD, same.shape[0] // 2 + rank)
+    columns = same.shape[0] // 2 + rank
+    shape = (NZ, tokens + tokens * EARLY // columns, columns)
     return pl.pallas_call(
         first_kernel,
         out_shape=(
@@ -222,7 +238,8 @@
     tokens, hidden = grads.shape[1:]
     same_other = flat(same_other)
     rows = (near.size + far.size) // hidden
-    shape = (NZ, tokens + tokens // FOLD, rows // 2)
+    late = same_other.shape[0] // 2 - EARLY
+    shape = (NZ, tokens + tokens * late // (rows // 2), rows // 2)
     return pl.pallas_call(
         rest_kernel,
         out_shape=jax.ShapeDtypeStruct(shape, jnp.bfloat16),
@@ -243,17 +260,16 @@
     tokens, rank = coords_ref.shape
     width = total.shape[1] - rank
     summed_ref[:, :width] = total[:tokens, :width]
-    summed_ref[:, width:] = unfolded(total[tokens:])
+    summed_ref[:, width:] = unfolded(total[tokens:], EARLY)
     coords_ref[...] = total[:tokens, width:].astype(jnp.bfloat16)
 
 
-def sum_first(pieces, rank):
-    tokens = pieces.shape[1] * FOLD // (FOLD + 1)
+def sum_first(pieces, tokens, rank):
     width = pieces.shape[2]
     return pl.pallas_call(
         sum_kernel,
         out_shape=(
-            jax.ShapeDtypeStruct((tokens, width - rank + width // FOLD), jnp.float32),
+            jax.ShapeDtypeStruct((tokens, width - rank + EARLY), jnp.float32),
             jax.ShapeDtypeStruct((tokens, rank), jnp.bfloat16),
         ),
         in_specs=whole(1),
@@ -266,14 +282,21 @@
     total = jnp.sum(pieces[...].astype(jnp.float32), axis=0)
     tokens, width = first.shape
     out_ref[:, :width] = first[...].astype(jnp.bfloat16)
-    rest = unfolded(total[tokens:])
-    out_ref[:, width : width + rest.shape[1]] = rest.astype(jnp.bfloat16)
-    out_ref[:, width + rest.shape[1] :] = total[:tokens].astype(jnp.bfloat16)
+    columns = total.shape[1]
+    below = tokens
+    late = (total.shape[0] - tokens) * columns // tokens
+    for count in [c for c in (EARLY, late - EARLY) if c > 0]:
+        rows = tokens * count // columns
+        part = unfolded(total[below : below + rows], count)
+        out_ref[:, width : width + count] = part.astype(jnp.bfloat16)
+        below += rows
+        width += count
+    out_ref[:, width:] = total[:tokens].astype(jnp.bfloat16)
 
 
 def join(first, pieces):
     tokens, width = first.shape
-    columns = width + pieces.shape[2] // FOLD + pieces.shape[2]
+    columns = width + pieces.shape[1] * pieces.shape[2] // tokens
     return pl.pallas_call(
         join_kernel,
         out_shape=jax.ShapeDtypeStruct((tokens, columns), jnp.bfloat16),
@@ -382,7 +405,7 @@
     second = rest_tiles(grads, same_other, near, far)
     first, second = lax.optimization_barrier((first, second))
     second = lax.all_to_all(second, "tensor", 0, 0, axis_index_groups=ALONG_Z)
-    first, coords = sum_first(first, basis.shape[1])
+    first, coords = sum_first(first, features.shape[0], basis.shape[1])
 
     coords = lax.all_gather(coords, "dp", axis=0, tiled=True, axis_index_groups=ALONG_X)
     parts, other = project(grads, coords)

time: 116 us -> 116 us (level)
  local copies, waits for them, and re-layouts: 3.41 us -> 1.3 us
  starting transfers between devices: 43.9 us -> 45.9 us
    unnamed x18 -> x14, local copies, waits for them, and re-layouts: 3.41 us -> 1.3 us
    ppermute x1, waiting for transfers between devices: 3.89 us -> 2.2 us  [body(): summed = lax.ppermute(join(first, second), ('dp', 'tensor'), HOME)]
    all_to_all x1, waiting for transfers between devices: 2.94 us -> 1.29 us  [body(): first = lax.all_to_all(first, 'tensor', 0, 0, axis_index_groups=ALONG_Z)]
    all_to_all x1, starting transfers between devices: 6.5 us -> 8.15 us  [body(): second = lax.all_to_all(second, 'tensor', 0, 0, axis_index_groups=ALONG_Z)]
    all_to_all x1, waiting for transfers between devices: 3.13 us -> 4.73 us  [body(): parts = lax.all_to_all(parts, 'dp', 0, 0, axis_index_groups=ALONG_Y)]
    all_to_all x1, waiting for transfers between devices: 0.01 us -> 1.33 us  [body(): second = lax.all_to_all(second, 'tensor', 0, 0, axis_index_groups=ALONG_Z)]
  transfers between devices with their start and end apart: 9 -> 9, of which waited for: 7 -> 8; matrix products, arithmetic and copies ran while one was open for 1% -> 1% of each run, Pallas kernels for 5% -> 5%
where the time goes in v7:
time: 116 us
  starting transfers between devices  45.9 us (40%)
  blocking collectives  31.6 us (27%)
  waiting for transfers between devices  21.2 us (18%)
  Pallas kernels  14 us (12%)
  local copies, waits for them, and re-layouts  1.3 us (1%)
    all_gather x1, blocking collectives, body(): same = lax.all_gather(weight, 'dp', axis=0, axis_index_groups=SAME_PARITY)  19.7 us
    all_gather x1, blocking collectives, body(): lax.all_gather(coords, 'dp', axis=0, tiled=True, axis_index_groups=ALONG_X)  12 us
    all_to_all x1, starting transfers between devices, body(): lax.all_to_all(spread(out_grad), 'dp', 0, 0, axis_index_groups=ALONG_X)  9.55 us
    all_to_all x1, starting transfers between devices, body(): first = lax.all_to_all(first, 'tensor', 0, 0, axis_index_groups=ALONG_Z)  9.41 us
    all_to_all x1, starting transfers between devices, body(): second = lax.all_to_all(second, 'tensor', 0, 0, axis_index_groups=ALONG_Z)  8.15 us
    ppermute x1, starting transfers between devices, body(): summed = lax.ppermute(join(first, second), ('dp', 'tensor'), HOME)  6.4 us
    ppermute x1, waiting for transfers between devices, body(): near = lax.ppermute(near, 'dp', TO_NEIGHBOUR)  5.37 us
    all_to_all x1, starting transfers between devices, body(): parts = lax.all_to_all(parts, 'dp', 0, 0, axis_index_groups=ALONG_Y)  4.77 us
  transfers between devices with their start and end apart: 9, of which 8 were waited for; matrix products, arithmetic and copies ran while one was open for 1% of the time, Pallas kernels for 5%

profile of v7, /device:TPU:6, one launch (start us, length us, event | category | flops | bytes accessed | tf_op | source)
XLA Modules:
  0.0 115.6 jit_solution(6294130633351131666)
XLA Ops:
  0.6 2.3 %shard_map.93 = bf16[4,128,1792]{2,1,0:T(8,128)(2,1)} custom-call(bf16[128,1792]{1,0:T(8,128)(2,1)} %grads.1), custom_call_target="tpu_custom_call" | custom-call | tf_op jit(solution)/shard_map/pallas_call | solution.py:75
  3.0 0.0 copy-start.6
  3.0 0.0 copy-start.3
  3.0 9.6 %all-to-all-start = ((bf16[4,128,1792]{2,1,0:T(8,128)(2,1)}), bf16[4,128,1792]{2,1,0:T(8,128)(2,1)S(1)}, u32[]{:S(2)}, u32[]{:S(2)}) async-start(bf16[4,128,1792]{2,1,0:T(8,128)(2,1)} %shard_map.93), calls=%async_computation | async-start | bytes 3670016 | tf_op jit(solution)/shard_map/all_to_all | solution.py:396
  12.5 0.0 copy-done.6
  12.5 19.7 %all-gather.same = bf16[256,1792]{1,0:T(8,128)(2,1)S(1)} all-gather(bf16[64,1792]{1,0:T(8,128)(2,1)S(1)} %copy-done.6), channel_id=2, replica_groups={{0,32,64,96},{8,40,72,104},{16,48,80,112},{24,56,88,120},{128,160,192,2..., dimensions={0}, use_global_device_ids=true | all-gather | bytes 1146880 | tf_op jit(solution)/shard_map/all_gather | solution.py:397
  32.2 1.9 %collective-permute-start = (bf16[4,64,1792]{2,1,0:T(8,128)(2,1)S(1)}, bf16[4,64,1792]{2,1,0:T(8,128)(2,1)}, u32[]{:S(2)}, u32[]{:S(2)}) collective-permute-start(bf16[4,64,1792]{2,1,0:T(8,128)(2,1)S(1)} %bitcast.11), channel_id=1, source_target_pairs={{0,8},{8,0},{16,24},{24,16},{32,40},{40,32},{48,56},{56,48},{64,72... | collective-permute-start | bytes 2752520 | tf_op jit(solution)/shard_map/ppermute | solution.py:399
  34.1 2.6 %collective-permute-done = bf16[4,64,1792]{2,1,0:T(8,128)(2,1)} collective-permute-done((bf16[4,64,1792]{2,1,0:T(8,128)(2,1)S(1)}, bf16[4,64,1792]{2,1,0:T(8,128)(2,1)}, u32[]{:S(2)}, u32[]{:S(2)}) %collective-permute-start) | collective-permute-done | bytes 917536 | tf_op jit(solution)/shard_map/ppermute | solution.py:399
  36.7 0.0 all-to-all-done
  36.7 0.0 copy-start
  36.7 1.3 %copy-done = bf16[4,128,1792]{2,1,0:T(8,128)(2,1)} copy-done((bf16[4,128,1792]{2,1,0:T(8,128)(2,1)}, bf16[4,128,1792]{2,1,0:T(8,128)(2,1)S(1)}, u32[]{:S(2)}) %copy-start) | copy-done | bytes 1835032
  38.0 0.0 copy-done.3
  38.0 4.1 %shard_map.94 = (bf16[8,144,256]{2,1,0:T(8,128)(2,1)}, bf16[2,2,64,1792]{3,2,1,0:T(8,128)(2,1)}) custom-call(bf16[512,1792]{1,0:T(8,128)(2,1)} %bitcast.8, bf16[256,1792]{1,0:T(8,128)(2,1)S(1)} %all-gather.same, bf16[256,1792]{1,0:T(8,128)(2,1)} %bitcast.2.same_other, bf16[128,512]{1,0:T(8,128)(2,1)S(1)} %copy-done.3, bf16[4096,128]{1,0:T(8,128)(2,1)} %basis_ref.1), custom_call_target="tpu_custom_call" | custom-call | flops 1000000000 | tf_op jit(solution)/shard_map/pallas_call | solution.py:217
  42.1 1.9 %collective-permute-start.1 = (bf16[2,2,64,1792]{3,2,1,0:T(8,128)(2,1)}, bf16[2,2,64,1792]{3,2,1,0:T(8,128)(2,1)S(1)}, u32[]{:S(2)}, u32[]{:S(2)}) collective-permute-start(bf16[2,2,64,1792]{3,2,1,0:T(8,128)(2,1)} %get-tuple-element.18), channel_id=1, source_target_pairs={{0,16},{8,120},{16,32},{24,8},{32,48},{40,24},{48,64},{56,40},{64,... | collective-permute-start | bytes 2752520 | tf_op jit(solution)/shard_map/ppermute | solution.py:403
  44.0 9.4 %all-to-all-start.1 = ((bf16[8,144,256]{2,1,0:T(8,128)(2,1)}), bf16[8,144,256]{2,1,0:T(8,128)(2,1)S(1)}, u32[]{:S(2)}, u32[]{:S(2)}) async-start(bf16[8,144,256]{2,1,0:T(8,128)(2,1)} %get-tuple-element.17), calls=%async_computation.1 | async-start | bytes 1179648 | tf_op jit(solution)/shard_map/all_to_all | solution.py:401
  53.4 5.4 %collective-permute-done.1.near = bf16[2,2,64,1792]{3,2,1,0:T(8,128)(2,1)S(1)} collective-permute-done((bf16[2,2,64,1792]{3,2,1,0:T(8,128)(2,1)}, bf16[2,2,64,1792]{3,2,1,0:T(8,128)(2,1)S(1)}, u32[]{:S(2)}, u32[]{:S(2)}) %collective-permute-start.1) | collective-permute-done | bytes 917536 | tf_op jit(solution)/shard_map/ppermute | solution.py:403
  58.8 1.9 %collective-permute-start.2 = (bf16[2,2,64,1792]{3,2,1,0:T(8,128)(2,1)S(1)}, bf16[2,2,64,1792]{3,2,1,0:T(8,128)(2,1)S(1)}, u32[]{:S(2)}, u32[]{:S(2)}) collective-permute-start(bf16[2,2,64,1792]{3,2,1,0:T(8,128)(2,1)S(1)} %collective-permute-done.1.near), channel_id=1, source_target_pairs={{0,8},{8,0},{16,24},{24,16},{32,40},{40,32},{48,56},{56,48},{64,72... | collective-permute-start | bytes 2752520 | tf_op jit(solution)/shard_map/ppermute | solution.py:404
  60.7 2.4 %collective-permute-done.2.far = bf16[2,2,64,1792]{3,2,1,0:T(8,128)(2,1)S(1)} collective-permute-done((bf16[2,2,64,1792]{3,2,1,0:T(8,128)(2,1)S(1)}, bf16[2,2,64,1792]{3,2,1,0:T(8,128)(2,1)S(1)}, u32[]{:S(2)}, u32[]{:S(2)}) %collective-permute-start.2) | collective-permute-done | bytes 917536 | tf_op jit(solution)/shard_map/ppermute | solution.py:404
  63.1 4.4 %shard_map.95 = bf16[8,176,256]{2,1,0:T(8,128)(2,1)} custom-call(bf16[512,1792]{1,0:T(8,128)(2,1)} %bitcast.9, bf16[256,1792]{1,0:T(8,128)(2,1)} %bitcast.2.same_other, bf16[2,2,64,1792]{3,2,1,0:T(8,128)(2,1)S(1)} %collective-permute-done.1.near, bf16[2,2,64,1792]{3,2,1,0:T(8,128)(2,1)S(1)} %collective-permute-done.2.far), custom_call_target="tpu_custom_call" | custom-call | flops 1000000000 | tf_op jit(solution)/shard_map/pallas_call | solution.py:243
  67.5 0.0 copy-start.1
  67.5 1.3 %all-to-all-done.1.pieces = bf16[8,144,256]{2,1,0:T(8,128)(2,1)S(1)} async-done(((bf16[8,144,256]{2,1,0:T(8,128)(2,1)}), bf16[8,144,256]{2,1,0:T(8,128)(2,1)S(1)}, u32[]{:S(2)}, u32[]{:S(2)}) %all-to-all-start.1) | async-done | bytes 589856 | tf_op jit(solution)/shard_map/all_to_all | solution.py:401
  68.8 8.2 %all-to-all-start.2 = ((bf16[8,176,256]{2,1,0:T(8,128)(2,1)}), bf16[8,176,256]{2,1,0:T(8,128)(2,1)S(1)}, u32[]{:S(2)}, u32[]{:S(2)}) async-start(bf16[8,176,256]{2,1,0:T(8,128)(2,1)} %shard_map.95), calls=%async_computation.2 | async-start | bytes 1441792 | tf_op jit(solution)/shard_map/all_to_all | solution.py:407
  77.0 0.2 shard_map.96
  77.1 12.0 %all_gather.11.coords = bf16[512,128]{1,0:T(8,128)(2,1)S(1)} all-gather(bf16[128,128]{1,0:T(8,128)(2,1)S(1)} %get-tuple-element.21), channel_id=1, replica_groups={{0,128,256,384},{8,136,264,392},{16,144,272,400},{24,152,280,408},{32,1..., dimensions={0}, use_global_device_ids=true | all-gather | bytes 163840 | tf_op jit(solution)/shard_map/all_gather | solution.py:410
  89.1 0.0 copy-done.1
  89.1 0.7 shard_map.97
  89.8 1.9 %collective-permute-start.3 = (f32[8,28,128]{2,1,0:T(8,128)S(1)}, f32[8,28,128]{2,1,0:T(8,128)S(1)}, u32[]{:S(2)}, u32[]{:S(2)}) collective-permute-start(f32[8,28,128]{2,1,0:T(8,128)S(1)} %get-tuple-element.23), channel_id=1, source_target_pairs={{0,8},{8,0},{16,24},{24,16},{32,40},{40,32},{48,56},{56,48},{64,72... | collective-permute-start | bytes 344072 | tf_op jit(solution)/shard_map/ppermute | solution.py:412
  91.8 1.3 %collective-permute-done.3 = f32[8,28,128]{2,1,0:T(8,128)S(1)} collective-permute-done((f32[8,28,128]{2,1,0:T(8,128)S(1)}, f32[8,28,128]{2,1,0:T(8,128)S(1)}, u32[]{:S(2)}, u32[]{:S(2)}) %collective-permute-start.3) | collective-permute-done | bytes 114720 | tf_op jit(solution)/shard_map/ppermute | solution.py:412
  93.1 0.7 add.3
  93.7 1.3 %all-to-all-done.2.pieces = bf16[8,176,256]{2,1,0:T(8,128)(2,1)S(1)} async-done(((bf16[8,176,256]{2,1,0:T(8,128)(2,1)}), bf16[8,176,256]{2,1,0:T(8,128)(2,1)S(1)}, u32[]{:S(2)}, u32[]{:S(2)}) %all-to-all-start.2) | async-done | bytes 720928 | tf_op jit(solution)/shard_map/all_to_all | solution.py:407
  95.1 0.2 shard_map.98
  95.3 6.4 %collective-permute-start.4 = (bf16[128,512]{1,0:T(8,128)(2,1)S(1)}, bf16[128,512]{1,0:T(8,128)(2,1)S(1)}, u32[]{:S(2)}, u32[]{:S(2)}) collective-permute-start(bf16[128,512]{1,0:T(8,128)(2,1)S(1)} %shard_map.98), channel_id=1, source_target_pairs={{0,0},{1,1},{2,128},{3,129},{4,256},{5,257},{6,384},{7,385},{8,8},... | collective-permute-start | bytes 393224 | tf_op jit(solution)/shard_map/ppermute | solution.py:415
  101.7 4.8 %all-to-all-start.3 = ((f32[8,28,128]{2,1,0:T(8,128)}), f32[8,28,128]{2,1,0:T(8,128)S(1)}, u32[]{:S(2)}, u32[]{:S(2)}) async-start(f32[8,28,128]{2,1,0:T(8,128)} %add.3), calls=%async_computation.3 | async-start | bytes 262144 | tf_op jit(solution)/shard_map/all_to_all | solution.py:418
  106.4 0.0 copy-start.2
  106.4 0.0 copy-start.4
  106.5 0.0 copy-start.5
  106.5 2.2 %collective-permute-done.4.parts = bf16[128,512]{1,0:T(8,128)(2,1)S(1)} collective-permute-done((bf16[128,512]{1,0:T(8,128)(2,1)S(1)}, bf16[128,512]{1,0:T(8,128)(2,1)S(1)}, u32[]{:S(2)}, u32[]{:S(2)}) %collective-permute-start.4) | collective-permute-done | bytes 131104 | tf_op jit(solution)/shard_map/ppermute | solution.py:415
  108.7 0.9 shard_map.99
  109.6 4.7 %all-to-all-done.3.parts_ref = f32[8,28,128]{2,1,0:T(8,128)S(1)} async-done(((f32[8,28,128]{2,1,0:T(8,128)}), f32[8,28,128]{2,1,0:T(8,128)S(1)}, u32[]{:S(2)}, u32[]{:S(2)}) %all-to-all-start.3) | async-done | bytes 114720 | tf_op jit(solution)/shard_map/all_to_all | solution.py:418
  114.3 0.0 copy-done.2
  114.3 0.0 copy-done.4
  114.3 0.0 copy-done.5
  114.3 1.3 %shard_map.100 = (f32[28,1,128]{2,1,0:T(1,128)}, f32[28,1,128]{2,1,0:T(1,128)}, f32[28,1,4096]{2,1,0:T(1,128)}) custom-call(f32[8,28,128]{2,1,0:T(8,128)S(1)} %all-to-all-done.3.parts_ref, bf16[4096,128]{1,0:T(8,128)(2,1)S(1)} %copy-done.2, f32[28,1,128]{2,1,0:T(1,128)S(1)} %bitcast.12, f32[28,1,128]{2,1,0:T(1,128)S(1)} %bitcast.13), custom_call_target="tpu_custom_call" | custom-call | tf_op jit(solution)/shard_map/pallas_call | solution.py:382
Async XLA Ops:
  3.0 9.6 %copy-start.6 = (bf16[64,1792]{1,0:T(8,128)(2,1)S(1)}, bf16[64,1792]{1,0:T(8,128)(2,1)}, u32[]{:S(2)}) copy-start(bf16[64,1792]{1,0:T(8,128)(2,1)} %param.8) | copy-start | bytes 688132
  3.0 35.0 %copy-start.3 = (bf16[128,512]{1,0:T(8,128)(2,1)S(1)}, bf16[128,512]{1,0:T(8,128)(2,1)}, u32[]{:S(2)}) copy-start(bf16[128,512]{1,0:T(8,128)(2,1)} %features.1) | copy-start | bytes 393220
  3.0 33.7 %all-to-all-start = ((bf16[4,128,1792]{2,1,0:T(8,128)(2,1)}), bf16[4,128,1792]{2,1,0:T(8,128)(2,1)S(1)}, u32[]{:S(2)}, u32[]{:S(2)}) async-start(bf16[4,128,1792]{2,1,0:T(8,128)(2,1)} %shard_map.93), calls=%async_computation | async-start | bytes 3670016 | tf_op jit(solution)/shard_map/all_to_all | solution.py:396
  32.2 4.5 %collective-permute-start = (bf16[4,64,1792]{2,1,0:T(8,128)(2,1)S(1)}, bf16[4,64,1792]{2,1,0:T(8,128)(2,1)}, u32[]{:S(2)}, u32[]{:S(2)}) collective-permute-start(bf16[4,64,1792]{2,1,0:T(8,128)(2,1)S(1)} %bitcast.11), channel_id=1, source_target_pairs={{0,8},{8,0},{16,24},{24,16},{32,40},{40,32},{48,56},{56,48},{64,72... | collective-permute-start | bytes 2752520 | tf_op jit(solution)/shard_map/ppermute | solution.py:399
  36.7 1.3 %copy-start = (bf16[4,128,1792]{2,1,0:T(8,128)(2,1)}, bf16[4,128,1792]{2,1,0:T(8,128)(2,1)S(1)}, u32[]{:S(2)}) copy-start(bf16[4,128,1792]{2,1,0:T(8,128)(2,1)S(1)} %all-to-all-done) | copy-start | bytes 5505028
  42.1 16.7 %collective-permute-start.1 = (bf16[2,2,64,1792]{3,2,1,0:T(8,128)(2,1)}, bf16[2,2,64,1792]{3,2,1,0:T(8,128)(2,1)S(1)}, u32[]{:S(2)}, u32[]{:S(2)}) collective-permute-start(bf16[2,2,64,1792]{3,2,1,0:T(8,128)(2,1)} %get-tuple-element.18), channel_id=1, source_target_pairs={{0,16},{8,120},{16,32},{24,8},{32,48},{40,24},{48,64},{56,40},{64,... | collective-permute-start | bytes 2752520 | tf_op jit(solution)/shard_map/ppermute | solution.py:403
  44.0 24.8 %all-to-all-start.1 = ((bf16[8,144,256]{2,1,0:T(8,128)(2,1)}), bf16[8,144,256]{2,1,0:T(8,128)(2,1)S(1)}, u32[]{:S(2)}, u32[]{:S(2)}) async-start(bf16[8,144,256]{2,1,0:T(8,128)(2,1)} %get-tuple-element.17), calls=%async_computation.1 | async-start | bytes 1179648 | tf_op jit(solution)/shard_map/all_to_all | solution.py:401
  58.8 4.4 %collective-permute-start.2 = (bf16[2,2,64,1792]{3,2,1,0:T(8,128)(2,1)S(1)}, bf16[2,2,64,1792]{3,2,1,0:T(8,128)(2,1)S(1)}, u32[]{:S(2)}, u32[]{:S(2)}) collective-permute-start(bf16[2,2,64,1792]{3,2,1,0:T(8,128)(2,1)S(1)} %collective-permute-done.1.near), channel_id=1, source_target_pairs={{0,8},{8,0},{16,24},{24,16},{32,40},{40,32},{48,56},{56,48},{64,72... | collective-permute-start | bytes 2752520 | tf_op jit(solution)/shard_map/ppermute | solution.py:404
  67.5 21.6 %copy-start.1 = (bf16[4,128,1792]{2,1,0:T(8,128)(2,1)S(1)}, bf16[4,128,1792]{2,1,0:T(8,128)(2,1)}, u32[]{:S(2)}) copy-start(bf16[4,128,1792]{2,1,0:T(8,128)(2,1)} %copy-done) | copy-start | bytes 5505028
  68.8 26.3 %all-to-all-start.2 = ((bf16[8,176,256]{2,1,0:T(8,128)(2,1)}), bf16[8,176,256]{2,1,0:T(8,128)(2,1)S(1)}, u32[]{:S(2)}, u32[]{:S(2)}) async-start(bf16[8,176,256]{2,1,0:T(8,128)(2,1)} %shard_map.95), calls=%async_computation.2 | async-start | bytes 1441792 | tf_op jit(solution)/shard_map/all_to_all | solution.py:407
  89.8 3.2 %collective-permute-start.3 = (f32[8,28,128]{2,1,0:T(8,128)S(1)}, f32[8,28,128]{2,1,0:T(8,128)S(1)}, u32[]{:S(2)}, u32[]{:S(2)}) collective-permute-start(f32[8,28,128]{2,1,0:T(8,128)S(1)} %get-tuple-element.23), channel_id=1, source_target_pairs={{0,8},{8,0},{16,24},{24,16},{32,40},{40,32},{48,56},{56,48},{64,72... | collective-permute-start | bytes 344072 | tf_op jit(solution)/shard_map/ppermute | solution.py:412
  95.3 13.4 %collective-permute-start.4 = (bf16[128,512]{1,0:T(8,128)(2,1)S(1)}, bf16[128,512]{1,0:T(8,128)(2,1)S(1)}, u32[]{:S(2)}, u32[]{:S(2)}) collective-permute-start(bf16[128,512]{1,0:T(8,128)(2,1)S(1)} %shard_map.98), channel_id=1, source_target_pairs={{0,0},{1,1},{2,128},{3,129},{4,256},{5,257},{6,384},{7,385},{8,8},... | collective-permute-start | bytes 393224 | tf_op jit(solution)/shard_map/ppermute | solution.py:415
  101.7 12.7 %all-to-all-start.3 = ((f32[8,28,128]{2,1,0:T(8,128)}), f32[8,28,128]{2,1,0:T(8,128)S(1)}, u32[]{:S(2)}, u32[]{:S(2)}) async-start(f32[8,28,128]{2,1,0:T(8,128)} %add.3), calls=%async_computation.3 | async-start | bytes 262144 | tf_op jit(solution)/shard_map/all_to_all | solution.py:418
  106.4 7.9 %copy-start.2 = (bf16[4096,128]{1,0:T(8,128)(2,1)S(1)}, bf16[4096,128]{1,0:T(8,128)(2,1)}, u32[]{:S(2)}) copy-start(bf16[4096,128]{1,0:T(8,128)(2,1)} %basis_ref.1) | copy-start | bytes 3145732
  106.4 7.9 %copy-start.4 = (f32[1,28,128]{2,0,1:T(1,128)S(1)}, f32[1,28,128]{2,0,1:T(1,128)}, u32[]{:S(2)}) copy-start(f32[1,28,128]{2,0,1:T(1,128)} %param.10) | copy-start | bytes 43012
  106.5 7.9 %copy-start.5 = (f32[1,28,128]{2,0,1:T(1,128)S(1)}, f32[1,28,128]{2,0,1:T(1,128)}, u32[]{:S(2)}) copy-start(f32[1,28,128]{2,0,1:T(1,128)} %param.11) | copy-start | bytes 43012
